TPU v7x, 256 devices: a whole 4x4x8 slice. The times are simulated.
256 devices in a mesh: dp: 32 (over z, x_lo, core), seq: 8 (over y, x_hi).
Axes of the slice: x: 4 (x_hi: 2, x_lo: 2; x = x_hi * 2 + x_lo), y: 4, z: 8, core: 2. Of those that a mesh axis runs over, the one named last changes fastest.
Arguments:
- hidden: bfloat16 [32, 1024, 8192], P('dp', 'seq'), may hold values from -48 to 48
- w_query: bfloat16 [8192, 128], P('dp'), may hold values from -0.0625 to 0.0625
- w_key: bfloat16 [8192, 128], P('dp'), may hold values from -0.0625 to 0.0625
- w_value: bfloat16 [8192, 128], P('dp'), may hold values from -0.0625 to 0.0625
- score_vec: float32 [128], replicated, may hold values from -4 to 4
- labels: int32 [32], replicated, may hold values from 0 to 1
- lengths: int32 [32], replicated, may hold values from 1 to 8, as said below
- partner: int32 [32], replicated, may hold values from 0 to 31, as said below
Outputs:
- loss: float32 [], replicated
- grad_query: float32 [8192, 128], P('dp')
- grad_key: float32 [8192, 128], P('dp')
- grad_value: float32 [8192, 128], P('dp')
- grad_score: float32 [128], replicated
- grad_hidden: bfloat16 [32, 1024, 8192], P('dp', 'seq')
Inputs may be any that keep to these rules, and one draw needn't show every extreme that they name: partner[partner[g]] = g and partner[g] != g; at least one pair joins two neighbouring responses (indices differing by one, counted round). Response g holds 128 * lengths[g] live tokens from its start; some response fills all 8 blocks.
All inputs are finite; a program needn't handle non-finite values.
Results may differ from a plain program's by a relative error of at most 0.033.
Values may be sent and summed in bfloat16 or wider, within the bound.
No kernel may reach another device: no remote copies, remote signals or barrier semaphores. Data moves between devices by JAX's collectives and lax.ppermute only.
A program may use at most 128 MiB of HBM per device.

v0:
```python
import math

import jax
import jax.numpy as jnp
from jax import lax
from jax.sharding import PartitionSpec as P

BLK = 128


def fetch_pair(block, partner_id):
    piece = lax.all_gather(block[None], "dp", axis=0, tiled=True)
    index = jnp.arange(piece.shape[0])
    hit = (index == partner_id)[:, None, None]
    return jnp.sum(jnp.where(hit, piece, jnp.zeros_like(piece)), axis=0)


def return_grads(block, partner_id):
    piece = lax.all_gather(block[None], "dp", axis=0, tiled=True)
    index = jnp.arange(piece.shape[0])
    hit = (index == partner_id)[:, None, None]
    return jnp.sum(jnp.where(hit, piece, jnp.zeros_like(piece)), axis=0)


def per_device(hidden, w_query, w_key, w_value, score_vec, labels, lengths, partner):
    rows = hidden.shape[1]
    width = hidden.shape[2]
    head = w_query.shape[1]
    groups = lax.axis_size("dp")
    tokens = hidden.reshape(rows, width)
    group = lax.axis_index("dp")
    window = lax.axis_index("seq")
    full_query, full_key, full_value = (
        lax.all_gather(w_query, "dp", axis=0, tiled=True),
        lax.all_gather(w_key, "dp", axis=0, tiled=True),
        lax.all_gather(w_value, "dp", axis=0, tiled=True),
    )
    stacked = jnp.concatenate([full_query, full_key, full_value], axis=1)
    proj = jnp.dot(tokens, stacked, preferred_element_type=jnp.float32).astype(jnp.bfloat16)
    query = proj[:, :head]
    own_kv = proj[:, head:]
    slots = jnp.arange(groups)
    mine = slots == group
    partner_id = jnp.sum(jnp.where(mine, partner, 0))
    own_len = jnp.sum(jnp.where(mine, lengths, 0))
    other_len = jnp.sum(jnp.where(slots == partner_id, lengths, 0))
    label = jnp.sum(jnp.where(mine, labels, 0))
    factor = 32.0 * (1.0 + 2.0 * group.astype(jnp.float32) / (groups - 1))
    mate_kv = fetch_pair(own_kv, partner_id)
    whole_kv = lax.all_gather(mate_kv, "seq", axis=0, tiled=True)
    length = whole_kv.shape[0]
    keys = whole_kv[:, :head]
    values = whole_kv[:, head:]
    usable = jnp.arange(length) < BLK * other_len
    live = (window * rows + jnp.arange(rows) < BLK * own_len).astype(jnp.float32)
    contract_last = (((1,), (1,)), ((), ()))
    contract_first = (((0,), (0,)), ((), ()))
    scores = lax.dot_general(
        query, keys, contract_last, preferred_element_type=jnp.float32
    ) / math.sqrt(head)
    scores = jnp.where(usable[None, :], scores, jnp.float32(-1e30))
    top = jnp.max(scores, axis=-1, keepdims=True)
    expo = jnp.exp(scores - top)
    probs = expo / jnp.sum(expo, axis=-1, keepdims=True)
    probs_b = probs.astype(jnp.bfloat16)
    attended = jnp.dot(probs_b, values, preferred_element_type=jnp.float32)
    token_score = jnp.sum(attended * score_vec[None, :], axis=-1)
    partial_total = jnp.sum(token_score * live)
    total = lax.psum(partial_total, "seq")
    count = (BLK * own_len).astype(jnp.float32)
    total = total / jnp.sqrt(count)
    sign = (2 * label - 1).astype(jnp.float32)
    loss_term = factor * jax.nn.softplus(-sign * total)
    grad_total = -factor * sign * jax.nn.sigmoid(-sign * total)
    grad_token = live * grad_total / jnp.sqrt(count)
    readout_part = jnp.sum(attended * grad_token[:, None], axis=0)
    loss = lax.psum(loss_term, "dp")
    grad_score = lax.psum(readout_part, ("dp", "seq"))
    grad_att = (grad_token[:, None] * score_vec[None, :]).astype(jnp.bfloat16)
    grad_vals = lax.dot_general(
        probs_b, grad_att, contract_first, preferred_element_type=jnp.float32
    )
    grad_prob = lax.dot_general(grad_att, values, contract_last, preferred_element_type=jnp.float32)
    grad_scores = (
        probs * (grad_prob - jnp.sum(grad_prob * probs, axis=-1, keepdims=True)) / math.sqrt(head)
    )
    grad_scores_b = grad_scores.astype(jnp.bfloat16)
    grad_q = jnp.dot(grad_scores_b, keys, preferred_element_type=jnp.float32).astype(jnp.bfloat16)
    grad_keys = lax.dot_general(
        grad_scores_b, query, contract_first, preferred_element_type=jnp.float32
    )
    mate_grads = jnp.concatenate([grad_keys, grad_vals], axis=1)
    window_sum = lax.psum_scatter(mate_grads, "seq", scatter_dimension=0, tiled=True).astype(
        jnp.bfloat16
    )
    kv_grad = return_grads(window_sum, partner_id)
    grad_all = jnp.concatenate([grad_q, kv_grad], axis=1)
    grad_hidden = lax.dot_general(
        grad_all, stacked, contract_last, preferred_element_type=jnp.float32
    )
    grad_hidden = grad_hidden.astype(jnp.bfloat16).reshape(1, rows, width)
    shares = lax.psum_scatter(
        lax.dot_general(tokens, grad_all, contract_first, preferred_element_type=jnp.float32),
        "dp",
        scatter_dimension=0,
        tiled=True,
    )
    summed = lax.psum(shares, "seq")
    return (
        loss,
        summed[:, :head],
        summed[:, head : 2 * head],
        summed[:, 2 * head :],
        grad_score,
        grad_hidden,
    )


def solution(mesh):
    return jax.shard_map(
        per_device,
        mesh=mesh,
        in_specs=(
            P("dp", "seq", None),
            P("dp", None),
            P("dp", None),
            P("dp", None),
            P(),
            P(),
            P(),
            P(),
        ),
        out_specs=(P(), P("dp", None), P("dp", None), P("dp", None), P(), P("dp", "seq", None)),
        check_vma=False,
    )
```

profile of v0, /device:TPU:2, one launch (start us, length us, event | category | flops | bytes accessed | tf_op | source)
XLA Modules:
  0.0 746.9 jit_solution(15764541184373515351)
XLA Ops:
  7.2 0.0 copy-start
  7.2 0.0 all-gather.8.cloned.1.call-start
  7.2 0.7 all-gather.8.cloned.1.call-update
  7.9 0.0 all-gather.10.cloned.1.call-start
  8.0 0.7 all-gather.10.cloned.1.call-update
  8.7 0.0 all-gather.12.cloned.1.call-start
  8.7 0.7 all-gather.12.cloned.1.call-update
  9.4 0.0 all-gather.14.cloned.1.call-start
  9.4 67.6 %all-gather.8.cloned.1.call-done = bf16[8192,128]{1,0:T(8,128)(2,1)} async-done(((bf16[256,128]{1,0:T(8,128)(2,1)}), bf16[8192,128]{1,0:T(8,128)(2,1)}) %all-gather.8.cloned.1.call-update) | async-done | bytes 2097168 | tf_op jit(solution)/shard_map/all_gather | solution.py:34
  77.1 3.1 constant_dynamic-update-slice_fusion.2
  80.2 63.1 %all-gather.10.cloned.1.call-done = bf16[8192,128]{1,0:T(8,128)(2,1)} async-done(((bf16[256,128]{1,0:T(8,128)(2,1)}), bf16[8192,128]{1,0:T(8,128)(2,1)}) %all-gather.10.cloned.1.call-update) | async-done | bytes 2097168 | tf_op jit(solution)/shard_map/all_gather | solution.py:35
  143.3 3.2 constant_dynamic-update-slice_fusion.1
  146.5 63.1 %all-gather.12.cloned.1.call-done = bf16[8192,128]{1,0:T(8,128)(2,1)} async-done(((bf16[256,128]{1,0:T(8,128)(2,1)}), bf16[8192,128]{1,0:T(8,128)(2,1)}) %all-gather.12.cloned.1.call-update) | async-done | bytes 2097168 | tf_op jit(solution)/shard_map/all_gather | solution.py:36
  209.6 3.2 constant_dynamic-update-slice_fusion
  212.8 0.0 copy-done
  212.8 4.7 fusion.10
  217.5 0.6 slice.29
  218.1 0.0 all-gather.14.cloned.1.call-update
  218.2 0.0 reduce-scatter.3.cloned.1.call-start
  218.2 0.0 copy-done.4
  218.2 0.6 select_reduce_fusion.1
  218.9 0.0 copy-done.2
  218.9 1.3 select_reduce_fusion.2
  222.2 0.7 iota_compare_fusion.1
  222.9 61.4 %all-gather.14.cloned.1.call-done = bf16[4096,256]{0,1:T(8,128)(2,1)} async-done(((bf16[128,256]{0,1:T(8,128)(2,1)}), bf16[4096,256]{0,1:T(8,128)(2,1)}) %all-gather.14.cloned.1.call-update) | async-done | bytes 2097168 | tf_op jit(solution)/shard_map/all_gather | solution.py:12
  284.2 2.1 copy.21
  286.3 0.0 copy-start.5
  286.3 1.1 fusion.2
  287.4 32.7 %all_gather.22 = bf16[1024,256]{0,1:T(8,128)(2,1)S(1)} all-gather(bf16[128,256]{0,1:T(8,128)(2,1)S(1)} %fusion.2), channel_id=1, replica_groups=mesh['dp'=32,'seq'=8] {'seq'}, dimensions={0}, use_global_device_ids=true | all-gather | bytes 589824 | tf_op jit(solution)/shard_map/all_gather | solution.py:50
  320.2 0.3 fusion.38
  320.5 0.2 fusion.14
  320.7 0.9 multiply_reduce_fusion.2
  321.7 0.6 fusion.31
  322.3 23.1 %psum.28 = f32[]{:T(128)} all-reduce(f32[]{:T(128)} %fusion.31), channel_id=1, replica_groups=mesh['dp'=32,'seq'=8] {'seq'}, use_global_device_ids=true, to_apply=%region_9.10 | all-reduce | flops 1 | bytes 8 | tf_op jit(solution)/shard_map/psum | solution.py:69
  346.2 0.4 multiply_reduce_fusion
  346.5 0.3 fusion.21
  346.9 0.2 multiply_convert_fusion
  347.1 0.2 fusion.28
  347.3 1.0 pad_maximum_fusion
  348.4 0.0 reduce-scatter.3.cloned.1.call-update
  348.4 0.0 all-gather.16.cloned.1.call-start
  348.4 70.0 %reduce-scatter.3.cloned.1.call-done = f32[128,256]{0,1:T(8,128)} async-done(((f32[1024,256]{0,1:T(8,128)}), f32[128,256]{0,1:T(8,128)}) %reduce-scatter.3.cloned.1.call-update) | async-done | bytes 131088 | tf_op jit(solution)/shard_map/reduce_scatter | solution.py:93
  418.4 1.5 convert_element_type.47
  420.0 0.0 all-gather.16.cloned.1.call-update
  420.0 0.0 reduce-scatter.5.cloned.1.call-start
  420.0 0.2 convolution_convert_fusion.1
  420.3 66.1 %all-gather.16.cloned.1.call-done = bf16[4096,256]{0,1:T(8,128)(2,1)} async-done(((bf16[128,256]{0,1:T(8,128)(2,1)}), bf16[4096,256]{0,1:T(8,128)(2,1)}) %all-gather.16.cloned.1.call-update) | async-done | bytes 2097168 | tf_op jit(solution)/shard_map/all_gather | solution.py:19
  486.3 2.1 copy.22
  488.4 1.1 fusion.1
  489.5 6.4 convolution_bitcast_fusion
  495.9 0.0 reduce-scatter.5.cloned.1.call-update
  495.9 0.0 all-reduce.2.cloned.1.call-start
  496.0 52.5 %psum.29 = f32[]{:T(128)} all-reduce(f32[]{:T(128)S(6)} %mul.70), channel_id=1, replica_groups=mesh['dp'=32,'seq'=8] {'dp'}, use_global_device_ids=true, to_apply=%region_10.11 | all-reduce | flops 1 | bytes 8 | tf_op jit(solution)/shard_map/psum | solution.py:77
  548.6 0.0 copy-done.1
  548.6 0.1 multiply_reduce_fusion.1
  548.7 77.8 %psum.31 = f32[128]{0:T(128)} all-reduce(f32[128]{0:T(128)S(1)} %multiply_reduce_fusion.1), channel_id=1, replica_groups=mesh['dp'=32,'seq'=8] {'dp','seq'}, use_global_device_ids=true, to_apply=%region_17.18 | all-reduce | flops 128 | bytes 1024 | tf_op jit(solution)/shard_map/psum | solution.py:78
  626.4 16.6 %reduce-scatter.5.cloned.1.call-done = f32[256,384]{0,1:T(8,128)} async-done(((f32[8192,384]{0,1:T(8,128)}), f32[256,384]{0,1:T(8,128)}) %reduce-scatter.5.cloned.1.call-update) | async-done | bytes 393232 | tf_op jit(solution)/shard_map/reduce_scatter | solution.py:102
  643.1 0.0 all-reduce.2.cloned.1.call-update
  643.1 6.2 fusion
  649.3 87.4 %all-reduce.2.cloned.1.call-done = f32[256,384]{0,1:T(8,128)} async-done(((f32[256,384]{0,1:T(8,128)}), f32[256,384]{0,1:T(8,128)}) %all-reduce.2.cloned.1.call-update) | async-done | bytes 393232 | tf_op jit(solution)/shard_map/psum | solution.py:108
  736.7 1.1 fusion.37
  737.8 0.8 copy.18
  738.6 0.8 copy.19
  739.3 0.8 copy.20
  (8 shorter events, 0.0 us)
Async XLA Ops:
  7.2 205.7 %copy-start = (bf16[1,128,8192]{2,1,0:T(8,128)(2,1)S(1)}, bf16[1,128,8192]{2,1,0:T(8,128)(2,1)}, u32[]{:S(2)}) copy-start(bf16[1,128,8192]{2,1,0:T(8,128)(2,1)} %param.8) | copy-start | bytes 6291460
  7.2 69.9 %all-gather.8.cloned.1.call-start = ((), (), s32[]{:S(2)}) async-start(), calls=%async_computation.2 | async-start | bytes 2162688 | tf_op jit(solution)/shard_map/all_gather | solution.py:34
  7.9 135.4 %all-gather.10.cloned.1.call-start = ((), (), s32[]{:S(2)}) async-start(), calls=%async_computation.3 | async-start | bytes 2162688 | tf_op jit(solution)/shard_map/all_gather | solution.py:35
  8.7 201.0 %all-gather.12.cloned.1.call-start = ((), (), s32[]{:S(2)}) async-start(), calls=%async_computation.4 | async-start | bytes 2162688 | tf_op jit(solution)/shard_map/all_gather | solution.py:36
  9.4 274.8 %all-gather.14.cloned.1.call-start = ((), (), s32[]{:S(2)}) async-start(), calls=%async_computation.8 | async-start | bytes 2162688 | tf_op jit(solution)/shard_map/all_gather | solution.py:12
  212.8 5.4 copy-start.4
  212.8 6.0 copy-start.2
  212.8 6.0 copy-start.3
  218.2 200.3 %reduce-scatter.3.cloned.1.call-start = ((), (), s32[]{:S(2)}) async-start(), calls=%async_computation.5 | async-start | bytes 1179648 | tf_op jit(solution)/shard_map/reduce_scatter | solution.py:93
  286.3 34.4 %copy-start.5 = (f32[128]{0:T(128)S(1)}, f32[128]{0:T(128)}, u32[]{:S(2)}) copy-start(f32[128]{0:T(128)} %param.12) | copy-start | bytes 1540
  348.4 137.9 %all-gather.16.cloned.1.call-start = ((), (), s32[]{:S(2)}) async-start(), calls=%async_computation.9 | async-start | bytes 2162688 | tf_op jit(solution)/shard_map/all_gather | solution.py:19
  420.0 223.1 %reduce-scatter.5.cloned.1.call-start = ((), (), s32[]{:S(2)}) async-start(), calls=%async_computation.6 | async-start | bytes 12976128 | tf_op jit(solution)/shard_map/reduce_scatter | solution.py:102
  495.9 52.7 %copy-start.1 = (f32[128,128]{1,0:T(8,128)S(1)}, f32[128,128]{1,0:T(8,128)}, u32[]{:S(2)}) copy-start(f32[128,128]{1,0:T(8,128)} %get-tuple-element.26) | copy-start | bytes 196612
  495.9 240.8 %all-reduce.2.cloned.1.call-start = ((), (), s32[]{:S(2)}) async-start(), calls=%async_computation.7 | async-start | bytes 786432 | tf_op jit(solution)/shard_map/psum | solution.py:108
Sparse Core Ops, SparseCore 0:
  9.9 67.1 all-gather.7
  78.9 64.3 all-gather.9
  145.2 64.3 all-gather.11
  218.3 65.9 all-gather.13
  348.5 69.8 reduce-scatter.2
  420.7 65.5 all-gather.15
  496.0 147.0 reduce-scatter.4
  645.9 90.8 all-reduce.1
where the time goes:
time: 748 us; the launch traced here: 747 us
  waiting for transfers between devices  497 us (66%)
  blocking collectives  186 us (25%)
  matrix products  19.6 us (3%)
  local copies, waits for them, and re-layouts  17.6 us (2%)
  between operations  17.1 us (2%)
  other arithmetic  8.58 us (1%)
    psum x1, waiting for transfers between devices, per_device(): summed = lax.psum(shares, 'seq')  87.4 us
    psum x1, blocking collectives, per_device(): grad_score = lax.psum(readout_part, ('dp', 'seq'))  77.8 us
    reduce_scatter x1, waiting for transfers between devices, per_device(): lax.psum_scatter(mate_grads, 'seq', scatter_dimension=0, tiled=True)  70 us
    all_gather x1, waiting for transfers between devices, per_device(): lax.all_gather(w_query, 'dp', axis=0, tiled=True)  67.6 us
    all_gather x1, waiting for transfers between devices, return_grads(): piece = lax.all_gather(block[None], 'dp', axis=0, tiled=True)  66.1 us
    all_gather x1, waiting for transfers between devices, per_device(): lax.all_gather(w_key, 'dp', axis=0, tiled=True)  63.1 us
    all_gather x1, waiting for transfers between devices, per_device(): lax.all_gather(w_value, 'dp', axis=0, tiled=True)  63.1 us
    all_gather x1, waiting for transfers between devices, fetch_pair(): piece = lax.all_gather(block[None], 'dp', axis=0, tiled=True)  61.4 us
  transfers between devices with their start and end apart: 8, of which 8 were waited for; matrix products, arithmetic and copies ran while one was open for 2% of the time, Pallas kernels for 0%

commit v1 on v0

v1 whole, which is shorter than its diff:
```python
import functools
import math

import jax
import jax.numpy as jnp
from jax import lax
from jax.experimental import pallas as pl
from jax.experimental.pallas import tpu as pltpu
from jax.sharding import Mesh
from jax.sharding import PartitionSpec as P

F32 = jnp.float32
BF16 = jnp.bfloat16
NZ, NX, NC = 8, 2, 2
NDP = NZ * NX * NC
NSEQ = 8
BLK = 128
HEAD = 128
ROWS = 256
EXT = 16
SHARE = ROWS // NSEQ
COLS = NDP * SHARE
SEQLEN = NSEQ * BLK
TB = 256
DP = ("z", "xl", "c")
SEQ = ("y", "xh")
LAST = (((1,), (1,)), ((), ()))
VM = pl.BlockSpec(memory_space=pltpu.VMEM)
SM = pl.BlockSpec(memory_space=pltpu.SMEM)


def call(kernel, outs, ins, scratch=(), flops=0, bytes_accessed=0, name=None):
    return pl.pallas_call(
        kernel,
        out_shape=outs,
        in_specs=[SM if a.dtype == jnp.int32 else VM for a in ins],
        out_specs=jax.tree.map(lambda _: VM, outs),
        scratch_shapes=list(scratch),
        compiler_params=pltpu.CompilerParams(vmem_limit_bytes=50 * 1024 * 1024),
        cost_estimate=pl.CostEstimate(flops=flops, bytes_accessed=bytes_accessed, transcendentals=0),
        name=name,
    )(*ins)


def shape(dims, dtype):
    return jax.ShapeDtypeStruct(dims, dtype)


def halves(x):
    high = x.astype(BF16).astype(F32)
    return high, x - high


def pack_weights(wq, wk, wv, score, out):
    out[0:ROWS, 0:HEAD] = wq[...]
    out[0:ROWS, HEAD : 2 * HEAD] = wk[...]
    s1, rest = halves(score[...])
    s2, s3 = halves(rest)
    row = lax.broadcasted_iota(jnp.int32, (EXT, HEAD), 0)
    lhs = jnp.where(row == 0, s1, jnp.where(row == 1, s2, jnp.where(row == 2, s3, 0.0)))
    product = lax.dot_general(lhs.astype(BF16), wv[...], LAST, preferred_element_type=F32)
    total = jnp.sum(product, axis=0, keepdims=True)
    high, low = halves(total)
    row = lax.broadcasted_iota(jnp.int32, (EXT, ROWS), 0)
    ext = jnp.where((row == 0) | (row == 2), high, jnp.where(row == 1, low, 0.0))
    out[ROWS : ROWS + EXT, :] = ext.astype(BF16)


def split_columns(hidden, out):
    size = 4 * BLK
    o = lax.broadcasted_iota(jnp.int32, (size, size), 0)
    i = lax.broadcasted_iota(jnp.int32, (size, size), 1)
    source = BLK * ((o & 127) >> 5) + SHARE * (o >> 7) + (o & 31)
    perm = jnp.where(i == source, 1.0, 0.0).astype(BF16)
    for q in range(NDP // 4):
        for h in range(2):
            parts = [hidden[:, ROWS * (4 * q + k) + BLK * h :][:, :BLK] for k in range(4)]
            x = jnp.concatenate(parts, axis=1)
            y = lax.dot_general(perm, x, LAST, preferred_element_type=F32).astype(BF16)
            for r in range(4):
                out[4 * h + r, BLK * q : BLK * (q + 1), :] = y[BLK * r : BLK * (r + 1)]


def project(ids, hidden, *refs):
    blocks, out = refs[:-1], refs[-1]
    acc = jnp.zeros((BLK, 2 * HEAD), F32)
    wide = jnp.zeros((EXT, BLK), F32)
    for n, block in enumerate(blocks):
        start = pl.multiple_of(ids[n] * ROWS, ROWS)
        x = hidden[:, pl.ds(start, ROWS)]
        acc += jnp.dot(x, block[0:ROWS, :], preferred_element_type=F32)
        wide += lax.dot_general(block[ROWS : ROWS + EXT, :], x, LAST, preferred_element_type=F32)
    qk = acc.astype(BF16)
    high, low = halves(wide[0:1] + wide[1:2])
    row = lax.broadcasted_iota(jnp.int32, (EXT, 2 * HEAD), 0)
    ext = jnp.where(row == 0, jnp.concatenate([high, low], axis=1), 0.0).astype(BF16)
    for s in range(NSEQ):
        out[s, 0:BLK, :] = qk
        out[s, BLK : BLK + EXT, :] = ext


def pick_for_planes(ids, a, b, c, d, out, items):
    for n, ref in enumerate((a, b, c, d)):
        items[n] = ref[...]
    for z in range(NZ):
        out[z] = items[ids[z]]


def pick_partner(ids, received, out):
    mine = received[ids[0]]
    for s in range(NSEQ):
        out[s] = mine


def attention(ids, own, mate, grads, crows, loss, q_t, k_t, q_own, k_own, q_mate, k_mate, wcol, scores, dots, dq, dk, cacc):
    scale = 1.0 / math.sqrt(HEAD)
    exponent = scale * math.log2(math.e)
    own_len, mate_len = ids[0], ids[1]
    for i in range(NSEQ):
        at = slice(BLK * i, BLK * (i + 1))
        q_own[at, :] = own[i, 0:BLK, 0:HEAD]
        k_own[at, :] = own[i, 0:BLK, HEAD : 2 * HEAD]
        q_mate[at, :] = mate[i, 0:BLK, 0:HEAD]
        k_mate[at, :] = mate[i, 0:BLK, HEAD : 2 * HEAD]
        k_t[:, at] = mate[i, 0:BLK, HEAD : 2 * HEAD].astype(F32).T.astype(BF16)
        for n, ref in enumerate((mate, own)):
            ext = ref[i, BLK : BLK + EXT, :].astype(F32)
            row = ext[0:1, 0:BLK] + ext[0:1, BLK : 2 * BLK]
            wcol[n, at, :] = jnp.broadcast_to(row, (BLK, BLK)).T

    def softmax(side, queries, keys, start, key_len):
        q = queries[pl.ds(start, TB), :]
        top = jnp.full((8, TB), -jnp.inf, F32)
        for u in range(NSEQ):
            at = slice(BLK * u, BLK * (u + 1))
            s = lax.dot_general(keys[at, :], q, LAST, preferred_element_type=F32)
            s = s * exponent + jnp.where(u < key_len, 0.0, -1e30).astype(F32)
            scores[at, :] = s
            top = jnp.maximum(top, jnp.max(s.reshape(BLK // 8, 8, TB), axis=0))
        top = jnp.max(top, axis=0, keepdims=True)
        total = jnp.zeros((8, TB), F32)
        weighed = jnp.zeros((8, TB), F32)
        for u in range(2 * NSEQ):
            at = slice(64 * u, 64 * (u + 1))
            e = jnp.exp2(scores[at, :] - top)
            scores[at, :] = e
            w = wcol[side, at, :]
            total += jnp.sum(e.reshape(8, 8, TB), axis=0)
            weighed += jnp.sum((e * jnp.concatenate([w, w], axis=1)).reshape(8, 8, TB), axis=0)
        total = jnp.sum(total, axis=0, keepdims=True)
        inverse = 1.0 / total
        s_row = jnp.sum(weighed, axis=0, keepdims=True) * inverse
        return inverse, s_row

    def live_row(start, length):
        t = lax.broadcasted_iota(jnp.int32, (1, TB), 1) + start
        return jnp.where(t < BLK * length, 1.0, 0.0).astype(F32)

    def first(n, z):
        start = pl.multiple_of(n * TB, TB)
        inverse, s_row = softmax(0, q_own, k_mate, start, mate_len)
        live = live_row(start, own_len)
        for u in range(2 * NSEQ):
            at = slice(64 * u, 64 * (u + 1))
            w = wcol[0, at, :]
            dots[at, :] = (scores[at, :] * (jnp.concatenate([w, w], axis=1) - s_row)).astype(BF16)
        g = jnp.dot(k_t[...], dots[...], preferred_element_type=F32)
        dq[:, pl.ds(start, TB)] = g * (inverse * live)
        return z + s_row * live

    def second(n, z):
        start = pl.multiple_of(n * TB, TB)
        inverse, s_row = softmax(1, q_mate, k_own, start, own_len)
        live = live_row(start, mate_len)
        r = inverse * live
        for u in range(2 * NSEQ):
            at = slice(64 * u, 64 * (u + 1))
            w = wcol[1, at, :]
            f = scores[at, :] * r
            cacc[at, :] += f[:, 0:BLK] + f[:, BLK:TB]
            dots[at, :] = (f * (jnp.concatenate([w, w], axis=1) - s_row)).astype(BF16)
        q = q_mate[pl.ds(start, TB), :]
        dk[...] += jnp.dot(dots[...], q, preferred_element_type=F32)
        return z + s_row * live

    cacc[...] = jnp.zeros_like(cacc)
    dk[...] = jnp.zeros_like(dk)
    zero = jnp.zeros((1, TB), F32)
    z_own = lax.fori_loop(0, SEQLEN // TB, first, zero)
    z_mate = lax.fori_loop(0, SEQLEN // TB, second, zero)

    def head(z_row, length, label, index):
        count = jnp.full((1, 1), BLK * length, jnp.int32).astype(F32)
        sign = jnp.full((1, 1), 2 * label - 1, jnp.int32).astype(F32)
        factor = 32.0 * (1.0 + 2.0 * jnp.full((1, 1), index, jnp.int32).astype(F32) / (NDP - 1))
        root = jnp.sqrt(count)
        x = -sign * (jnp.sum(z_row, axis=1, keepdims=True) / root)
        e = jnp.exp(-jnp.abs(x))
        term = factor * (jnp.maximum(x, 0.0) + jnp.log1p(e))
        sigmoid = jnp.where(x >= 0, 1.0, e) / (1.0 + e)
        return term, -factor * sign * sigmoid / root

    term, ds_own = head(z_own, own_len, ids[2], ids[4])
    _, ds_mate = head(z_mate, mate_len, ids[3], ids[5])
    loss[...] = jnp.broadcast_to(term, (8, BLK))
    row = lax.broadcasted_iota(jnp.int32, (EXT, BLK), 0)
    for i in range(NSEQ):
        at = slice(BLK * i, BLK * (i + 1))
        grads[i, :, 0:HEAD] = (dq[:, at] * (ds_own * scale)).T.astype(BF16)
        grads[i, :, HEAD : 2 * HEAD] = (dk[at, :] * (ds_mate * scale)).astype(BF16)
        c_row = jnp.sum(cacc[at, :].T, axis=0, keepdims=True) * ds_mate
        high, low = halves(c_row)
        crows[i] = jnp.where(row < 2, high, jnp.where(row == 2, low, 0.0)).astype(BF16)


def weight_grads(hidden_t, grads, crows, loss, value_rows, out, ext):
    chunk = 256
    wide = []
    for n in range(COLS // chunk):
        at = slice(chunk * n, chunk * (n + 1))
        acc = jnp.zeros((chunk, 2 * HEAD), F32)
        u = jnp.zeros((EXT, chunk), F32)
        for s in range(NSEQ):
            x = hidden_t[s, at, :]
            acc += jnp.dot(x, grads[s], preferred_element_type=F32)
            u += lax.dot_general(crows[s], x, LAST, preferred_element_type=F32)
        acc = acc.astype(BF16)
        for k in range(chunk // SHARE):
            out[n * (chunk // SHARE) + k, 0:SHARE, :] = acc[SHARE * k : SHARE * (k + 1)]
        wide.append(u[0:1] + u[2:3])
    row = lax.broadcasted_iota(jnp.int32, (EXT, chunk), 0)
    gs = jnp.zeros((EXT, HEAD), F32)
    ext[...] = jnp.zeros_like(ext)
    for n, u in enumerate(wide):
        high, low = halves(u)
        ext[n : n + 1, :] = high
        ext[4 + n : 5 + n, :] = low
        lhs = jnp.where(row == 0, high, jnp.where(row == 1, low, 0.0)).astype(BF16)
        gs += jnp.dot(lhs, value_rows[chunk * n : chunk * (n + 1), :], preferred_element_type=F32)
    high, low = halves(gs[0:1] + gs[1:2])
    ext[8:9, 0:HEAD] = high
    ext[8:9, HEAD : 2 * HEAD] = low
    high, low = halves(loss[0:1, :])
    ext[9:10, 0:HEAD] = high
    ext[9:10, HEAD : 2 * HEAD] = low
    tail = ext[...].astype(BF16)
    for d in range(NDP):
        out[d, SHARE : SHARE + EXT, :] = tail


def sum_shares(received, out, ext):
    acc = received[0].astype(F32)
    for n in range(1, NDP):
        acc += received[n].astype(F32)
    tail = acc[SHARE : SHARE + EXT]
    ext[...] = jnp.zeros_like(ext)
    high, low = halves(tail[0:4] + tail[4:8])
    ext[0:4, :] = high
    ext[4:8, :] = low
    for n in (8, 9):
        high, low = halves(tail[n : n + 1, 0:HEAD] + tail[n : n + 1, HEAD : 2 * HEAD])
        ext[n : n + 1, 0:HEAD] = high
        ext[n : n + 1, HEAD : 2 * HEAD] = low
    rows = acc[0:SHARE].astype(BF16)
    tail = ext[...].astype(BF16)
    for s in range(NSEQ):
        out[s, 0:SHARE, :] = rows
        out[s, SHARE : SHARE + EXT, :] = tail


def unpack(ids, received, score, gq, gk, gv, gs, loss):
    d = ids[0]
    sub = lax.broadcasted_iota(jnp.int32, (4, 2 * HEAD), 0)
    lane = lax.broadcasted_iota(jnp.int32, (SHARE, 2 * HEAD), 1)
    j = lax.broadcasted_iota(jnp.int32, (SHARE, 2 * HEAD), 0)
    hit = lane == SHARE * (d % 8) + j
    readout = jnp.zeros((1, HEAD), F32)
    for s in range(NSEQ):
        at = slice(SHARE * s, SHARE * (s + 1))
        block = received[s].astype(F32)
        gq[at, :] = block[0:SHARE, 0:HEAD]
        gk[at, :] = block[0:SHARE, HEAD : 2 * HEAD]
        tail = block[SHARE : SHARE + EXT]
        u = tail[0:4] + tail[4:8]
        u = jnp.sum(jnp.where(sub == d // 8, u, 0.0), axis=0, keepdims=True)
        column = jnp.sum(jnp.where(hit, u, 0.0), axis=1, keepdims=True)
        gv[at, :] = column * score[...]
        readout += tail[8:9, 0:HEAD] + tail[8:9, HEAD : 2 * HEAD]
        if s == 0:
            loss[...] = tail[9:10, 0:HEAD] + tail[9:10, HEAD : 2 * HEAD]
    gs[...] = readout


def hidden_grads(ids, grads, crows, *refs):
    blocks, out = refs[:-1], refs[-1]
    window = ids[len(blocks)]
    g = grads[window]
    c = crows[window].astype(F32).T.astype(BF16)
    for n, block in enumerate(blocks):
        start = pl.multiple_of(ids[n] * ROWS, ROWS)
        y = lax.dot_general(g, block[0:ROWS, :], LAST, preferred_element_type=F32)
        y += jnp.dot(c, block[ROWS : ROWS + EXT, :], preferred_element_type=F32)
        out[:, pl.ds(start, ROWS)] = y.astype(BF16)


def gather_weights(block):
    swap = [(0, 1), (1, 0)]
    up = [(i, (i + 1) % NZ) for i in range(NZ)]
    down = [(i, (i - 1) % NZ) for i in range(NZ)]
    other = lax.ppermute(block, "xl", swap)
    found = {(0, 0): block, (0, 1): other}
    for step in range(1, NZ // 2 + 1):
        for x in (0, 1):
            if step < NZ // 2 or x == 0:
                found[(-step, x)] = lax.ppermute(found[(1 - step, x)], "z", up)
            if step < NZ // 2 or x == 1:
                found[(step, x)] = lax.ppermute(found[(step - 1, x)], "z", down)
    result = []
    for (dz, dx), piece in found.items():
        result.append(((dz, dx, 0), piece))
        result.append(((dz, dx, 1), lax.ppermute(piece, "c", swap)))
    return result


def per_device(hidden, w_query, w_key, w_value, score_vec, labels, lengths, partner):
    tokens = hidden.reshape(BLK, NDP * ROWS)
    score = score_vec.reshape(1, HEAD)
    z, xl, c = (lax.axis_index(a) for a in DP)
    group = (z * NX + xl) * NC + c
    window = lax.axis_index("y") * 2 + lax.axis_index("xh")
    mate = partner[group]
    swap = [(0, 1), (1, 0)]

    block = call(
        pack_weights, shape((ROWS + EXT, ROWS), BF16), (w_query, w_key, w_value, score), name="pack_weights"
    )
    gathered = gather_weights(block)
    places = [((z + dz) % NZ) * 4 + (xl ^ dx) * 2 + (c ^ dc) for (dz, dx, dc), _ in gathered]
    place_ids = jnp.stack(places + [window]).astype(jnp.int32)
    blocks = [piece for _, piece in gathered]

    split = call(split_columns, shape((NSEQ, COLS, BLK), BF16), (tokens,), name="split_columns", flops=1 << 30)
    hidden_t = lax.all_to_all(split, SEQ, 0, 0, tiled=True)
    own_rows = lax.dynamic_slice_in_dim(w_value, window * SHARE, SHARE, 0)
    value_rows = lax.all_gather(own_rows, DP, axis=0, tiled=True)

    payload = call(
        project,
        shape((NSEQ, BLK + EXT, 2 * HEAD), BF16),
        (place_ids, tokens, *blocks),
        name="project",
        flops=1 << 29,
        bytes_accessed=6 << 20,
    )
    own = lax.all_to_all(payload, SEQ, 0, 0, tiled=True)
    mine = payload[0]
    core = lax.ppermute(mine, "c", swap)
    side = lax.ppermute(mine, "xl", swap)
    both = lax.ppermute(core, "xl", swap)
    here = xl * 2 + c
    wanted = (partner[jnp.arange(NZ) * 4 + here] % 4) ^ here
    slots = call(
        pick_for_planes,
        shape((NZ, BLK + EXT, 2 * HEAD), BF16),
        (wanted.astype(jnp.int32), mine, core, side, both),
        scratch=[pltpu.VMEM((4, BLK + EXT, 2 * HEAD), BF16)],
        name="pick_for_planes",
    )
    arrived = lax.all_to_all(slots, "z", 0, 0, tiled=True)
    theirs = call(
        pick_partner,
        shape((NSEQ, BLK + EXT, 2 * HEAD), BF16),
        ((mate // 4).reshape(1).astype(jnp.int32), arrived),
        name="pick_partner",
    )
    other = lax.all_to_all(theirs, SEQ, 0, 0, tiled=True)

    heads = jnp.stack([lengths[group], lengths[mate], labels[group], labels[mate], group, mate]).astype(jnp.int32)
    grads, crows, term = call(
        attention,
        (shape((NSEQ, BLK, 2 * HEAD), BF16), shape((NSEQ, EXT, BLK), BF16), shape((8, BLK), F32)),
        (heads, own, other),
        scratch=[
            pltpu.VMEM((HEAD, SEQLEN), BF16),
            pltpu.VMEM((HEAD, SEQLEN), BF16),
            pltpu.VMEM((SEQLEN, HEAD), BF16),
            pltpu.VMEM((SEQLEN, HEAD), BF16),
            pltpu.VMEM((SEQLEN, HEAD), BF16),
            pltpu.VMEM((SEQLEN, HEAD), BF16),
            pltpu.VMEM((2, SEQLEN, BLK), F32),
            pltpu.VMEM((SEQLEN, TB), F32),
            pltpu.VMEM((SEQLEN, TB), BF16),
            pltpu.VMEM((HEAD, SEQLEN), F32),
            pltpu.VMEM((SEQLEN, HEAD), F32),
            pltpu.VMEM((SEQLEN, BLK), F32),
        ],
        name="attention",
        flops=1 << 31,
    )
    shares = call(
        weight_grads,
        shape((NDP, SHARE + EXT, 2 * HEAD), BF16),
        (hidden_t, grads, crows, term, value_rows),
        scratch=[pltpu.VMEM((EXT, 2 * HEAD), F32)],
        name="weight_grads",
        flops=1 << 29,
    )
    arrived = lax.all_to_all(shares, DP, 0, 0, tiled=True)
    grad_hidden = call(
        hidden_grads,
        shape((BLK, NDP * ROWS), BF16),
        (place_ids, grads, crows, *blocks),
        name="hidden_grads",
        flops=1 << 29,
        bytes_accessed=6 << 20,
    )
    sums = call(
        sum_shares,
        shape((NSEQ, SHARE + EXT, 2 * HEAD), BF16),
        (arrived,),
        scratch=[pltpu.VMEM((EXT, 2 * HEAD), F32)],
        name="sum_shares",
    )
    arrived = lax.all_to_all(sums, SEQ, 0, 0, tiled=True)
    grad_query, grad_key, grad_value, grad_score, loss = call(
        unpack,
        (
            shape((ROWS, HEAD), F32),
            shape((ROWS, HEAD), F32),
            shape((ROWS, HEAD), F32),
            shape((1, HEAD), F32),
            shape((1, HEAD), F32),
        ),
        (group.reshape(1).astype(jnp.int32), arrived, score),
        name="unpack",
    )
    return (
        loss[0, 0],
        grad_query,
        grad_key,
        grad_value,
        grad_score.reshape(HEAD),
        grad_hidden.reshape(1, BLK, NDP * ROWS),
    )


def solution(mesh):
    parts = Mesh(mesh.devices.reshape(NZ, NX, NC, 4, 2), DP + SEQ)
    return jax.shard_map(
        per_device,
        mesh=parts,
        in_specs=(P(DP, SEQ, None), P(DP, None), P(DP, None), P(DP, None), P(), P(), P(), P()),
        out_specs=(P(), P(DP, None), P(DP, None), P(DP, None), P(), P(DP, SEQ, None)),
        check_vma=False,
    )
```

time: 748 us -> 232 us (0.31)
  waiting for transfers between devices: 497 us -> 32.8 us
  blocking collectives: 186 us -> 92.1 us
  starting transfers between devices: 0.32 us -> 47 us
  Pallas kernels: 0 us -> 26.2 us
  matrix products: 19.6 us -> 0 us
  between operations: 17.1 us -> 5.21 us
  local copies, waits for them, and re-layouts: 17.6 us -> 26.4 us
  other arithmetic: 8.58 us -> 0.02 us
    all_gather x5 -> x0, waiting for transfers between devices: 321 us -> none  [the longest x1 67.6 us: per_device(): lax.all_gather(w_query, 'dp', axis=0, tiled=True)]
    psum x3 -> x0, blocking collectives: 153 us -> none  [the longest x1 77.8 us: per_device(): grad_score = lax.psum(readout_part, ('dp', 'seq'))]
    psum x1 -> x0, waiting for transfers between devices: 87.4 us -> none  [per_device(): summed = lax.psum(shares, 'seq')]
    reduce_scatter x2 -> x0, waiting for transfers between devices: 86.6 us -> none  [the longest x1 70 us: per_device(): lax.psum_scatter(mate_grads, 'seq', scatter_dimension=0, tiled=True)]
    all_to_all x0 -> x2, blocking collectives: none -> 52.1 us  [the longest x1 29.8 us: per_device(): arrived = lax.all_to_all(shares, DP, 0, 0, tiled=True)]
    ppermute x0 -> x34, starting transfers between devices: none -> 27.2 us  [the longest x7 18.4 us: gather_weights(): found[step, x] = lax.ppermute(found[step - 1, x], 'z', down)]
    pallas_call x0 -> x10, Pallas kernels: none -> 26.2 us  [call(): pl.pallas_call(kernel, out_shape=outs, in_specs=[SM if a.dtype == jnp.int...]
    ppermute x0 -> x34, waiting for transfers between devices: none -> 21.3 us  [the longest x7 11.4 us: gather_weights(): found[-step, x] = lax.ppermute(found[1 - step, x], 'z', up)]
  transfers between devices with their start and end apart: 8 -> 38, of which waited for: 8 -> 15; matrix products, arithmetic and copies ran while one was open for 2% -> 3% of each run, Pallas kernels for 0% -> 8%
where the time goes in v1:
time: 232 us; the launch traced here: 230 us
  blocking collectives  92.1 us (40%)
  starting transfers between devices  47 us (20%)
  waiting for transfers between devices  32.8 us (14%)
  local copies, waits for them, and re-layouts  26.4 us (11%)
  Pallas kernels  26.2 us (11%)
  between operations  5.21 us (2%)
    all_gather x1, blocking collectives, per_device(): value_rows = lax.all_gather(own_rows, DP, axis=0, tiled=True)  40.1 us
    all_to_all x1, blocking collectives, per_device(): arrived = lax.all_to_all(shares, DP, 0, 0, tiled=True)  29.8 us
    pallas_call x10, Pallas kernels, call(): pl.pallas_call(kernel, out_shape=outs, in_specs=[SM if a.dtype == jnp.int...  26.2 us
    all_to_all x1, blocking collectives, per_device(): arrived = lax.all_to_all(slots, 'z', 0, 0, tiled=True)  22.3 us
    unnamed x122, local copies, waits for them, and re-layouts  19.5 us
    ppermute x7, starting transfers between devices, gather_weights(): found[step, x] = lax.ppermute(found[step - 1, x], 'z', down)  18.4 us
    ppermute x7, waiting for transfers between devices, gather_weights(): found[-step, x] = lax.ppermute(found[1 - step, x], 'z', up)  11.4 us
    all_to_all x1, waiting for transfers between devices, per_device(): own = lax.all_to_all(payload, SEQ, 0, 0, tiled=True)  6.48 us
  transfers between devices with their start and end apart: 38, of which 15 were waited for; matrix products, arithmetic and copies ran while one was open for 3% of the time, Pallas kernels for 8%

profile of v1, /device:TPU:2, one launch (start us, length us, event | category | flops | bytes accessed | tf_op | source)
XLA Modules:
  0.0 229.8 jit_solution(8552086050886151572)
XLA Ops:
  0.6 0.8 copy-done.53
  1.5 0.8 copy-done.54
  2.3 0.8 copy-done.55
  3.2 0.7 copy-done.56
  4.0 2.4 %collective-permute-start.1 = (bf16[272,256]{1,0:T(8,128)(2,1)S(1)}, bf16[272,256]{1,0:T(8,128)(2,1)S(1)}, u32[]{:S(2)}, u32[]{:S(2)}) collective-permute-start(bf16[272,256]{1,0:T(8,128)(2,1)S(1)} %pack_weights.1.refs_0_), channel_id=1, source_target_pairs={{0,16},{16,0},{1,17},{17,1},{2,18},{18,2},{3,19},{19,3},{4,20},{20... | collective-permute-start | bytes 417800 | tf_op jit(solution)/shard_map/ppermute | solution.py:310
  6.5 3.9 %collective-permute-start.5 = (bf16[272,256]{1,0:T(8,128)(2,1)S(1)}, bf16[272,256]{1,0:T(8,128)(2,1)S(1)}, u32[]{:S(2)}, u32[]{:S(2)}) collective-permute-start(bf16[272,256]{1,0:T(8,128)(2,1)S(1)} %pack_weights.1.refs_0_), channel_id=1, source_target_pairs={{0,224},{32,0},{64,32},{96,64},{128,96},{160,128},{192,160},{224,1... | collective-permute-start | bytes 417800 | tf_op jit(solution)/shard_map/ppermute | solution.py:317
  10.5 4.9 %collective-permute-start.9 = (bf16[272,256]{1,0:T(8,128)(2,1)S(1)}, bf16[272,256]{1,0:T(8,128)(2,1)S(1)}, u32[]{:S(2)}, u32[]{:S(2)}) collective-permute-start(bf16[272,256]{1,0:T(8,128)(2,1)S(1)} %collective-permute-done.1.refs_2_), channel_id=1, source_target_pairs={{0,224},{32,0},{64,32},{96,64},{128,96},{160,128},{192,160},{224,1... | collective-permute-start | bytes 417800 | tf_op jit(solution)/shard_map/ppermute | solution.py:317
  15.4 3.3 %collective-permute-start.13 = (bf16[272,256]{1,0:T(8,128)(2,1)S(1)}, bf16[272,256]{1,0:T(8,128)(2,1)S(1)}, u32[]{:S(2)}, u32[]{:S(2)}) collective-permute-start(bf16[272,256]{1,0:T(8,128)(2,1)S(1)} %collective-permute-done.5.refs_6_), channel_id=1, source_target_pairs={{0,224},{32,0},{64,32},{96,64},{128,96},{160,128},{192,160},{224,1... | collective-permute-start | bytes 417800 | tf_op jit(solution)/shard_map/ppermute | solution.py:317
  19.2 3.1 %collective-permute-done.7.refs_8_ = bf16[272,256]{1,0:T(8,128)(2,1)S(1)} collective-permute-done((bf16[272,256]{1,0:T(8,128)(2,1)S(1)}, bf16[272,256]{1,0:T(8,128)(2,1)S(1)}, u32[]{:S(2)}, u32[]{:S(2)}) %collective-permute-start.7) | collective-permute-done | bytes 139296 | tf_op jit(solution)/shard_map/ppermute | solution.py:315
  22.3 1.5 collective-permute-done.11.refs_12_
  24.1 1.8 collective-permute-start.15
  25.9 3.1 %collective-permute-start.21 = (bf16[272,256]{1,0:T(8,128)(2,1)S(1)}, bf16[272,256]{1,0:T(8,128)(2,1)S(1)}, u32[]{:S(2)}, u32[]{:S(2)}) collective-permute-start(bf16[272,256]{1,0:T(8,128)(2,1)S(1)} %collective-permute-done.13.refs_14_), channel_id=1, source_target_pairs={{0,224},{32,0},{64,32},{96,64},{128,96},{160,128},{192,160},{224,1... | collective-permute-start | bytes 417800 | tf_op jit(solution)/shard_map/ppermute | solution.py:317
  29.1 0.9 collective-permute-done.17.refs_18_
  30.0 1.2 collective-permute-done.15.refs_16_
  31.2 1.5 collective-permute-done.19.refs_20_
  32.7 2.6 %collective-permute-start.25 = (bf16[272,256]{1,0:T(8,128)(2,1)S(1)}, bf16[272,256]{1,0:T(8,128)(2,1)S(1)}, u32[]{:S(2)}, u32[]{:S(2)}) collective-permute-start(bf16[272,256]{1,0:T(8,128)(2,1)S(1)} %collective-permute-done.17.refs_18_), channel_id=1, source_target_pairs={{0,224},{32,0},{64,32},{96,64},{128,96},{160,128},{192,160},{224,1... | collective-permute-start | bytes 417800 | tf_op jit(solution)/shard_map/ppermute | solution.py:317
  36.1 2.7 %collective-permute-done.25.refs_26_ = bf16[272,256]{1,0:T(8,128)(2,1)S(1)} collective-permute-done((bf16[272,256]{1,0:T(8,128)(2,1)S(1)}, bf16[272,256]{1,0:T(8,128)(2,1)S(1)}, u32[]{:S(2)}, u32[]{:S(2)}) %collective-permute-start.25) | collective-permute-done | bytes 139296 | tf_op jit(solution)/shard_map/ppermute | solution.py:317
  38.8 2.8 %collective-permute-done.23.refs_24_ = bf16[272,256]{1,0:T(8,128)(2,1)S(1)} collective-permute-done((bf16[272,256]{1,0:T(8,128)(2,1)S(1)}, bf16[272,256]{1,0:T(8,128)(2,1)S(1)}, u32[]{:S(2)}, u32[]{:S(2)}) %collective-permute-start.23) | collective-permute-done | bytes 139296 | tf_op jit(solution)/shard_map/ppermute | solution.py:315
  41.9 1.2 collective-permute-done.27.refs_28_
  43.1 0.7 copy-done.44
  44.3 0.7 copy-done.47
  45.0 0.7 copy-done.50
  46.1 0.7 collective-permute-done.29.refs_30_
  47.2 1.2 collective-permute-done.30.refs_31_
  48.5 0.9 copy-done.45
  49.4 0.9 copy-done.48
  50.3 0.9 copy-done.51
  51.2 3.9 %project.1 = bf16[8,144,256]{2,1,0:T(8,128)(2,1)} custom-call(s32[33]{0:T(128)S(1)} %stack.140.ids, bf16[128,8192]{1,0:T(8,128)(2,1)} %bitcast.48, bf16[272,256]{1,0:T(8,128)(2,1)S(1)} %pack_weights.1.refs_0_, bf16[272,256]{1,0:T(8,128)(2,1)S(1)} %collective-permute-done.refs_1_, bf16[272,256]{1,0:T(8,128)(2,1)S(1)} %collective-permute-done.1.refs_2_, ...), custom_call_target="tpu_custom_call" | custom-call | flops 536870912 | bytes 6291456 | tf_op jit(solution)/shard_map/project/pallas_call | solution.py:33
  55.3 0.9 slice_bitcast_fusion.a
  56.3 0.6 gather_fusion
  57.0 0.6 collective-permute-start.32
  57.6 1.5 collective-permute-start.33
  59.1 3.0 %collective-permute-done.32.c = bf16[144,256]{1,0:T(8,128)(2,1)S(1)} collective-permute-done((bf16[144,256]{1,0:T(8,128)(2,1)S(1)}, bf16[144,256]{1,0:T(8,128)(2,1)S(1)}, u32[]{:S(2)}, u32[]{:S(2)}) %collective-permute-start.32) | collective-permute-done | bytes 73760 | tf_op jit(solution)/shard_map/ppermute | solution.py:358
  62.2 1.0 collective-permute-done.33.d
  63.8 22.3 %all_to_all.30.received = bf16[8,144,256]{2,1,0:T(8,128)(2,1)S(1)} all-to-all(bf16[8,144,256]{2,1,0:T(8,128)(2,1)S(1)} %pick_for_planes.1), channel_id=1, replica_groups=mesh['z'=8,'xl'=2,'c'=2,'y'=4,'xh'=2] {'z'}, dimensions={0} | all-to-all | bytes 1179648 | tf_op jit(solution)/shard_map/all_to_all | solution.py:369
  86.0 6.1 %all-to-all-start.1 = ((bf16[8,144,256]{2,1,0:T(8,128)(2,1)}), bf16[8,144,256]{2,1,0:T(8,128)(2,1)S(1)}, u32[]{:S(2)}, u32[]{:S(2)}) async-start(bf16[8,144,256]{2,1,0:T(8,128)(2,1)} %project.1), calls=%async_computation.1 | async-start | bytes 1179648 | tf_op jit(solution)/shard_map/all_to_all | solution.py:355
  95.3 0.9 pick_partner.1
  96.2 6.5 %all-to-all-done.1.own = bf16[8,144,256]{2,1,0:T(8,128)(2,1)S(1)} async-done(((bf16[8,144,256]{2,1,0:T(8,128)(2,1)}), bf16[8,144,256]{2,1,0:T(8,128)(2,1)S(1)}, u32[]{:S(2)}, u32[]{:S(2)}) %all-to-all-start.1) | async-done | bytes 589856 | tf_op jit(solution)/shard_map/all_to_all | solution.py:355
  102.7 3.8 %all-to-all-start.3 = ((bf16[8,144,256]{2,1,0:T(8,128)(2,1)}), bf16[8,144,256]{2,1,0:T(8,128)(2,1)S(1)}, u32[]{:S(2)}, u32[]{:S(2)}) async-start(bf16[8,144,256]{2,1,0:T(8,128)(2,1)} %pick_partner.1), calls=%async_computation.3 | async-start | bytes 1179648 | tf_op jit(solution)/shard_map/all_to_all | solution.py:376
  106.5 3.9 %split_columns.1 = bf16[8,1024,128]{2,1,0:T(8,128)(2,1)S(1)} custom-call(bf16[128,8192]{1,0:T(8,128)(2,1)} %bitcast.49), custom_call_target="tpu_custom_call" | custom-call | flops 1073741824 | tf_op jit(solution)/shard_map/split_columns/pallas_call | solution.py:33
  110.4 1.3 copy-done
  111.8 5.0 %all-to-all-done.3.mate = bf16[8,144,256]{2,1,0:T(8,128)(2,1)S(1)} async-done(((bf16[8,144,256]{2,1,0:T(8,128)(2,1)}), bf16[8,144,256]{2,1,0:T(8,128)(2,1)S(1)}, u32[]{:S(2)}, u32[]{:S(2)}) %all-to-all-start.3) | async-done | bytes 589856 | tf_op jit(solution)/shard_map/all_to_all | solution.py:376
  116.7 0.8 copy-done.4
  117.6 3.6 %all-to-all-start = ((bf16[8,1024,128]{2,1,0:T(8,128)(2,1)}), bf16[8,1024,128]{2,1,0:T(8,128)(2,1)S(1)}, u32[]{:S(2)}, u32[]{:S(2)}) async-start(bf16[8,1024,128]{2,1,0:T(8,128)(2,1)} %copy-done), calls=%async_computation | async-start | bytes 4194304 | tf_op jit(solution)/shard_map/all_to_all | solution.py:343
  123.1 3.3 %stack.106.ids = s32[6]{0:T(128)S(1)} concatenate(s32[1]{0:T(128)} %get-tuple-element.26, s32[1]{0:T(128)} %get-tuple-element.27, s32[1]{0:T(128)} %get-tuple-element.23, s32[1]{0:T(128)} %get-tuple-element.22, s32[1]{0:T(128)} %bitcast.ids, s32[1]{0:T(128)} %dynamic_slice.19), dimensions={0} | concatenate | bytes 48 | tf_op jit(solution)/shard_map/stack | solution.py:378
  126.4 0.7 constant_dynamic-slice_fusion
  127.1 40.1 %all_gather.3.value_rows = bf16[1024,128]{1,0:T(8,128)(2,1)S(1)} all-gather(bf16[32,128]{1,0:T(8,128)(2,1)S(1)} %constant_dynamic-slice_fusion), channel_id=1, replica_groups=mesh['z'=8,'xl'=2,'c'=2,'y'=4,'xh'=2] {'z','xl','c'}, dimensions={0}, use_global_device_ids=true | all-gather | bytes 270336 | tf_op jit(solution)/shard_map/all_gather | solution.py:345
  167.2 1.1 copy-done.3
  168.3 1.1 copy-done.5
  169.3 8.5 %attention.1 = (bf16[8,128,256]{2,1,0:T(8,128)(2,1)S(1)}, bf16[8,16,128]{2,1,0:T(8,128)(2,1)S(1)}, f32[8,128]{1,0:T(8,128)S(1)}) custom-call(s32[6]{0:T(128)S(1)} %stack.106.ids, bf16[8,144,256]{2,1,0:T(8,128)(2,1)S(1)} %copy-done.3, bf16[8,144,256]{2,1,0:T(8,128)(2,1)S(1)} %copy-done.5), custom_call_target="tpu_custom_call" | custom-call | flops 2147483648 | tf_op jit(solution)/shard_map/attention/pallas_call | solution.py:33
  177.9 1.8 weight_grads.1
  179.8 29.8 %all_to_all.31.received = bf16[32,48,256]{2,1,0:T(8,128)(2,1)S(1)} all-to-all(bf16[32,48,256]{2,1,0:T(8,128)(2,1)S(1)} %weight_grads.1), channel_id=1, replica_groups=mesh['z'=8,'xl'=2,'c'=2,'y'=4,'xh'=2] {'z','xl','c'}, dimensions={0} | all-to-all | bytes 1572864 | tf_op jit(solution)/shard_map/all_to_all | solution.py:408
  209.6 0.8 sum_shares.1
  210.4 6.3 %all-to-all-start.5 = ((bf16[8,48,256]{2,1,0:T(8,128)(2,1)}), bf16[8,48,256]{2,1,0:T(8,128)(2,1)S(1)}, u32[]{:S(2)}, u32[]{:S(2)}) async-start(bf16[8,48,256]{2,1,0:T(8,128)(2,1)} %sum_shares.1), calls=%async_computation.5 | async-start | bytes 393216 | tf_op jit(solution)/shard_map/all_to_all | solution.py:424
  216.8 0.9 copy-done.35
  217.7 0.9 copy-done.37
  218.6 0.9 copy-done.39
  219.5 0.9 copy-done.41
  220.4 0.9 copy-done.43
  221.3 0.9 copy-done.46
  222.2 0.9 copy-done.49
  223.2 0.9 copy-done.52
  224.1 4.9 %hidden_grads.1 = bf16[128,8192]{1,0:T(8,128)(2,1)} custom-call(s32[33]{0:T(128)S(1)} %stack.140.ids, bf16[8,128,256]{2,1,0:T(8,128)(2,1)} %copy-done.1, bf16[8,16,128]{2,1,0:T(8,128)(2,1)S(1)} %get-tuple-element.15.crows, bf16[272,256]{1,0:T(8,128)(2,1)S(1)} %pack_weights.1.refs_0_, bf16[272,256]{1,0:T(8,128)(2,1)S(1)} %copy-done.7, ...), custom_call_target="tpu_custom_call" | custom-call | flops 536870912 | bytes 6291456 | tf_op jit(solution)/shard_map/hidden_grads/pallas_call | solution.py:33
  228.9 0.8 unpack.1
  (157 shorter events, 5.7 us)
Async XLA Ops:
  4.0 6.5 %collective-permute-start.1 = (bf16[272,256]{1,0:T(8,128)(2,1)S(1)}, bf16[272,256]{1,0:T(8,128)(2,1)S(1)}, u32[]{:S(2)}, u32[]{:S(2)}) collective-permute-start(bf16[272,256]{1,0:T(8,128)(2,1)S(1)} %pack_weights.1.refs_0_), channel_id=1, source_target_pairs={{0,16},{16,0},{1,17},{17,1},{2,18},{18,2},{3,19},{19,3},{4,20},{20... | collective-permute-start | bytes 417800 | tf_op jit(solution)/shard_map/ppermute | solution.py:310
  6.3 9.0 %collective-permute-start.3 = (bf16[272,256]{1,0:T(8,128)(2,1)S(1)}, bf16[272,256]{1,0:T(8,128)(2,1)S(1)}, u32[]{:S(2)}, u32[]{:S(2)}) collective-permute-start(bf16[272,256]{1,0:T(8,128)(2,1)S(1)} %pack_weights.1.refs_0_), channel_id=1, source_target_pairs={{0,32},{32,64},{64,96},{96,128},{128,160},{160,192},{192,224},{224... | collective-permute-start | bytes 417800 | tf_op jit(solution)/shard_map/ppermute | solution.py:315
  6.5 8.8 %collective-permute-start.5 = (bf16[272,256]{1,0:T(8,128)(2,1)S(1)}, bf16[272,256]{1,0:T(8,128)(2,1)S(1)}, u32[]{:S(2)}, u32[]{:S(2)}) collective-permute-start(bf16[272,256]{1,0:T(8,128)(2,1)S(1)} %pack_weights.1.refs_0_), channel_id=1, source_target_pairs={{0,224},{32,0},{64,32},{96,64},{128,96},{160,128},{192,160},{224,1... | collective-permute-start | bytes 417800 | tf_op jit(solution)/shard_map/ppermute | solution.py:317
  10.5 8.2 %collective-permute-start = (bf16[272,256]{1,0:T(8,128)(2,1)S(1)}, bf16[272,256]{1,0:T(8,128)(2,1)S(1)}, u32[]{:S(2)}, u32[]{:S(2)}) collective-permute-start(bf16[272,256]{1,0:T(8,128)(2,1)S(1)} %pack_weights.1.refs_0_), channel_id=1, source_target_pairs={{0,8},{8,0},{1,9},{9,1},{2,10},{10,2},{3,11},{11,3},{4,12},{12,4},... | collective-permute-start | bytes 417800 | tf_op jit(solution)/shard_map/ppermute | solution.py:321
  10.5 8.2 %collective-permute-start.9 = (bf16[272,256]{1,0:T(8,128)(2,1)S(1)}, bf16[272,256]{1,0:T(8,128)(2,1)S(1)}, u32[]{:S(2)}, u32[]{:S(2)}) collective-permute-start(bf16[272,256]{1,0:T(8,128)(2,1)S(1)} %collective-permute-done.1.refs_2_), channel_id=1, source_target_pairs={{0,224},{32,0},{64,32},{96,64},{128,96},{160,128},{192,160},{224,1... | collective-permute-start | bytes 417800 | tf_op jit(solution)/shard_map/ppermute | solution.py:317
  15.3 7.0 %collective-permute-start.7 = (bf16[272,256]{1,0:T(8,128)(2,1)S(1)}, bf16[272,256]{1,0:T(8,128)(2,1)S(1)}, u32[]{:S(2)}, u32[]{:S(2)}) collective-permute-start(bf16[272,256]{1,0:T(8,128)(2,1)S(1)} %collective-permute-done.1.refs_2_), channel_id=1, source_target_pairs={{0,32},{32,64},{64,96},{96,128},{128,160},{160,192},{192,224},{224... | collective-permute-start | bytes 417800 | tf_op jit(solution)/shard_map/ppermute | solution.py:315
  15.3 8.4 %collective-permute-start.11 = (bf16[272,256]{1,0:T(8,128)(2,1)S(1)}, bf16[272,256]{1,0:T(8,128)(2,1)S(1)}, u32[]{:S(2)}, u32[]{:S(2)}) collective-permute-start(bf16[272,256]{1,0:T(8,128)(2,1)S(1)} %collective-permute-done.3.refs_4_), channel_id=1, source_target_pairs={{0,32},{32,64},{64,96},{96,128},{128,160},{160,192},{192,224},{224... | collective-permute-start | bytes 417800 | tf_op jit(solution)/shard_map/ppermute | solution.py:315
  15.4 8.7 %collective-permute-start.13 = (bf16[272,256]{1,0:T(8,128)(2,1)S(1)}, bf16[272,256]{1,0:T(8,128)(2,1)S(1)}, u32[]{:S(2)}, u32[]{:S(2)}) collective-permute-start(bf16[272,256]{1,0:T(8,128)(2,1)S(1)} %collective-permute-done.5.refs_6_), channel_id=1, source_target_pairs={{0,224},{32,0},{64,32},{96,64},{128,96},{160,128},{192,160},{224,1... | collective-permute-start | bytes 417800 | tf_op jit(solution)/shard_map/ppermute | solution.py:317
  18.7 36.4 %copy-start.6 = (bf16[272,256]{1,0:T(8,128)(2,1)}, bf16[272,256]{1,0:T(8,128)(2,1)S(1)}, u32[]{:S(2)}) copy-start(bf16[272,256]{1,0:T(8,128)(2,1)S(1)} %collective-permute-done.refs_1_) | copy-start | bytes 417796
  18.7 7.2 %collective-permute-start.2 = (bf16[272,256]{1,0:T(8,128)(2,1)S(1)}, bf16[272,256]{1,0:T(8,128)(2,1)S(1)}, u32[]{:S(2)}, u32[]{:S(2)}) collective-permute-start(bf16[272,256]{1,0:T(8,128)(2,1)S(1)} %collective-permute-done.1.refs_2_), channel_id=1, source_target_pairs={{0,8},{8,0},{1,9},{9,1},{2,10},{10,2},{3,11},{11,3},{4,12},{12,4},... | collective-permute-start | bytes 417800 | tf_op jit(solution)/shard_map/ppermute | solution.py:321
  18.7 36.4 %copy-start.8 = (bf16[272,256]{1,0:T(8,128)(2,1)}, bf16[272,256]{1,0:T(8,128)(2,1)S(1)}, u32[]{:S(2)}) copy-start(bf16[272,256]{1,0:T(8,128)(2,1)S(1)} %collective-permute-done.9.refs_10_) | copy-start | bytes 417796
  18.7 7.2 %collective-permute-start.4 = (bf16[272,256]{1,0:T(8,128)(2,1)S(1)}, bf16[272,256]{1,0:T(8,128)(2,1)S(1)}, u32[]{:S(2)}, u32[]{:S(2)}) collective-permute-start(bf16[272,256]{1,0:T(8,128)(2,1)S(1)} %collective-permute-done.3.refs_4_), channel_id=1, source_target_pairs={{0,8},{8,0},{1,9},{9,1},{2,10},{10,2},{3,11},{11,3},{4,12},{12,4},... | collective-permute-start | bytes 417800 | tf_op jit(solution)/shard_map/ppermute | solution.py:321
  22.3 32.8 %copy-start.10 = (bf16[272,256]{1,0:T(8,128)(2,1)}, bf16[272,256]{1,0:T(8,128)(2,1)S(1)}, u32[]{:S(2)}) copy-start(bf16[272,256]{1,0:T(8,128)(2,1)S(1)} %collective-permute-done.7.refs_8_) | copy-start | bytes 417796
  22.3 6.8 %collective-permute-start.6 = (bf16[272,256]{1,0:T(8,128)(2,1)S(1)}, bf16[272,256]{1,0:T(8,128)(2,1)S(1)}, u32[]{:S(2)}, u32[]{:S(2)}) collective-permute-start(bf16[272,256]{1,0:T(8,128)(2,1)S(1)} %collective-permute-done.5.refs_6_), channel_id=1, source_target_pairs={{0,8},{8,0},{1,9},{9,1},{2,10},{10,2},{3,11},{11,3},{4,12},{12,4},... | collective-permute-start | bytes 417800 | tf_op jit(solution)/shard_map/ppermute | solution.py:321
  23.8 31.3 %copy-start.12 = (bf16[272,256]{1,0:T(8,128)(2,1)}, bf16[272,256]{1,0:T(8,128)(2,1)S(1)}, u32[]{:S(2)}) copy-start(bf16[272,256]{1,0:T(8,128)(2,1)S(1)} %collective-permute-done.11.refs_12_) | copy-start | bytes 417796
  23.8 6.2 %collective-permute-start.17 = (bf16[272,256]{1,0:T(8,128)(2,1)S(1)}, bf16[272,256]{1,0:T(8,128)(2,1)S(1)}, u32[]{:S(2)}, u32[]{:S(2)}) collective-permute-start(bf16[272,256]{1,0:T(8,128)(2,1)S(1)} %collective-permute-done.9.refs_10_), channel_id=1, source_target_pairs={{0,224},{32,0},{64,32},{96,64},{128,96},{160,128},{192,160},{224,1... | collective-permute-start | bytes 417800 | tf_op jit(solution)/shard_map/ppermute | solution.py:317
  24.1 31.1 %copy-start.14 = (bf16[272,256]{1,0:T(8,128)(2,1)}, bf16[272,256]{1,0:T(8,128)(2,1)S(1)}, u32[]{:S(2)}) copy-start(bf16[272,256]{1,0:T(8,128)(2,1)S(1)} %collective-permute-done.13.refs_14_) | copy-start | bytes 417796
  24.1 7.1 %collective-permute-start.15 = (bf16[272,256]{1,0:T(8,128)(2,1)S(1)}, bf16[272,256]{1,0:T(8,128)(2,1)S(1)}, u32[]{:S(2)}, u32[]{:S(2)}) collective-permute-start(bf16[272,256]{1,0:T(8,128)(2,1)S(1)} %collective-permute-done.7.refs_8_), channel_id=1, source_target_pairs={{0,32},{32,64},{64,96},{96,128},{128,160},{160,192},{192,224},{224... | collective-permute-start | bytes 417800 | tf_op jit(solution)/shard_map/ppermute | solution.py:315
  25.8 29.3 %copy-start.16 = (bf16[272,256]{1,0:T(8,128)(2,1)}, bf16[272,256]{1,0:T(8,128)(2,1)S(1)}, u32[]{:S(2)}) copy-start(bf16[272,256]{1,0:T(8,128)(2,1)S(1)} %collective-permute-done.2.refs_3_) | copy-start | bytes 417796
  25.8 6.9 %collective-permute-start.19 = (bf16[272,256]{1,0:T(8,128)(2,1)S(1)}, bf16[272,256]{1,0:T(8,128)(2,1)S(1)}, u32[]{:S(2)}, u32[]{:S(2)}) collective-permute-start(bf16[272,256]{1,0:T(8,128)(2,1)S(1)} %collective-permute-done.11.refs_12_), channel_id=1, source_target_pairs={{0,32},{32,64},{64,96},{96,128},{128,160},{160,192},{192,224},{224... | collective-permute-start | bytes 417800 | tf_op jit(solution)/shard_map/ppermute | solution.py:315
  25.9 29.2 %copy-start.18 = (bf16[272,256]{1,0:T(8,128)(2,1)}, bf16[272,256]{1,0:T(8,128)(2,1)S(1)}, u32[]{:S(2)}) copy-start(bf16[272,256]{1,0:T(8,128)(2,1)S(1)} %collective-permute-done.4.refs_5_) | copy-start | bytes 417796
  25.9 6.8 %collective-permute-start.21 = (bf16[272,256]{1,0:T(8,128)(2,1)S(1)}, bf16[272,256]{1,0:T(8,128)(2,1)S(1)}, u32[]{:S(2)}, u32[]{:S(2)}) collective-permute-start(bf16[272,256]{1,0:T(8,128)(2,1)S(1)} %collective-permute-done.13.refs_14_), channel_id=1, source_target_pairs={{0,224},{32,0},{64,32},{96,64},{128,96},{160,128},{192,160},{224,1... | collective-permute-start | bytes 417800 | tf_op jit(solution)/shard_map/ppermute | solution.py:317
  29.1 26.1 %copy-start.20 = (bf16[272,256]{1,0:T(8,128)(2,1)}, bf16[272,256]{1,0:T(8,128)(2,1)S(1)}, u32[]{:S(2)}) copy-start(bf16[272,256]{1,0:T(8,128)(2,1)S(1)} %collective-permute-done.6.refs_7_) | copy-start | bytes 417796
  29.1 6.3 %collective-permute-start.10 = (bf16[272,256]{1,0:T(8,128)(2,1)S(1)}, bf16[272,256]{1,0:T(8,128)(2,1)S(1)}, u32[]{:S(2)}, u32[]{:S(2)}) collective-permute-start(bf16[272,256]{1,0:T(8,128)(2,1)S(1)} %collective-permute-done.9.refs_10_), channel_id=1, source_target_pairs={{0,8},{8,0},{1,9},{9,1},{2,10},{10,2},{3,11},{11,3},{4,12},{12,4},... | collective-permute-start | bytes 417800 | tf_op jit(solution)/shard_map/ppermute | solution.py:321
  30.0 25.2 %copy-start.22 = (bf16[272,256]{1,0:T(8,128)(2,1)}, bf16[272,256]{1,0:T(8,128)(2,1)S(1)}, u32[]{:S(2)}) copy-start(bf16[272,256]{1,0:T(8,128)(2,1)S(1)} %collective-permute-done.17.refs_18_) | copy-start | bytes 417796
  30.0 5.4 %collective-permute-start.8 = (bf16[272,256]{1,0:T(8,128)(2,1)S(1)}, bf16[272,256]{1,0:T(8,128)(2,1)S(1)}, u32[]{:S(2)}, u32[]{:S(2)}) collective-permute-start(bf16[272,256]{1,0:T(8,128)(2,1)S(1)} %collective-permute-done.7.refs_8_), channel_id=1, source_target_pairs={{0,8},{8,0},{1,9},{9,1},{2,10},{10,2},{3,11},{11,3},{4,12},{12,4},... | collective-permute-start | bytes 417800 | tf_op jit(solution)/shard_map/ppermute | solution.py:321
  31.2 24.0 %copy-start.24 = (bf16[272,256]{1,0:T(8,128)(2,1)}, bf16[272,256]{1,0:T(8,128)(2,1)S(1)}, u32[]{:S(2)}) copy-start(bf16[272,256]{1,0:T(8,128)(2,1)S(1)} %collective-permute-done.15.refs_16_) | copy-start | bytes 417796
  31.2 4.3 %collective-permute-start.12 = (bf16[272,256]{1,0:T(8,128)(2,1)S(1)}, bf16[272,256]{1,0:T(8,128)(2,1)S(1)}, u32[]{:S(2)}, u32[]{:S(2)}) collective-permute-start(bf16[272,256]{1,0:T(8,128)(2,1)S(1)} %collective-permute-done.11.refs_12_), channel_id=1, source_target_pairs={{0,8},{8,0},{1,9},{9,1},{2,10},{10,2},{3,11},{11,3},{4,12},{12,4},... | collective-permute-start | bytes 417800 | tf_op jit(solution)/shard_map/ppermute | solution.py:321
  32.7 22.5 %copy-start.26 = (bf16[272,256]{1,0:T(8,128)(2,1)}, bf16[272,256]{1,0:T(8,128)(2,1)S(1)}, u32[]{:S(2)}) copy-start(bf16[272,256]{1,0:T(8,128)(2,1)S(1)} %collective-permute-done.19.refs_20_) | copy-start | bytes 417796
  32.7 2.9 %collective-permute-start.14 = (bf16[272,256]{1,0:T(8,128)(2,1)S(1)}, bf16[272,256]{1,0:T(8,128)(2,1)S(1)}, u32[]{:S(2)}, u32[]{:S(2)}) collective-permute-start(bf16[272,256]{1,0:T(8,128)(2,1)S(1)} %collective-permute-done.13.refs_14_), channel_id=1, source_target_pairs={{0,8},{8,0},{1,9},{9,1},{2,10},{10,2},{3,11},{11,3},{4,12},{12,4},... | collective-permute-start | bytes 417800 | tf_op jit(solution)/shard_map/ppermute | solution.py:321
  32.7 6.1 %collective-permute-start.25 = (bf16[272,256]{1,0:T(8,128)(2,1)S(1)}, bf16[272,256]{1,0:T(8,128)(2,1)S(1)}, u32[]{:S(2)}, u32[]{:S(2)}) collective-permute-start(bf16[272,256]{1,0:T(8,128)(2,1)S(1)} %collective-permute-done.17.refs_18_), channel_id=1, source_target_pairs={{0,224},{32,0},{64,32},{96,64},{128,96},{160,128},{192,160},{224,1... | collective-permute-start | bytes 417800 | tf_op jit(solution)/shard_map/ppermute | solution.py:317
  35.3 6.3 %collective-permute-start.23 = (bf16[272,256]{1,0:T(8,128)(2,1)S(1)}, bf16[272,256]{1,0:T(8,128)(2,1)S(1)}, u32[]{:S(2)}, u32[]{:S(2)}) collective-permute-start(bf16[272,256]{1,0:T(8,128)(2,1)S(1)} %collective-permute-done.15.refs_16_), channel_id=1, source_target_pairs={{0,32},{32,64},{64,96},{96,128},{128,160},{160,192},{192,224},{224... | collective-permute-start | bytes 417800 | tf_op jit(solution)/shard_map/ppermute | solution.py:315
  35.4 7.7 %collective-permute-start.27 = (bf16[272,256]{1,0:T(8,128)(2,1)S(1)}, bf16[272,256]{1,0:T(8,128)(2,1)S(1)}, u32[]{:S(2)}, u32[]{:S(2)}) collective-permute-start(bf16[272,256]{1,0:T(8,128)(2,1)S(1)} %collective-permute-done.19.refs_20_), channel_id=1, source_target_pairs={{0,32},{32,64},{64,96},{96,128},{128,160},{160,192},{192,224},{224... | collective-permute-start | bytes 417800 | tf_op jit(solution)/shard_map/ppermute | solution.py:315
  35.5 7.6 %collective-permute-start.16 = (bf16[272,256]{1,0:T(8,128)(2,1)S(1)}, bf16[272,256]{1,0:T(8,128)(2,1)S(1)}, u32[]{:S(2)}, u32[]{:S(2)}) collective-permute-start(bf16[272,256]{1,0:T(8,128)(2,1)S(1)} %collective-permute-done.15.refs_16_), channel_id=1, source_target_pairs={{0,8},{8,0},{1,9},{9,1},{2,10},{10,2},{3,11},{11,3},{4,12},{12,4},... | collective-permute-start | bytes 417800 | tf_op jit(solution)/shard_map/ppermute | solution.py:321
  35.6 8.7 %collective-permute-start.18 = (bf16[272,256]{1,0:T(8,128)(2,1)S(1)}, bf16[272,256]{1,0:T(8,128)(2,1)S(1)}, u32[]{:S(2)}, u32[]{:S(2)}) collective-permute-start(bf16[272,256]{1,0:T(8,128)(2,1)S(1)} %collective-permute-done.17.refs_18_), channel_id=1, source_target_pairs={{0,8},{8,0},{1,9},{9,1},{2,10},{10,2},{3,11},{11,3},{4,12},{12,4},... | collective-permute-start | bytes 417800 | tf_op jit(solution)/shard_map/ppermute | solution.py:321
  38.8 6.2 %collective-permute-start.20 = (bf16[272,256]{1,0:T(8,128)(2,1)S(1)}, bf16[272,256]{1,0:T(8,128)(2,1)S(1)}, u32[]{:S(2)}, u32[]{:S(2)}) collective-permute-start(bf16[272,256]{1,0:T(8,128)(2,1)S(1)} %collective-permute-done.19.refs_20_), channel_id=1, source_target_pairs={{0,8},{8,0},{1,9},{9,1},{2,10},{10,2},{3,11},{11,3},{4,12},{12,4},... | collective-permute-start | bytes 417800 | tf_op jit(solution)/shard_map/ppermute | solution.py:321
  41.6 5.2 %collective-permute-start.29 = (bf16[272,256]{1,0:T(8,128)(2,1)S(1)}, bf16[272,256]{1,0:T(8,128)(2,1)}, u32[]{:S(2)}, u32[]{:S(2)}) collective-permute-start(bf16[272,256]{1,0:T(8,128)(2,1)S(1)} %collective-permute-done.25.refs_26_), channel_id=1, source_target_pairs={{0,224},{32,0},{64,32},{96,64},{128,96},{160,128},{192,160},{224,1... | collective-permute-start | bytes 417800 | tf_op jit(solution)/shard_map/ppermute | solution.py:317
  43.1 3.8 %collective-permute-start.22 = (bf16[272,256]{1,0:T(8,128)(2,1)S(1)}, bf16[272,256]{1,0:T(8,128)(2,1)}, u32[]{:S(2)}, u32[]{:S(2)}) collective-permute-start(bf16[272,256]{1,0:T(8,128)(2,1)S(1)} %collective-permute-done.21.refs_22_), channel_id=1, source_target_pairs={{0,8},{8,0},{1,9},{9,1},{2,10},{10,2},{3,11},{11,3},{4,12},{12,4},... | collective-permute-start | bytes 417800 | tf_op jit(solution)/shard_map/ppermute | solution.py:321
  43.8 3.1 %collective-permute-start.26 = (bf16[272,256]{1,0:T(8,128)(2,1)S(1)}, bf16[272,256]{1,0:T(8,128)(2,1)}, u32[]{:S(2)}, u32[]{:S(2)}) collective-permute-start(bf16[272,256]{1,0:T(8,128)(2,1)S(1)} %collective-permute-done.25.refs_26_), channel_id=1, source_target_pairs={{0,8},{8,0},{1,9},{9,1},{2,10},{10,2},{3,11},{11,3},{4,12},{12,4},... | collective-permute-start | bytes 417800 | tf_op jit(solution)/shard_map/ppermute | solution.py:321
  44.9 2.0 collective-permute-start.24
  45.6 1.6 collective-permute-start.28
  46.8 1.7 collective-permute-start.30
  56.2 1.4 collective-permute-start.31
  57.0 5.2 %collective-permute-start.32 = (bf16[144,256]{1,0:T(8,128)(2,1)S(1)}, bf16[144,256]{1,0:T(8,128)(2,1)S(1)}, u32[]{:S(2)}, u32[]{:S(2)}) collective-permute-start(bf16[144,256]{1,0:T(8,128)(2,1)S(1)} %slice_bitcast_fusion.a), channel_id=1, source_target_pairs={{0,16},{16,0},{1,17},{17,1},{2,18},{18,2},{3,19},{19,3},{4,20},{20... | collective-permute-start | bytes 221192 | tf_op jit(solution)/shard_map/ppermute | solution.py:358
  57.6 5.6 %collective-permute-start.33 = (bf16[144,256]{1,0:T(8,128)(2,1)S(1)}, bf16[144,256]{1,0:T(8,128)(2,1)S(1)}, u32[]{:S(2)}, u32[]{:S(2)}) collective-permute-start(bf16[144,256]{1,0:T(8,128)(2,1)S(1)} %collective-permute-done.31.b), channel_id=1, source_target_pairs={{0,16},{16,0},{1,17},{17,1},{2,18},{18,2},{3,19},{19,3},{4,20},{20... | collective-permute-start | bytes 221192 | tf_op jit(solution)/shard_map/ppermute | solution.py:359
  86.0 16.7 %all-to-all-start.1 = ((bf16[8,144,256]{2,1,0:T(8,128)(2,1)}), bf16[8,144,256]{2,1,0:T(8,128)(2,1)S(1)}, u32[]{:S(2)}, u32[]{:S(2)}) async-start(bf16[8,144,256]{2,1,0:T(8,128)(2,1)} %project.1), calls=%async_computation.1 | async-start | bytes 1179648 | tf_op jit(solution)/shard_map/all_to_all | solution.py:355
  102.7 14.0 %all-to-all-start.3 = ((bf16[8,144,256]{2,1,0:T(8,128)(2,1)}), bf16[8,144,256]{2,1,0:T(8,128)(2,1)S(1)}, u32[]{:S(2)}, u32[]{:S(2)}) async-start(bf16[8,144,256]{2,1,0:T(8,128)(2,1)} %pick_partner.1), calls=%async_computation.3 | async-start | bytes 1179648 | tf_op jit(solution)/shard_map/all_to_all | solution.py:376
  117.6 60.3 %all-to-all-start = ((bf16[8,1024,128]{2,1,0:T(8,128)(2,1)}), bf16[8,1024,128]{2,1,0:T(8,128)(2,1)S(1)}, u32[]{:S(2)}, u32[]{:S(2)}) async-start(bf16[8,1024,128]{2,1,0:T(8,128)(2,1)} %copy-done), calls=%async_computation | async-start | bytes 4194304 | tf_op jit(solution)/shard_map/all_to_all | solution.py:343
  177.8 31.7 %copy-start.1 = (bf16[8,128,256]{2,1,0:T(8,128)(2,1)}, bf16[8,128,256]{2,1,0:T(8,128)(2,1)S(1)}, u32[]{:S(2)}) copy-start(bf16[8,128,256]{2,1,0:T(8,128)(2,1)S(1)} %get-tuple-element.14.grads) | copy-start | bytes 1572868
  179.6 37.0 %copy-start.7 = (bf16[272,256]{1,0:T(8,128)(2,1)S(1)}, bf16[272,256]{1,0:T(8,128)(2,1)}, u32[]{:S(2)}) copy-start(bf16[272,256]{1,0:T(8,128)(2,1)} %copy-done.6) | copy-start | bytes 417796
  179.6 37.0 %copy-start.9 = (bf16[272,256]{1,0:T(8,128)(2,1)S(1)}, bf16[272,256]{1,0:T(8,128)(2,1)}, u32[]{:S(2)}) copy-start(bf16[272,256]{1,0:T(8,128)(2,1)} %copy-done.8) | copy-start | bytes 417796
  179.7 37.0 %copy-start.11 = (bf16[272,256]{1,0:T(8,128)(2,1)S(1)}, bf16[272,256]{1,0:T(8,128)(2,1)}, u32[]{:S(2)}) copy-start(bf16[272,256]{1,0:T(8,128)(2,1)} %copy-done.10) | copy-start | bytes 417796
  179.7 37.0 %copy-start.13 = (bf16[272,256]{1,0:T(8,128)(2,1)S(1)}, bf16[272,256]{1,0:T(8,128)(2,1)}, u32[]{:S(2)}) copy-start(bf16[272,256]{1,0:T(8,128)(2,1)} %copy-done.12) | copy-start | bytes 417796
  179.7 37.0 %copy-start.15 = (bf16[272,256]{1,0:T(8,128)(2,1)S(1)}, bf16[272,256]{1,0:T(8,128)(2,1)}, u32[]{:S(2)}) copy-start(bf16[272,256]{1,0:T(8,128)(2,1)} %copy-done.14) | copy-start | bytes 417796
  179.7 37.0 %copy-start.17 = (bf16[272,256]{1,0:T(8,128)(2,1)S(1)}, bf16[272,256]{1,0:T(8,128)(2,1)}, u32[]{:S(2)}) copy-start(bf16[272,256]{1,0:T(8,128)(2,1)} %copy-done.16) | copy-start | bytes 417796
  179.7 37.0 %copy-start.19 = (bf16[272,256]{1,0:T(8,128)(2,1)S(1)}, bf16[272,256]{1,0:T(8,128)(2,1)}, u32[]{:S(2)}) copy-start(bf16[272,256]{1,0:T(8,128)(2,1)} %copy-done.18) | copy-start | bytes 417796
  179.7 37.0 %copy-start.21 = (bf16[272,256]{1,0:T(8,128)(2,1)S(1)}, bf16[272,256]{1,0:T(8,128)(2,1)}, u32[]{:S(2)}) copy-start(bf16[272,256]{1,0:T(8,128)(2,1)} %copy-done.20) | copy-start | bytes 417796
  179.7 37.0 %copy-start.23 = (bf16[272,256]{1,0:T(8,128)(2,1)S(1)}, bf16[272,256]{1,0:T(8,128)(2,1)}, u32[]{:S(2)}) copy-start(bf16[272,256]{1,0:T(8,128)(2,1)} %copy-done.22) | copy-start | bytes 417796
  179.7 37.0 %copy-start.25 = (bf16[272,256]{1,0:T(8,128)(2,1)S(1)}, bf16[272,256]{1,0:T(8,128)(2,1)}, u32[]{:S(2)}) copy-start(bf16[272,256]{1,0:T(8,128)(2,1)} %copy-done.24) | copy-start | bytes 417796
  179.7 37.0 %copy-start.27 = (bf16[272,256]{1,0:T(8,128)(2,1)S(1)}, bf16[272,256]{1,0:T(8,128)(2,1)}, u32[]{:S(2)}) copy-start(bf16[272,256]{1,0:T(8,128)(2,1)} %copy-done.26) | copy-start | bytes 417796
  179.7 37.0 %copy-start.29 = (bf16[272,256]{1,0:T(8,128)(2,1)S(1)}, bf16[272,256]{1,0:T(8,128)(2,1)}, u32[]{:S(2)}) copy-start(bf16[272,256]{1,0:T(8,128)(2,1)} %copy-done.28) | copy-start | bytes 417796
  179.8 37.0 %copy-start.31 = (bf16[272,256]{1,0:T(8,128)(2,1)S(1)}, bf16[272,256]{1,0:T(8,128)(2,1)}, u32[]{:S(2)}) copy-start(bf16[272,256]{1,0:T(8,128)(2,1)} %copy-done.30) | copy-start | bytes 417796
  179.8 37.0 %copy-start.33 = (bf16[272,256]{1,0:T(8,128)(2,1)S(1)}, bf16[272,256]{1,0:T(8,128)(2,1)}, u32[]{:S(2)}) copy-start(bf16[272,256]{1,0:T(8,128)(2,1)} %copy-done.32) | copy-start | bytes 417796
  210.4 18.6 %all-to-all-start.5 = ((bf16[8,48,256]{2,1,0:T(8,128)(2,1)}), bf16[8,48,256]{2,1,0:T(8,128)(2,1)S(1)}, u32[]{:S(2)}, u32[]{:S(2)}) async-start(bf16[8,48,256]{2,1,0:T(8,128)(2,1)} %sum_shares.1), calls=%async_computation.5 | async-start | bytes 393216 | tf_op jit(solution)/shard_map/all_to_all | solution.py:424
  (35 other events, 202.5 us)

commit v2 on v1

v2 whole, which is shorter than its diff:
```python
import functools
import math

import jax
import jax.numpy as jnp
from jax import lax
from jax.experimental import pallas as pl
from jax.experimental.pallas import tpu as pltpu
from jax.sharding import Mesh
from jax.sharding import PartitionSpec as P

F32 = jnp.float32
BF16 = jnp.bfloat16
NZ, NX, NC = 8, 2, 2
NDP = NZ * NX * NC
NSEQ = 8
BLK = 128
HEAD = 128
ROWS = 256
EXT = 16
BLOCK = ROWS + 2 * EXT
SHARE = ROWS // NSEQ
COLS = NDP * SHARE
SEQLEN = NSEQ * BLK
TB = 256
DP = ("z", "xl", "c")
SEQ = ("y", "xh")
LAST = (((1,), (1,)), ((), ()))
VM = pl.BlockSpec(memory_space=pltpu.VMEM)
SM = pl.BlockSpec(memory_space=pltpu.SMEM)
HBM = pl.BlockSpec(memory_space=pltpu.HBM)
WINDOW, GROUP, WANTED, MATE_STEP, HEADS, CORE = 16, 17, 18, 26, 27, 33


def call(kernel, outs, ins, scratch=(), far=(), far_out=(), flops=0, bytes_accessed=0, name=None, limit=48):
    return pl.pallas_call(
        kernel,
        out_shape=outs,
        in_specs=[SM if a.dtype == jnp.int32 else HBM if n in far else VM for n, a in enumerate(ins)],
        out_specs=jax.tree.map(lambda o: SM if o.dtype == jnp.int32 else HBM if o.shape in far_out else VM, outs),
        scratch_shapes=list(scratch),
        compiler_params=pltpu.CompilerParams(vmem_limit_bytes=limit * 1024 * 1024),
        cost_estimate=pl.CostEstimate(flops=flops, bytes_accessed=bytes_accessed, transcendentals=0),
        name=name,
    )(*ins)


def shape(dims, dtype):
    return jax.ShapeDtypeStruct(dims, dtype)


def halves(x):
    high = x.astype(BF16).astype(F32)
    return high, x - high


def pack_weights(pos, lengths, labels, partner, wq, wk, wv, score, out, ids, wvs, sems):
    copies = [
        pltpu.make_async_copy(wq, out.at[0:ROWS, 0:HEAD], sems.at[0]),
        pltpu.make_async_copy(wk, out.at[0:ROWS, HEAD : 2 * HEAD], sems.at[1]),
        pltpu.make_async_copy(wv, wvs, sems.at[2]),
    ]
    for copy in copies:
        copy.start()
    z, xl, c, window = pos[0], pos[1], pos[2], pos[3]
    here = xl * 2 + c
    for n, (dz, dx) in enumerate(ORDER):
        ids[n] = ((z + dz + NZ) % NZ) * 4 + (xl ^ dx) * 2 + c
    group = z * 4 + here
    mate = partner[group]
    ids[WINDOW] = window
    ids[GROUP] = group
    for k in range(NZ):
        ids[WANTED + k] = (partner[((z + k) % NZ) * 4 + here] & 3) ^ here
    ids[MATE_STEP] = (z - (mate >> 2) + NZ) % NZ
    for n, x in enumerate((lengths[group], lengths[mate], labels[group], labels[mate], group, mate)):
        ids[HEADS + n] = x
    ids[CORE] = c
    for copy in copies:
        copy.wait()
    s1, rest = halves(score[...])
    s2, s3 = halves(rest)
    row = lax.broadcasted_iota(jnp.int32, (EXT, HEAD), 0)
    lhs = jnp.where(row == 0, s1, jnp.where(row == 1, s2, jnp.where(row == 2, s3, 0.0)))
    product = lax.dot_general(lhs.astype(BF16), wvs[...], LAST, preferred_element_type=F32)
    total = jnp.sum(product, axis=0, keepdims=True)
    high, low = halves(total)
    row = lax.broadcasted_iota(jnp.int32, (EXT, ROWS), 0)
    ext = jnp.where((row == 0) | (row == 2), high, jnp.where(row == 1, low, 0.0))
    out[ROWS : ROWS + EXT, :] = ext.astype(BF16)
    for h in range(2):
        start = pl.multiple_of(window * SHARE + EXT * h, EXT)
        out[ROWS + EXT : BLOCK, HEAD * h : HEAD * (h + 1)] = wvs[pl.ds(start, EXT), :]


def split_columns(hidden, out):
    size, many = 4 * BLK, 4
    i = lax.broadcasted_iota(jnp.int32, (size, size), 0)
    o = lax.broadcasted_iota(jnp.int32, (size, size), 1)
    source = BLK * ((o & 127) >> 5) + SHARE * (o >> 7) + (o & 31)
    perm = jnp.where(i == source, 1.0, 0.0).astype(BF16)
    for h in range(2):
        for first in range(0, NDP // 4, many):
            x = [
                jnp.concatenate([hidden[:, ROWS * (4 * q + k) + BLK * h :][:, :BLK] for k in range(4)], axis=1)
                for q in range(first, first + many)
            ]
            y = jnp.dot(jnp.concatenate(x, axis=0), perm, preferred_element_type=F32).astype(BF16)
            for k in range(many):
                for r in range(4):
                    out[4 * h + r, :, BLK * (first + k) : BLK * (first + k + 1)] = y[BLK * k :][:BLK, BLK * r :][:, :BLK]


def project(ids, hidden, sibling, *refs):
    blocks, (out, kept, x, w, exts, sems, out_sems) = refs[:-7], refs[-7:]
    arrivals, leaving = [], []
    for n, block in enumerate(blocks):
        columns = pl.ds(pl.multiple_of(ids[n] * ROWS, ROWS), ROWS)
        at = slice(ROWS * n, ROWS * (n + 1))
        pairs = (
            (block.at[0:ROWS], w.at[at]),
            (block.at[ROWS:BLOCK], exts.at[n]),
            (hidden.at[:, columns], x.at[0:BLK, at]),
            (sibling.at[:, columns], x.at[BLK : 2 * BLK, at]),
        )
        arrivals.append([pltpu.make_async_copy(a, b, sems.at[n, i]) for i, (a, b) in enumerate(pairs)])
        leaving.append(pltpu.make_async_copy(w.at[at], kept.at[n, 0:ROWS], out_sems.at[n, 0]))
        leaving.append(pltpu.make_async_copy(exts.at[n], kept.at[n, ROWS:BLOCK], out_sems.at[n, 1]))
    for group in arrivals:
        for copy in group:
            copy.start()
    acc = jnp.zeros((2 * BLK, 2 * HEAD), F32)
    wide = [jnp.zeros((BLK, BLK), F32)] * 2
    many = 4
    for first in range(0, len(blocks), many):
        for n in range(first, first + many):
            for copy in arrivals[n]:
                copy.wait()
            leaving[2 * n].start()
            leaving[2 * n + 1].start()
        at = slice(ROWS * first, ROWS * (first + many))
        acc += jnp.dot(x[:, at], w[at, :], preferred_element_type=F32)
        for n in range(first, first + many):
            ext = exts[n, 0:EXT, :].astype(F32)
            row = ext[0:1] + ext[1:2]
            for m in range(2):
                product = x[BLK * m : BLK * (m + 1), ROWS * n : ROWS * (n + 1)].astype(F32) * row
                wide[m] += product[:, 0:BLK] + product[:, BLK : 2 * BLK]
    zeros = jnp.zeros((8, 2 * HEAD), F32)
    for m in range(2):
        total = jnp.sum(wide[m].T, axis=0, keepdims=True)
        out[m, 0:BLK, :] = acc[BLK * m : BLK * (m + 1)]
        out[m, BLK : BLK + 8, :] = zeros + jnp.concatenate([total, total], axis=1)
    for copy in leaving:
        copy.wait()


def join_cores(mine, theirs, items):
    row = lax.broadcasted_iota(jnp.int32, (EXT, 2 * HEAD), 0)
    for n in range(2):
        full = mine[n] + theirs[1 - n]
        high, low = halves(full[BLK : BLK + 1, 0:BLK])
        items[n, 0:BLK, :] = full[0:BLK].astype(BF16)
        items[n, BLK : BLK + EXT, :] = jnp.where(row == 0, jnp.concatenate([high, low], axis=1), 0.0).astype(BF16)


def repeat_own(items, out, sems):
    copies = [pltpu.make_async_copy(items.at[0], out.at[s], sems.at[s]) for s in range(NSEQ)]
    for copy in copies:
        copy.start()
    for copy in copies:
        copy.wait()


def pick_for_planes(ids, near, side, *refs):
    outs, items = refs[:-1], refs[-1]
    items[0:2] = near[...]
    items[2:4] = side[...]
    for k, out in enumerate(outs):
        out[...] = items[ids[WANTED + k]]


def pick_partner(ids, *refs):
    received, (out, mine, sem, sems) = refs[:-4], refs[-4:]
    for k, ref in enumerate(received):

        @pl.when(ids[MATE_STEP] == k)
        def _(ref=ref):
            copy = pltpu.make_async_copy(ref, mine, sem.at[0])
            copy.start()
            copy.wait()

    copies = [pltpu.make_async_copy(mine, out.at[s], sems.at[s]) for s in range(NSEQ)]
    for copy in copies:
        copy.start()
    for copy in copies:
        copy.wait()


def collect_values(ids, kept, swapped, out, rows, sems):
    copies = [
        pltpu.make_async_copy(ref.at[:, ROWS + EXT : BLOCK, :], rows.at[n], sems.at[n])
        for n, ref in enumerate((kept, swapped))
    ]
    for copy in copies:
        copy.start()
    for flip, copy in enumerate(copies):
        copy.wait()
        for n in range(len(ORDER)):
            d = ids[n] ^ flip
            for h in range(2):
                start = pl.multiple_of(d * SHARE + EXT * h, EXT)
                out[pl.ds(start, EXT), :] = rows[flip, n, :, HEAD * h : HEAD * (h + 1)]


def attention(
    ids,
    own,
    mate,
    hidden,
    values,
    keep,
    send,
    grads,
    crows,
    exts,
    k_t,
    q_own,
    k_own,
    q_mate,
    k_mate,
    wcol,
    scores,
    dots,
    dq,
    dk,
    cacc,
    all_grads,
    columns,
    value_rows,
    shares,
    ext,
    sems,
    late_sems,
):
    copies = []
    for n, (ref, q, k) in enumerate(((mate, q_mate, k_mate), (own, q_own, k_own))):
        copies.append(pltpu.make_async_copy(ref.at[:, 0:BLK, 0:HEAD], q, sems.at[3 * n]))
        copies.append(pltpu.make_async_copy(ref.at[:, 0:BLK, HEAD : 2 * HEAD], k, sems.at[3 * n + 1]))
        copies.append(pltpu.make_async_copy(ref.at[:, BLK : BLK + EXT, :], exts.at[n], sems.at[3 * n + 2]))
    for copy in copies:
        copy.start()
    late = [
        pltpu.make_async_copy(hidden, columns, late_sems.at[0]),
        pltpu.make_async_copy(values, value_rows, late_sems.at[1]),
    ]
    for copy in late:
        copy.start()
    cacc[...] = jnp.zeros_like(cacc)
    dk[...] = jnp.zeros_like(dk)
    for copy in copies:
        copy.wait()
    scale = 1.0 / math.sqrt(HEAD)
    exponent = scale * math.log2(math.e)
    own_len, mate_len = ids[HEADS], ids[HEADS + 1]
    for i in range(NSEQ):
        at = slice(BLK * i, BLK * (i + 1))
        k_t[:, at] = k_mate[i].astype(F32).T.astype(BF16)
        for n in range(2):
            extra = exts[n, i].astype(F32)
            row = extra[0:1, 0:BLK] + extra[0:1, BLK : 2 * BLK]
            wcol[n, at, :] = jnp.broadcast_to(row, (BLK, BLK)).T

    def softmax(side, queries, keys, start, key_len):
        q = queries[pl.ds(start // BLK, TB // BLK)].reshape(TB, HEAD)
        top = jnp.full((8, TB), -jnp.inf, F32)
        for u in range(NSEQ):
            at = slice(BLK * u, BLK * (u + 1))
            s = lax.dot_general(keys[u], q, LAST, preferred_element_type=F32)
            s = s * exponent + jnp.where(u < key_len, 0.0, -1e30).astype(F32)
            scores[side, at, :] = s
            top = jnp.maximum(top, jnp.max(s.reshape(BLK // 8, 8, TB), axis=0))
        top = jnp.max(top, axis=0, keepdims=True)
        total = jnp.zeros((8, TB), F32)
        weighed = jnp.zeros((8, TB), F32)
        for u in range(2 * NSEQ):
            at = slice(64 * u, 64 * (u + 1))
            e = jnp.exp2(scores[side, at, :] - top)
            scores[side, at, :] = e
            w = wcol[side, at, :]
            total += jnp.sum(e.reshape(8, 8, TB), axis=0)
            weighed += jnp.sum((e * jnp.concatenate([w, w], axis=1)).reshape(8, 8, TB), axis=0)
        total = jnp.sum(total, axis=0, keepdims=True)
        inverse = 1.0 / total
        s_row = jnp.sum(weighed, axis=0, keepdims=True) * inverse
        return inverse, s_row

    def live_row(start, length):
        t = lax.broadcasted_iota(jnp.int32, (1, TB), 1) + start
        return jnp.where(t < BLK * length, 1.0, 0.0).astype(F32)

    def first(n, z):
        side = 0
        start = pl.multiple_of(n * TB, TB)
        inverse, s_row = softmax(0, q_own, k_mate, start, mate_len)
        live = live_row(start, own_len)
        for u in range(2 * NSEQ):
            at = slice(64 * u, 64 * (u + 1))
            w = wcol[0, at, :]
            dots[side, at, :] = (scores[side, at, :] * (jnp.concatenate([w, w], axis=1) - s_row)).astype(BF16)
        g = jnp.dot(k_t[...], dots[side], preferred_element_type=F32)
        dq[:, pl.ds(start, TB)] = g * (inverse * live)
        return z + s_row * live

    def second(n, z):
        side = 1
        start = pl.multiple_of(n * TB, TB)
        inverse, s_row = softmax(1, q_mate, k_own, start, own_len)
        live = live_row(start, mate_len)
        r = inverse * live
        for u in range(2 * NSEQ):
            at = slice(64 * u, 64 * (u + 1))
            w = wcol[1, at, :]
            f = scores[side, at, :] * r
            cacc[at, :] += f[:, 0:BLK] + f[:, BLK:TB]
            dots[side, at, :] = (f * (jnp.concatenate([w, w], axis=1) - s_row)).astype(BF16)
        q = q_mate[pl.ds(start // BLK, TB // BLK)].reshape(TB, HEAD)
        dk[...] += jnp.dot(dots[side], q, preferred_element_type=F32)
        return z + s_row * live

    zero = jnp.zeros((1, TB), F32)

    def both(n, z):
        return first(n, z[0]), second(n, z[1])

    z_own, z_mate = lax.fori_loop(0, SEQLEN // TB, both, (zero, zero))

    def head(z_row, length, label, index):
        count = jnp.full((1, 1), BLK * length, jnp.int32).astype(F32)
        sign = jnp.full((1, 1), 2 * label - 1, jnp.int32).astype(F32)
        factor = 32.0 * (1.0 + 2.0 * jnp.full((1, 1), index, jnp.int32).astype(F32) / (NDP - 1))
        root = jnp.sqrt(count)
        x = -sign * (jnp.sum(z_row, axis=1, keepdims=True) / root)
        e = jnp.exp(-jnp.abs(x))
        term = factor * (jnp.maximum(x, 0.0) + jnp.log1p(e))
        sigmoid = jnp.where(x >= 0, 1.0, e) / (1.0 + e)
        return term, -factor * sign * sigmoid / root

    term, ds_own = head(z_own, own_len, ids[HEADS + 2], ids[HEADS + 4])
    _, ds_mate = head(z_mate, mate_len, ids[HEADS + 3], ids[HEADS + 5])
    row = lax.broadcasted_iota(jnp.int32, (EXT, BLK), 0)
    for i in range(NSEQ):
        at = slice(BLK * i, BLK * (i + 1))
        all_grads[0:HEAD, at] = (dq[:, at] * (ds_own * scale)).astype(BF16)
        all_grads[HEAD : 2 * HEAD, at] = (dk[at, :] * (ds_mate * scale)).T.astype(BF16)
        c_row = jnp.sum(cacc[at, :].T, axis=0, keepdims=True) * ds_mate
        high, low = halves(c_row)
        c_rows = jnp.where(row < 2, high, jnp.where(row == 2, low, 0.0)).astype(BF16)
        all_grads[2 * HEAD : 2 * HEAD + EXT, at] = c_rows

        @pl.when(ids[WINDOW] == i)
        def _(at=at, c_rows=c_rows):
            grads[...] = all_grads[0 : 2 * HEAD, at].astype(F32).T.astype(BF16)
            crows[...] = c_rows

    for copy in late:
        copy.wait()
    chunk = 256
    wide = []
    for n in range(COLS // chunk):
        x = columns[:, :, chunk * n : chunk * (n + 1)].reshape(SEQLEN, chunk)
        y = jnp.dot(all_grads[...], x, preferred_element_type=F32)
        rows = y[0 : 2 * HEAD].T
        for k in range(chunk // SHARE):
            d = n * (chunk // SHARE) + k
            shares[(d & 1) ^ ids[CORE], d >> 1] = rows[SHARE * k : SHARE * (k + 1)]
        wide.append(y[2 * HEAD : 2 * HEAD + 1] + y[2 * HEAD + 2 : 2 * HEAD + 3])
    row = lax.broadcasted_iota(jnp.int32, (EXT, chunk), 0)
    gs = jnp.zeros((EXT, HEAD), F32)
    ext[...] = jnp.zeros_like(ext)
    for n, u in enumerate(wide):
        high, low = halves(u)
        ext[n : n + 1, :] = high
        ext[4 + n : 5 + n, :] = low
        lhs = jnp.where(row == 0, high, jnp.where(row == 1, low, 0.0)).astype(BF16)
        gs += jnp.dot(lhs, value_rows[chunk * n : chunk * (n + 1), :], preferred_element_type=F32)
    high, low = halves(gs[0:1] + gs[1:2])
    ext[8:9, 0:HEAD] = high
    ext[8:9, HEAD : 2 * HEAD] = low
    high, low = halves(jnp.broadcast_to(term, (1, HEAD)))
    ext[9:10, 0:HEAD] = high
    ext[9:10, HEAD : 2 * HEAD] = low
    tail = ext[...]
    for m in range(NDP // 2):
        keep[m, 0:SHARE, :] = shares[0, m]
        keep[m, SHARE : SHARE + EXT, :] = tail
        send[m, 0:SHARE, :] = shares[1, m].astype(BF16)
        send[m, SHARE : SHARE + EXT, :] = tail.astype(BF16)


def add_core(keep, received, out, ext):
    split_again(keep[0, SHARE : SHARE + EXT, :] + received[0, SHARE : SHARE + EXT, :].astype(F32), ext)
    tail = ext[...].astype(BF16)
    for m in range(NDP // 2):
        out[m, 0:SHARE, :] = (keep[m, 0:SHARE, :] + received[m, 0:SHARE, :].astype(F32)).astype(BF16)
        out[m, SHARE : SHARE + EXT, :] = tail


def split_again(tail, ext):
    ext[...] = jnp.zeros_like(ext)
    high, low = halves(tail[0:4] + tail[4:8])
    ext[0:4, :] = high
    ext[4:8, :] = low
    for n in (8, 9):
        high, low = halves(tail[n : n + 1, 0:HEAD] + tail[n : n + 1, HEAD : 2 * HEAD])
        ext[n : n + 1, 0:HEAD] = high
        ext[n : n + 1, HEAD : 2 * HEAD] = low


def sum_shares(received, out, ext):
    acc = received[0].astype(F32)
    for n in range(1, NDP // 2):
        acc += received[n].astype(F32)
    split_again(acc[SHARE : SHARE + EXT], ext)
    rows = acc[0:SHARE].astype(BF16)
    tail = ext[...].astype(BF16)
    for s in range(NSEQ):
        out[s, 0:SHARE, :] = rows
        out[s, SHARE : SHARE + EXT, :] = tail


def unpack(ids, received, score, gq, gk, gv, gs, loss):
    d = ids[GROUP]
    sub = lax.broadcasted_iota(jnp.int32, (4, 2 * HEAD), 0)
    lane = lax.broadcasted_iota(jnp.int32, (SHARE, 2 * HEAD), 1)
    j = lax.broadcasted_iota(jnp.int32, (SHARE, 2 * HEAD), 0)
    hit = lane == SHARE * (d % 8) + j
    readout = jnp.zeros((1, HEAD), F32)
    for s in range(NSEQ):
        at = slice(SHARE * s, SHARE * (s + 1))
        block = received[s].astype(F32)
        gq[at, :] = block[0:SHARE, 0:HEAD]
        gk[at, :] = block[0:SHARE, HEAD : 2 * HEAD]
        tail = block[SHARE : SHARE + EXT]
        u = tail[0:4] + tail[4:8]
        u = jnp.sum(jnp.where(sub == d // 8, u, 0.0), axis=0, keepdims=True)
        column = jnp.sum(jnp.where(hit, u, 0.0), axis=1, keepdims=True)
        gv[at, :] = column * score[...]
        readout += tail[8:9, 0:HEAD] + tail[8:9, HEAD : 2 * HEAD]
        if s == 0:
            loss[...] = tail[9:10, 0:HEAD] + tail[9:10, HEAD : 2 * HEAD]
    gs[...] = readout


def hidden_grads(ids, grads, crows, kept, swapped, out):
    g = grads[...]
    c = crows[...].astype(F32).T.astype(BF16)
    for flip, ref in enumerate((kept, swapped)):
        for n in range(len(ORDER)):
            start = pl.multiple_of((ids[n] ^ flip) * ROWS, ROWS)
            y = lax.dot_general(g, ref[n, 0:ROWS, :], LAST, preferred_element_type=F32)
            y += jnp.dot(c, ref[n, ROWS : ROWS + EXT, :], preferred_element_type=F32)
            out[:, pl.ds(start, ROWS)] = y.astype(BF16)


SWAP = [(0, 1), (1, 0)]
UP = [(i, (i + 1) % NZ) for i in range(NZ)]
DOWN = [(i, (i - 1) % NZ) for i in range(NZ)]
ORDER = [(0, 0), (0, 1)]
for _step in range(1, NZ // 2 + 1):
    for _x in (0, 1):
        if _step < NZ // 2 or _x == 0:
            ORDER.append((-_step, _x))
        if _step < NZ // 2 or _x == 1:
            ORDER.append((_step, _x))


def gather_weights(block, other, up, down):
    found = {(0, 0): block, (0, 1): other, (-1, 0): up, (1, 0): down}
    for dz, dx in ORDER[2:]:
        if (dz, dx) in found:
            continue
        if dz < 0:
            found[(dz, dx)] = lax.ppermute(found[(dz + 1, dx)], "z", UP)
        else:
            found[(dz, dx)] = lax.ppermute(found[(dz - 1, dx)], "z", DOWN)
    return [found[key] for key in ORDER]


def per_device(hidden, w_query, w_key, w_value, score_vec, labels, lengths, partner):
    tokens = hidden.reshape(BLK, NDP * ROWS)
    score = score_vec.reshape(1, HEAD)
    z, xl, c = (lax.axis_index(a) for a in DP)
    window = lax.axis_index("y") * 2 + lax.axis_index("xh")
    pos = jnp.stack([z, xl, c, window]).astype(jnp.int32)
    item = (BLK + EXT, 2 * HEAD)

    block, ids = call(
        pack_weights,
        (shape((BLOCK, ROWS), BF16), shape((64,), jnp.int32)),
        (pos, lengths, labels, partner, w_query, w_key, w_value, score),
        far=(4, 5, 6),
        scratch=[pltpu.VMEM((ROWS, HEAD), BF16), pltpu.SemaphoreType.DMA((3,))],
        name="pack_weights",
        limit=62,
    )
    other = lax.ppermute(block, "xl", SWAP)
    sibling = lax.ppermute(tokens, "c", SWAP)
    up = lax.ppermute(block, "z", UP)
    down = lax.ppermute(block, "z", DOWN)
    later, _ = lax.optimization_barrier((tokens, block))
    split = call(split_columns, shape((NSEQ, BLK, COLS), BF16), (later,), name="split_columns", flops=1 << 30)
    other, split = lax.optimization_barrier((other, split))
    hidden_t = lax.all_to_all(split, SEQ, 0, 0, tiled=True)
    blocks = gather_weights(block, other, up, down)

    partial, kept = call(
        project,
        (shape((2, BLK + 8, 2 * HEAD), F32), shape((len(ORDER), BLOCK, ROWS), BF16)),
        (ids, tokens, sibling, *blocks),
        far=range(1, 3 + len(ORDER)),
        far_out=((len(ORDER), BLOCK, ROWS),),
        scratch=[
            pltpu.VMEM((2 * BLK, len(ORDER) * ROWS), BF16),
            pltpu.VMEM((len(ORDER) * ROWS, ROWS), BF16),
            pltpu.VMEM((len(ORDER), 2 * EXT, ROWS), BF16),
            pltpu.SemaphoreType.DMA((len(ORDER), 4)),
            pltpu.SemaphoreType.DMA((len(ORDER), 2)),
        ],
        name="project",
        limit=62,
        flops=1 << 29,
        bytes_accessed=6 << 20,
    )
    theirs = lax.ppermute(partial, "c", SWAP)
    theirs, hidden_t = lax.optimization_barrier((theirs, hidden_t))
    items = call(join_cores, shape((2, *item), BF16), (partial, theirs), name="join_cores")
    side = lax.ppermute(items, "xl", SWAP)
    repeated = call(
        repeat_own,
        shape((NSEQ, *item), BF16),
        (items,),
        far_out=((NSEQ, *item),),
        scratch=[pltpu.SemaphoreType.DMA((NSEQ,))],
        name="repeat_own",
    )
    side, repeated = lax.optimization_barrier((side, repeated))
    own = lax.all_to_all(repeated, SEQ, 0, 0, tiled=True)
    slots = call(
        pick_for_planes,
        tuple(shape(item, BF16) for _ in range(NZ)),
        (ids, items, side),
        scratch=[pltpu.VMEM((4, *item), BF16)],
        name="pick_for_planes",
    )
    arrived = {0: slots[0]}
    for k in (4, 3, 5, 2, 6, 1, 7):
        arrived[k] = lax.ppermute(slots[k], "z", [(i, (i + k) % NZ) for i in range(NZ)])
    kept, _ = lax.optimization_barrier((kept, slots[0]))
    swapped = lax.ppermute(kept, "c", SWAP)
    values = call(
        collect_values,
        shape((COLS, HEAD), BF16),
        (ids, kept, swapped),
        far=(1, 2),
        scratch=[pltpu.VMEM((2, len(ORDER), EXT, ROWS), BF16), pltpu.SemaphoreType.DMA((2,))],
        name="collect_values",
        limit=62,
    )
    theirs = call(
        pick_partner,
        shape((NSEQ, *item), BF16),
        (ids, *[arrived[k] for k in range(NZ)]),
        far=range(1, 1 + NZ),
        far_out=((NSEQ, *item),),
        scratch=[pltpu.VMEM(item, BF16), pltpu.SemaphoreType.DMA((1,)), pltpu.SemaphoreType.DMA((NSEQ,))],
        name="pick_partner",
        limit=62,
    )
    theirs, values = lax.optimization_barrier((theirs, values))
    mate = lax.all_to_all(theirs, SEQ, 0, 0, tiled=True)

    message = (NDP // 2, SHARE + EXT, 2 * HEAD)
    ext = pltpu.VMEM((EXT, 2 * HEAD), F32)
    keep, send, grads, crows = call(
        attention,
        (shape(message, F32), shape(message, BF16), shape((BLK, 2 * HEAD), BF16), shape((EXT, BLK), BF16)),
        (ids, own, mate, hidden_t, values),
        far=(1, 2, 3, 4),
        scratch=[
            pltpu.VMEM((2, NSEQ, EXT, 2 * HEAD), BF16),
            pltpu.VMEM((HEAD, SEQLEN), BF16),
            *[pltpu.VMEM((NSEQ, BLK, HEAD), BF16)] * 4,
            pltpu.VMEM((2, SEQLEN, BLK), F32),
            pltpu.VMEM((2, SEQLEN, TB), F32),
            pltpu.VMEM((2, SEQLEN, TB), BF16),
            pltpu.VMEM((HEAD, SEQLEN), F32),
            pltpu.VMEM((SEQLEN, HEAD), F32),
            pltpu.VMEM((SEQLEN, BLK), F32),
            pltpu.VMEM((2 * HEAD + EXT, SEQLEN), BF16),
            pltpu.VMEM((NSEQ, BLK, COLS), BF16),
            pltpu.VMEM((COLS, HEAD), BF16),
            pltpu.VMEM((2, NDP // 2, SHARE, 2 * HEAD), F32),
            ext,
            pltpu.SemaphoreType.DMA((6,)),
            pltpu.SemaphoreType.DMA((2,)),
        ],
        name="attention",
        limit=62,
        flops=1 << 31,
    )
    shares = call(add_core, shape(message, BF16), (keep, lax.ppermute(send, "c", SWAP)), scratch=[ext], name="add_core")
    arrived = lax.all_to_all(shares, ("z", "xl"), 0, 0, tiled=True)
    grad_hidden = call(
        hidden_grads,
        shape((BLK, NDP * ROWS), BF16),
        (ids, grads, crows, kept, swapped),
        name="hidden_grads",
        flops=1 << 29,
        bytes_accessed=6 << 20,
    )
    arrived, grad_hidden = lax.optimization_barrier((arrived, grad_hidden))
    sums = call(
        sum_shares,
        shape((NSEQ, SHARE + EXT, 2 * HEAD), BF16),
        (arrived,),
        scratch=[ext],
        name="sum_shares",
    )
    arrived = lax.all_to_all(sums, SEQ, 0, 0, tiled=True)
    grad_query, grad_key, grad_value, grad_score, loss = call(
        unpack,
        (
            shape((ROWS, HEAD), F32),
            shape((ROWS, HEAD), F32),
            shape((ROWS, HEAD), F32),
            shape((1, HEAD), F32),
            shape((1, HEAD), F32),
        ),
        (ids, arrived, score),
        name="unpack",
    )
    return (
        loss[0, 0],
        grad_query,
        grad_key,
        grad_value,
        grad_score.reshape(HEAD),
        grad_hidden.reshape(1, BLK, NDP * ROWS),
    )


def solution(mesh):
    parts = Mesh(mesh.devices.reshape(NZ, NX, NC, 4, 2), DP + SEQ)
    return jax.shard_map(
        per_device,
        mesh=parts,
        in_specs=(P(DP, SEQ, None), P(DP, None), P(DP, None), P(DP, None), P(), P(), P(), P()),
        out_specs=(P(), P(DP, None), P(DP, None), P(DP, None), P(), P(DP, SEQ, None)),
        check_vma=False,
    )
```

time: 232 us -> 170 us (0.73)
  blocking collectives: 92.1 us -> 30.3 us
  local copies, waits for them, and re-layouts: 26.4 us -> 6.56 us
  Pallas kernels: 26.2 us -> 36.8 us
  starting transfers between devices: 47 us -> 57.3 us
  waiting for transfers between devices: 32.8 us -> 37.1 us
  between operations: 5.21 us -> 1.03 us
    all_gather x1 -> x0, blocking collectives: 40.1 us -> none  [per_device(): value_rows = lax.all_gather(own_rows, DP, axis=0, tiled=True)]
    all_to_all x2, blocking collectives: 52.1 us -> 30.3 us  [the longest x1 19.5 us: per_device(): mate = lax.all_to_all(theirs, SEQ, 0, 0, tiled=True)]
    ppermute x34 -> x27, starting transfers between devices: 27.2 us -> 40.3 us  [the longest x6 16.5 us: gather_weights(): found[dz, dx] = lax.ppermute(found[dz - 1, dx], 'z', DOWN)]
    unnamed x122 -> x70, local copies, waits for them, and re-layouts: 19.5 us -> 6.56 us
    pallas_call x10 -> x13, Pallas kernels: 26.2 us -> 36.8 us  [call(): pl.pallas_call(kernel, out_shape=outs, in_specs=[SM if a.dtype == jnp.int...]
    ppermute x34 -> x27, waiting for transfers between devices: 21.3 us -> 28.6 us  [the longest x7 9.4 us: per_device(): lax.ppermute(slots[k], 'z', [(i, (i + k) % NZ) for i in range(NZ)])]
    all_to_all x3 -> x2, starting transfers between devices: 16.2 us -> 11.5 us  [the longest x1 6.72 us: per_device(): own = lax.all_to_all(repeated, SEQ, 0, 0, tiled=True)]
    another operation x2 -> x0, local copies, waits for them, and re-layouts: 3.43 us -> none  [the longest x1 3.32 us: per_device(): jnp.stack([lengths[group], lengths[mate], labels[group], labels[mate], gr...]
  transfers between devices with their start and end apart: 38 -> 30, of which waited for: 15 -> 18; matrix products, arithmetic and copies ran while one was open for 3% -> 0% of each run, Pallas kernels for 8% -> 13%
where the time goes in v2:
time: 170 us
  starting transfers between devices  57.3 us (34%)
  waiting for transfers between devices  37.1 us (22%)
  Pallas kernels  36.8 us (22%)
  blocking collectives  30.3 us (18%)
  local copies, waits for them, and re-layouts  6.56 us (4%)
    pallas_call x13, Pallas kernels, call(): pl.pallas_call(kernel, out_shape=outs, in_specs=[SM if a.dtype == jnp.int...  36.8 us
    all_to_all x1, blocking collectives, per_device(): mate = lax.all_to_all(theirs, SEQ, 0, 0, tiled=True)  19.5 us
    ppermute x6, starting transfers between devices, gather_weights(): found[dz, dx] = lax.ppermute(found[dz - 1, dx], 'z', DOWN)  16.5 us
    ppermute x7, starting transfers between devices, per_device(): lax.ppermute(slots[k], 'z', [(i, (i + k) % NZ) for i in range(NZ)])  14.8 us
    all_to_all x1, blocking collectives, per_device(): arrived = lax.all_to_all(sums, SEQ, 0, 0, tiled=True)  10.9 us
    ppermute x7, waiting for transfers between devices, per_device(): lax.ppermute(slots[k], 'z', [(i, (i + k) % NZ) for i in range(NZ)])  9.4 us
    ppermute x6, waiting for transfers between devices, gather_weights(): found[dz, dx] = lax.ppermute(found[dz + 1, dx], 'z', UP)  9.27 us
    all_to_all x1, waiting for transfers between devices, per_device(): arrived = lax.all_to_all(shares, ('z', 'xl'), 0, 0, tiled=True)  8.44 us
  transfers between devices with their start and end apart: 30, of which 18 were waited for; matrix products, arithmetic and copies ran while one was open for 0% of the time, Pallas kernels for 13%

profile of v2, /device:TPU:2, one launch (start us, length us, event | category | flops | bytes accessed | tf_op | source)
XLA Modules:
  0.0 169.7 jit_solution(9727917978362134687)
XLA Ops:
  0.6 0.1 collective-permute-start
  0.7 0.6 pad_add_fusion.pos
  1.3 2.4 %pack_weights.1 = (bf16[288,256]{1,0:T(8,128)(2,1)}, s32[64]{0:T(128)}) custom-call(s32[4]{0:T(128)} %pad_add_fusion.pos, s32[32]{0:T(128)} %lengths.1, s32[32]{0:T(128)} %labels.1, s32[32]{0:T(128)} %partner.1, bf16[256,128]{1,0:T(8,128)(2,1)} %wq.1, bf16[256,128]{1,0:T(8,128)(2,1)} %wk.1, bf16[256,128]{1,0:T(8,128)(2,1)} %wv.1, f32[1,128]{1,0:T(1,128)} %bitcast.13), custom_call_target="tpu_custom_call" | custom-call | tf_op jit(solution)/shard_map/pack_weights/pallas_call | solution.py:36
  3.8 2.4 %collective-permute-start.1 = (bf16[288,256]{1,0:T(8,128)(2,1)}, bf16[288,256]{1,0:T(8,128)(2,1)S(1)}, u32[]{:S(2)}, u32[]{:S(2)}) collective-permute-start(bf16[288,256]{1,0:T(8,128)(2,1)} %get-tuple-element.40.refs_0_), channel_id=1, source_target_pairs={{0,16},{16,0},{1,17},{17,1},{2,18},{18,2},{3,19},{19,3},{4,20},{20... | collective-permute-start | bytes 442376 | tf_op jit(solution)/shard_map/ppermute | solution.py:507
  6.1 1.6 copy-done.1
  7.7 2.7 %split_columns.1 = bf16[8,128,1024]{2,1,0:T(8,128)(2,1)} custom-call(bf16[128,8192]{1,0:T(8,128)(2,1)S(1)} %bitcast.12), custom_call_target="tpu_custom_call" | custom-call | flops 1073741824 | tf_op jit(solution)/shard_map/split_columns/pallas_call | solution.py:36
  10.4 0.4 collective-permute-done.1.refs_1_
  10.8 5.5 %all-to-all-start = ((bf16[8,128,1024]{2,1,0:T(8,128)(2,1)}), bf16[8,128,1024]{2,1,0:T(8,128)(2,1)}, u32[]{:S(2)}, u32[]{:S(2)}) async-start(bf16[8,128,1024]{2,1,0:T(8,128)(2,1)} %split_columns.1), calls=%async_computation | async-start | bytes 4194304 | tf_op jit(solution)/shard_map/all_to_all | solution.py:514
  16.4 2.0 %collective-permute-start.2 = (bf16[288,256]{1,0:T(8,128)(2,1)S(1)}, bf16[288,256]{1,0:T(8,128)(2,1)S(1)}, u32[]{:S(2)}, u32[]{:S(2)}) collective-permute-start(bf16[288,256]{1,0:T(8,128)(2,1)S(1)} %copy-done.12), channel_id=1, source_target_pairs={{0,32},{32,64},{64,96},{96,128},{128,160},{160,192},{192,224},{224... | collective-permute-start | bytes 442376 | tf_op jit(solution)/shard_map/ppermute | solution.py:509
  18.3 4.0 %collective-permute-start.5 = (bf16[288,256]{1,0:T(8,128)(2,1)S(1)}, bf16[288,256]{1,0:T(8,128)(2,1)S(1)}, u32[]{:S(2)}, u32[]{:S(2)}) collective-permute-start(bf16[288,256]{1,0:T(8,128)(2,1)S(1)} %collective-permute-done.1.refs_1_), channel_id=1, source_target_pairs={{0,224},{32,0},{64,32},{96,64},{128,96},{160,128},{192,160},{224,1... | collective-permute-start | bytes 442376 | tf_op jit(solution)/shard_map/ppermute | solution.py:486
  22.4 1.9 %collective-permute-start.3 = (bf16[288,256]{1,0:T(8,128)(2,1)S(1)}, bf16[288,256]{1,0:T(8,128)(2,1)S(1)}, u32[]{:S(2)}, u32[]{:S(2)}) collective-permute-start(bf16[288,256]{1,0:T(8,128)(2,1)S(1)} %copy-done.12), channel_id=1, source_target_pairs={{0,224},{32,0},{64,32},{96,64},{128,96},{160,128},{192,160},{224,1... | collective-permute-start | bytes 442376 | tf_op jit(solution)/shard_map/ppermute | solution.py:510
  24.3 1.4 collective-permute-done.2.refs_2_
  25.7 0.1 collective-permute-start.4
  25.8 0.9 collective-permute-done.5.refs_5_
  26.7 3.7 %collective-permute-start.9 = (bf16[288,256]{1,0:T(8,128)(2,1)S(1)}, bf16[288,256]{1,0:T(8,128)(2,1)S(1)}, u32[]{:S(2)}, u32[]{:S(2)}) collective-permute-start(bf16[288,256]{1,0:T(8,128)(2,1)S(1)} %collective-permute-done.5.refs_5_), channel_id=1, source_target_pairs={{0,224},{32,0},{64,32},{96,64},{128,96},{160,128},{192,160},{224,1... | collective-permute-start | bytes 442376 | tf_op jit(solution)/shard_map/ppermute | solution.py:486
  30.3 1.9 %collective-permute-start.7 = (bf16[288,256]{1,0:T(8,128)(2,1)S(1)}, bf16[288,256]{1,0:T(8,128)(2,1)S(1)}, u32[]{:S(2)}, u32[]{:S(2)}) collective-permute-start(bf16[288,256]{1,0:T(8,128)(2,1)S(1)} %collective-permute-done.3.refs_3_), channel_id=1, source_target_pairs={{0,224},{32,0},{64,32},{96,64},{128,96},{160,128},{192,160},{224,1... | collective-permute-start | bytes 442376 | tf_op jit(solution)/shard_map/ppermute | solution.py:486
  32.3 0.9 collective-permute-done.6.refs_6_
  33.2 2.2 %collective-permute-done.4.refs_4_ = bf16[288,256]{1,0:T(8,128)(2,1)S(1)} collective-permute-done((bf16[288,256]{1,0:T(8,128)(2,1)S(1)}, bf16[288,256]{1,0:T(8,128)(2,1)S(1)}, u32[]{:S(2)}, u32[]{:S(2)}) %collective-permute-start.4) | collective-permute-done | bytes 147488 | tf_op jit(solution)/shard_map/ppermute | solution.py:484
  35.4 3.2 %collective-permute-start.13 = (bf16[288,256]{1,0:T(8,128)(2,1)S(1)}, bf16[288,256]{1,0:T(8,128)(2,1)S(1)}, u32[]{:S(2)}, u32[]{:S(2)}) collective-permute-start(bf16[288,256]{1,0:T(8,128)(2,1)S(1)} %collective-permute-done.9.refs_9_), channel_id=1, source_target_pairs={{0,224},{32,0},{64,32},{96,64},{128,96},{160,128},{192,160},{224,1... | collective-permute-start | bytes 442376 | tf_op jit(solution)/shard_map/ppermute | solution.py:486
  38.6 0.4 collective-permute-start.11
  39.1 0.7 collective-permute-done.10.refs_10_
  39.8 0.9 collective-permute-start.14
  40.7 2.3 %collective-permute-done.8.refs_8_ = bf16[288,256]{1,0:T(8,128)(2,1)S(1)} collective-permute-done((bf16[288,256]{1,0:T(8,128)(2,1)S(1)}, bf16[288,256]{1,0:T(8,128)(2,1)S(1)}, u32[]{:S(2)}, u32[]{:S(2)}) %collective-permute-start.8) | collective-permute-done | bytes 147488 | tf_op jit(solution)/shard_map/ppermute | solution.py:484
  43.0 3.2 %collective-permute-start.15 = (bf16[288,256]{1,0:T(8,128)(2,1)S(1)}, bf16[288,256]{1,0:T(8,128)(2,1)S(1)}, u32[]{:S(2)}, u32[]{:S(2)}) collective-permute-start(bf16[288,256]{1,0:T(8,128)(2,1)S(1)} %collective-permute-done.13.refs_13_), channel_id=1, source_target_pairs={{0,224},{32,0},{64,32},{96,64},{128,96},{160,128},{192,160},{224,1... | collective-permute-start | bytes 442376 | tf_op jit(solution)/shard_map/ppermute | solution.py:486
  46.2 0.2 collective-permute-done.14.refs_14_
  46.5 2.9 %collective-permute-done.12.refs_12_ = bf16[288,256]{1,0:T(8,128)(2,1)S(1)} collective-permute-done((bf16[288,256]{1,0:T(8,128)(2,1)S(1)}, bf16[288,256]{1,0:T(8,128)(2,1)S(1)}, u32[]{:S(2)}, u32[]{:S(2)}) %collective-permute-start.12) | collective-permute-done | bytes 147488 | tf_op jit(solution)/shard_map/ppermute | solution.py:484
  49.4 0.7 copy-done.27
  50.2 0.0 copy-start.6
  50.2 5.8 %project.1 = (f32[2,136,256]{2,1,0:T(8,128)}, bf16[16,288,256]{2,1,0:T(8,128)(2,1)}) custom-call(s32[64]{0:T(128)} %get-tuple-element.39.ids, bf16[128,8192]{1,0:T(8,128)(2,1)} %bitcast.11, bf16[128,8192]{1,0:T(8,128)(2,1)} %collective-permute-done.sibling, bf16[288,256]{1,0:T(8,128)(2,1)} %get-tuple-element.40.refs_0_, bf16[288,256]{1,0:T(8,128)(2,1)} %copy-done.13, ...), custom_call_target="tpu_custom_call" | custom-call | flops 536870912 | bytes 6291456 | tf_op jit(solution)/shard_map/project/pallas_call | solution.py:36
  56.0 0.1 collective-permute-start.16
  56.1 1.7 %collective-permute-done.16.theirs = f32[2,136,256]{2,1,0:T(8,128)S(1)} collective-permute-done((f32[2,136,256]{2,1,0:T(8,128)}, f32[2,136,256]{2,1,0:T(8,128)S(1)}, u32[]{:S(2)}, u32[]{:S(2)}) %collective-permute-start.16) | collective-permute-done | bytes 278560 | tf_op jit(solution)/shard_map/ppermute | solution.py:535
  57.9 1.0 copy-done.3
  58.9 1.5 collective-permute-start.17
  60.4 0.9 repeat_own.1
  61.3 3.6 %collective-permute-done.17.side = bf16[2,144,256]{2,1,0:T(8,128)(2,1)S(1)} collective-permute-done((bf16[2,144,256]{2,1,0:T(8,128)(2,1)S(1)}, bf16[2,144,256]{2,1,0:T(8,128)(2,1)S(1)}, u32[]{:S(2)}, u32[]{:S(2)}) %collective-permute-start.17) | collective-permute-done | bytes 147488 | tf_op jit(solution)/shard_map/ppermute | solution.py:538
  64.8 0.6 pick_for_planes.1
  65.5 0.6 copy-done.4
  66.1 6.7 %all-to-all-start.1 = ((bf16[8,144,256]{2,1,0:T(8,128)(2,1)}), bf16[8,144,256]{2,1,0:T(8,128)(2,1)S(1)}, u32[]{:S(2)}, u32[]{:S(2)}) async-start(bf16[8,144,256]{2,1,0:T(8,128)(2,1)} %repeat_own.1), calls=%async_computation.1 | async-start | bytes 1179648 | tf_op jit(solution)/shard_map/all_to_all | solution.py:548
  72.8 5.4 %collective-permute-start.19 = (bf16[144,256]{1,0:T(8,128)(2,1)S(1)}, bf16[144,256]{1,0:T(8,128)(2,1)S(1)}, u32[]{:S(2)}, u32[]{:S(2)}) collective-permute-start(bf16[144,256]{1,0:T(8,128)(2,1)S(1)} %get-tuple-element.50), channel_id=1, source_target_pairs={{0,64},{32,96},{64,128},{96,160},{128,192},{160,224},{192,0},{224,... | collective-permute-start | bytes 221192 | tf_op jit(solution)/shard_map/ppermute | solution.py:558
  78.2 3.3 %collective-permute-start.21 = (bf16[144,256]{1,0:T(8,128)(2,1)S(1)}, bf16[144,256]{1,0:T(8,128)(2,1)S(1)}, u32[]{:S(2)}, u32[]{:S(2)}) collective-permute-start(bf16[144,256]{1,0:T(8,128)(2,1)S(1)} %get-tuple-element.52), channel_id=1, source_target_pairs={{0,128},{32,160},{64,192},{96,224},{128,0},{160,32},{192,64},{224,... | collective-permute-start | bytes 221192 | tf_op jit(solution)/shard_map/ppermute | solution.py:558
  81.5 3.4 %collective-permute-start.22 = (bf16[144,256]{1,0:T(8,128)(2,1)S(1)}, bf16[144,256]{1,0:T(8,128)(2,1)S(1)}, u32[]{:S(2)}, u32[]{:S(2)}) collective-permute-start(bf16[144,256]{1,0:T(8,128)(2,1)S(1)} %get-tuple-element.53), channel_id=1, source_target_pairs={{0,160},{32,192},{64,224},{96,0},{128,32},{160,64},{192,96},{224,1... | collective-permute-start | bytes 221192 | tf_op jit(solution)/shard_map/ppermute | solution.py:558
  84.9 0.1 collective-permute-done.19.refs_2_
  84.9 2.7 %collective-permute-start.23 = (bf16[144,256]{1,0:T(8,128)(2,1)S(1)}, bf16[144,256]{1,0:T(8,128)(2,1)S(1)}, u32[]{:S(2)}, u32[]{:S(2)}) collective-permute-start(bf16[144,256]{1,0:T(8,128)(2,1)S(1)} %get-tuple-element.54), channel_id=1, source_target_pairs={{0,192},{32,224},{64,0},{96,32},{128,64},{160,96},{192,128},{224,1... | collective-permute-start | bytes 221192 | tf_op jit(solution)/shard_map/ppermute | solution.py:558
  87.6 1.8 %collective-permute-done.20.refs_3_ = bf16[144,256]{1,0:T(8,128)(2,1)S(1)} collective-permute-done((bf16[144,256]{1,0:T(8,128)(2,1)S(1)}, bf16[144,256]{1,0:T(8,128)(2,1)S(1)}, u32[]{:S(2)}, u32[]{:S(2)}) %collective-permute-start.20) | collective-permute-done | bytes 73760 | tf_op jit(solution)/shard_map/ppermute | solution.py:558
  89.5 3.0 %collective-permute-done.22.refs_5_ = bf16[144,256]{1,0:T(8,128)(2,1)S(1)} collective-permute-done((bf16[144,256]{1,0:T(8,128)(2,1)S(1)}, bf16[144,256]{1,0:T(8,128)(2,1)S(1)}, u32[]{:S(2)}, u32[]{:S(2)}) %collective-permute-start.22) | collective-permute-done | bytes 73760 | tf_op jit(solution)/shard_map/ppermute | solution.py:558
  92.5 2.6 %collective-permute-done.23.refs_6_ = bf16[144,256]{1,0:T(8,128)(2,1)S(1)} collective-permute-done((bf16[144,256]{1,0:T(8,128)(2,1)S(1)}, bf16[144,256]{1,0:T(8,128)(2,1)S(1)}, u32[]{:S(2)}, u32[]{:S(2)}) %collective-permute-start.23) | collective-permute-done | bytes 73760 | tf_op jit(solution)/shard_map/ppermute | solution.py:558
  95.1 1.9 %collective-permute-done.24.refs_7_ = bf16[144,256]{1,0:T(8,128)(2,1)S(1)} collective-permute-done((bf16[144,256]{1,0:T(8,128)(2,1)S(1)}, bf16[144,256]{1,0:T(8,128)(2,1)S(1)}, u32[]{:S(2)}, u32[]{:S(2)}) %collective-permute-start.24) | collective-permute-done | bytes 73760 | tf_op jit(solution)/shard_map/ppermute | solution.py:558
  97.1 0.6 copy-done.34
  97.7 2.5 %pick_partner.1 = bf16[8,144,256]{2,1,0:T(8,128)(2,1)} custom-call(s32[64]{0:T(128)} %get-tuple-element.39.ids, bf16[144,256]{1,0:T(8,128)(2,1)} %copy-done.4, bf16[144,256]{1,0:T(8,128)(2,1)} %copy-done.28, bf16[144,256]{1,0:T(8,128)(2,1)} %copy-done.29, bf16[144,256]{1,0:T(8,128)(2,1)} %copy-done.30, bf16[144,256]{1,0:T(8,128)(2,1)} %copy-done.31, ...), custom_call_target="tpu_custom_call" | custom-call | tf_op jit(solution)/shard_map/pick_partner/pallas_call | solution.py:36
  100.2 2.6 %collect_values.1.values = bf16[1024,128]{1,0:T(8,128)(2,1)} custom-call(s32[64]{0:T(128)} %get-tuple-element.39.ids, bf16[16,288,256]{2,1,0:T(8,128)(2,1)} %get-tuple-element.57.kept, bf16[16,288,256]{2,1,0:T(8,128)(2,1)} %collective-permute-done.25.swapped), custom_call_target="tpu_custom_call" | custom-call | tf_op jit(solution)/shard_map/collect_values/pallas_call | solution.py:36
  102.8 19.5 %all_to_all.25.mate = bf16[8,144,256]{2,1,0:T(8,128)(2,1)} all-to-all(bf16[8,144,256]{2,1,0:T(8,128)(2,1)S(1)} %copy-done.10), channel_id=1, replica_groups=mesh['z'=8,'xl'=2,'c'=2,'y'=4,'xh'=2] {'y','xh'}, dimensions={0} | all-to-all | bytes 1179648 | tf_op jit(solution)/shard_map/all_to_all | solution.py:581
  122.3 11.9 %attention.1 = (f32[16,48,256]{2,1,0:T(8,128)}, bf16[16,48,256]{2,1,0:T(8,128)(2,1)}, bf16[128,256]{1,0:T(8,128)(2,1)}, bf16[16,128]{1,0:T(8,128)(2,1)}) custom-call(s32[64]{0:T(128)} %get-tuple-element.39.ids, bf16[8,144,256]{2,1,0:T(8,128)(2,1)} %copy-done.11, bf16[8,144,256]{2,1,0:T(8,128)(2,1)} %all_to_all.25.mate, ...), custom_call_target="tpu_custom_call" | custom-call | flops 2147483648 | tf_op jit(solution)/shard_map/attention/pallas_call | solution.py:36
  134.2 0.1 collective-permute-start.26
  134.3 1.9 %collective-permute-done.26.received = bf16[16,48,256]{2,1,0:T(8,128)(2,1)S(1)} collective-permute-done((bf16[16,48,256]{2,1,0:T(8,128)(2,1)}, bf16[16,48,256]{2,1,0:T(8,128)(2,1)S(1)}, u32[]{:S(2)}, u32[]{:S(2)}) %collective-permute-start.26) | collective-permute-done | bytes 393248 | tf_op jit(solution)/shard_map/ppermute | solution.py:612
  136.2 1.1 copy-done.2
  137.3 0.8 add_core.1
  138.2 4.8 %all-to-all-start.3 = ((bf16[16,48,256]{2,1,0:T(8,128)(2,1)}), bf16[16,48,256]{2,1,0:T(8,128)(2,1)S(1)}, u32[]{:S(2)}, u32[]{:S(2)}) async-start(bf16[16,48,256]{2,1,0:T(8,128)(2,1)} %add_core.1), calls=%async_computation.3 | async-start | bytes 786432 | tf_op jit(solution)/shard_map/all_to_all | solution.py:613
  142.9 0.0 copy-start.5
  143.0 0.8 copy-done.5
  143.8 5.2 %hidden_grads.1 = bf16[128,8192]{1,0:T(8,128)(2,1)} custom-call(s32[64]{0:T(128)S(1)} %copy-done.7, bf16[128,256]{1,0:T(8,128)(2,1)S(1)} %copy-done.5, bf16[16,128]{1,0:T(8,128)(2,1)S(1)} %copy-done.8, bf16[16,288,256]{2,1,0:T(8,128)(2,1)S(1)} %copy-done, bf16[16,288,256]{2,1,0:T(8,128)(2,1)} %collective-permute-done.25.swapped), custom_call_target="tpu_custom_call" | custom-call | flops 536870912 | bytes 6291456 | tf_op jit(solution)/shard_map/hidden_grads/pallas_call | solution.py:36
  149.0 8.4 %all-to-all-done.3.received = bf16[16,48,256]{2,1,0:T(8,128)(2,1)S(1)} async-done(((bf16[16,48,256]{2,1,0:T(8,128)(2,1)}), bf16[16,48,256]{2,1,0:T(8,128)(2,1)S(1)}, u32[]{:S(2)}, u32[]{:S(2)}) %all-to-all-start.3) | async-done | bytes 393248 | tf_op jit(solution)/shard_map/all_to_all | solution.py:613
  157.4 0.1 sum_shares.1
  157.5 10.9 %all_to_all.26.received = bf16[8,48,256]{2,1,0:T(8,128)(2,1)S(1)} all-to-all(bf16[8,48,256]{2,1,0:T(8,128)(2,1)S(1)} %sum_shares.1), channel_id=1, replica_groups=mesh['z'=8,'xl'=2,'c'=2,'y'=4,'xh'=2] {'y','xh'}, dimensions={0} | all-to-all | bytes 393216 | tf_op jit(solution)/shard_map/all_to_all | solution.py:630
  168.3 1.3 unpack.1
  (82 shorter events, 0.2 us)
Async XLA Ops:
  0.6 48.7 %collective-permute-start = (bf16[128,8192]{1,0:T(8,128)(2,1)}, bf16[128,8192]{1,0:T(8,128)(2,1)}, u32[]{:S(2)}, u32[]{:S(2)}) collective-permute-start(bf16[128,8192]{1,0:T(8,128)(2,1)} %bitcast.10), channel_id=1, source_target_pairs={{0,8},{8,0},{1,9},{9,1},{2,10},{10,2},{3,11},{11,3},{4,12},{12,4},... | collective-permute-start | bytes 6291464 | tf_op jit(solution)/shard_map/ppermute | solution.py:508
  3.8 7.1 %collective-permute-start.1 = (bf16[288,256]{1,0:T(8,128)(2,1)}, bf16[288,256]{1,0:T(8,128)(2,1)S(1)}, u32[]{:S(2)}, u32[]{:S(2)}) collective-permute-start(bf16[288,256]{1,0:T(8,128)(2,1)} %get-tuple-element.40.refs_0_), channel_id=1, source_target_pairs={{0,16},{16,0},{1,17},{17,1},{2,18},{18,2},{3,19},{19,3},{4,20},{20... | collective-permute-start | bytes 442376 | tf_op jit(solution)/shard_map/ppermute | solution.py:507
  6.1 1.6 copy-start.1
  10.4 6.0 %copy-start.12 = (bf16[288,256]{1,0:T(8,128)(2,1)S(1)}, bf16[288,256]{1,0:T(8,128)(2,1)}, u32[]{:S(2)}) copy-start(bf16[288,256]{1,0:T(8,128)(2,1)} %get-tuple-element.40.refs_0_) | copy-start | bytes 442372
  10.8 14.9 %copy-start.13 = (bf16[288,256]{1,0:T(8,128)(2,1)}, bf16[288,256]{1,0:T(8,128)(2,1)S(1)}, u32[]{:S(2)}) copy-start(bf16[288,256]{1,0:T(8,128)(2,1)S(1)} %collective-permute-done.1.refs_1_) | copy-start | bytes 442372
  10.8 45.3 %all-to-all-start = ((bf16[8,128,1024]{2,1,0:T(8,128)(2,1)}), bf16[8,128,1024]{2,1,0:T(8,128)(2,1)}, u32[]{:S(2)}, u32[]{:S(2)}) async-start(bf16[8,128,1024]{2,1,0:T(8,128)(2,1)} %split_columns.1), calls=%async_computation | async-start | bytes 4194304 | tf_op jit(solution)/shard_map/all_to_all | solution.py:514
  16.4 9.4 %collective-permute-start.2 = (bf16[288,256]{1,0:T(8,128)(2,1)S(1)}, bf16[288,256]{1,0:T(8,128)(2,1)S(1)}, u32[]{:S(2)}, u32[]{:S(2)}) collective-permute-start(bf16[288,256]{1,0:T(8,128)(2,1)S(1)} %copy-done.12), channel_id=1, source_target_pairs={{0,32},{32,64},{64,96},{96,128},{128,160},{160,192},{192,224},{224... | collective-permute-start | bytes 442376 | tf_op jit(solution)/shard_map/ppermute | solution.py:509
  18.3 8.3 %collective-permute-start.5 = (bf16[288,256]{1,0:T(8,128)(2,1)S(1)}, bf16[288,256]{1,0:T(8,128)(2,1)S(1)}, u32[]{:S(2)}, u32[]{:S(2)}) collective-permute-start(bf16[288,256]{1,0:T(8,128)(2,1)S(1)} %collective-permute-done.1.refs_1_), channel_id=1, source_target_pairs={{0,224},{32,0},{64,32},{96,64},{128,96},{160,128},{192,160},{224,1... | collective-permute-start | bytes 442376 | tf_op jit(solution)/shard_map/ppermute | solution.py:486
  22.4 8.0 %collective-permute-start.3 = (bf16[288,256]{1,0:T(8,128)(2,1)S(1)}, bf16[288,256]{1,0:T(8,128)(2,1)S(1)}, u32[]{:S(2)}, u32[]{:S(2)}) collective-permute-start(bf16[288,256]{1,0:T(8,128)(2,1)S(1)} %copy-done.12), channel_id=1, source_target_pairs={{0,224},{32,0},{64,32},{96,64},{128,96},{160,128},{192,160},{224,1... | collective-permute-start | bytes 442376 | tf_op jit(solution)/shard_map/ppermute | solution.py:510
  25.7 24.3 %copy-start.14 = (bf16[288,256]{1,0:T(8,128)(2,1)}, bf16[288,256]{1,0:T(8,128)(2,1)S(1)}, u32[]{:S(2)}) copy-start(bf16[288,256]{1,0:T(8,128)(2,1)S(1)} %collective-permute-done.2.refs_2_) | copy-start | bytes 442372
  25.7 7.5 %collective-permute-start.6 = (bf16[288,256]{1,0:T(8,128)(2,1)S(1)}, bf16[288,256]{1,0:T(8,128)(2,1)S(1)}, u32[]{:S(2)}, u32[]{:S(2)}) collective-permute-start(bf16[288,256]{1,0:T(8,128)(2,1)S(1)} %collective-permute-done.2.refs_2_), channel_id=1, source_target_pairs={{0,32},{32,64},{64,96},{96,128},{128,160},{160,192},{192,224},{224... | collective-permute-start | bytes 442376 | tf_op jit(solution)/shard_map/ppermute | solution.py:484
  25.7 9.7 %collective-permute-start.4 = (bf16[288,256]{1,0:T(8,128)(2,1)S(1)}, bf16[288,256]{1,0:T(8,128)(2,1)S(1)}, u32[]{:S(2)}, u32[]{:S(2)}) collective-permute-start(bf16[288,256]{1,0:T(8,128)(2,1)S(1)} %collective-permute-done.1.refs_1_), channel_id=1, source_target_pairs={{0,32},{32,64},{64,96},{96,128},{128,160},{160,192},{192,224},{224... | collective-permute-start | bytes 442376 | tf_op jit(solution)/shard_map/ppermute | solution.py:484
  26.7 23.4 %copy-start.15 = (bf16[288,256]{1,0:T(8,128)(2,1)}, bf16[288,256]{1,0:T(8,128)(2,1)S(1)}, u32[]{:S(2)}) copy-start(bf16[288,256]{1,0:T(8,128)(2,1)S(1)} %collective-permute-done.5.refs_5_) | copy-start | bytes 442372
  26.7 8.7 %collective-permute-start.9 = (bf16[288,256]{1,0:T(8,128)(2,1)S(1)}, bf16[288,256]{1,0:T(8,128)(2,1)S(1)}, u32[]{:S(2)}, u32[]{:S(2)}) collective-permute-start(bf16[288,256]{1,0:T(8,128)(2,1)S(1)} %collective-permute-done.5.refs_5_), channel_id=1, source_target_pairs={{0,224},{32,0},{64,32},{96,64},{128,96},{160,128},{192,160},{224,1... | collective-permute-start | bytes 442376 | tf_op jit(solution)/shard_map/ppermute | solution.py:486
  30.3 19.7 %copy-start.16 = (bf16[288,256]{1,0:T(8,128)(2,1)}, bf16[288,256]{1,0:T(8,128)(2,1)S(1)}, u32[]{:S(2)}) copy-start(bf16[288,256]{1,0:T(8,128)(2,1)S(1)} %collective-permute-done.3.refs_3_) | copy-start | bytes 442372
  30.3 8.3 %collective-permute-start.7 = (bf16[288,256]{1,0:T(8,128)(2,1)S(1)}, bf16[288,256]{1,0:T(8,128)(2,1)S(1)}, u32[]{:S(2)}, u32[]{:S(2)}) collective-permute-start(bf16[288,256]{1,0:T(8,128)(2,1)S(1)} %collective-permute-done.3.refs_3_), channel_id=1, source_target_pairs={{0,224},{32,0},{64,32},{96,64},{128,96},{160,128},{192,160},{224,1... | collective-permute-start | bytes 442376 | tf_op jit(solution)/shard_map/ppermute | solution.py:486
  33.2 16.9 %copy-start.17 = (bf16[288,256]{1,0:T(8,128)(2,1)}, bf16[288,256]{1,0:T(8,128)(2,1)S(1)}, u32[]{:S(2)}) copy-start(bf16[288,256]{1,0:T(8,128)(2,1)S(1)} %collective-permute-done.6.refs_6_) | copy-start | bytes 442372
  33.2 6.6 %collective-permute-start.10 = (bf16[288,256]{1,0:T(8,128)(2,1)S(1)}, bf16[288,256]{1,0:T(8,128)(2,1)S(1)}, u32[]{:S(2)}, u32[]{:S(2)}) collective-permute-start(bf16[288,256]{1,0:T(8,128)(2,1)S(1)} %collective-permute-done.6.refs_6_), channel_id=1, source_target_pairs={{0,32},{32,64},{64,96},{96,128},{128,160},{160,192},{192,224},{224... | collective-permute-start | bytes 442376 | tf_op jit(solution)/shard_map/ppermute | solution.py:484
  35.4 14.7 %copy-start.18 = (bf16[288,256]{1,0:T(8,128)(2,1)}, bf16[288,256]{1,0:T(8,128)(2,1)S(1)}, u32[]{:S(2)}) copy-start(bf16[288,256]{1,0:T(8,128)(2,1)S(1)} %collective-permute-done.4.refs_4_) | copy-start | bytes 442372
  35.4 7.6 %collective-permute-start.8 = (bf16[288,256]{1,0:T(8,128)(2,1)S(1)}, bf16[288,256]{1,0:T(8,128)(2,1)S(1)}, u32[]{:S(2)}, u32[]{:S(2)}) collective-permute-start(bf16[288,256]{1,0:T(8,128)(2,1)S(1)} %collective-permute-done.4.refs_4_), channel_id=1, source_target_pairs={{0,32},{32,64},{64,96},{96,128},{128,160},{160,192},{192,224},{224... | collective-permute-start | bytes 442376 | tf_op jit(solution)/shard_map/ppermute | solution.py:484
  35.4 14.7 %copy-start.19 = (bf16[288,256]{1,0:T(8,128)(2,1)}, bf16[288,256]{1,0:T(8,128)(2,1)S(1)}, u32[]{:S(2)}) copy-start(bf16[288,256]{1,0:T(8,128)(2,1)S(1)} %collective-permute-done.9.refs_9_) | copy-start | bytes 442372
  35.4 7.6 %collective-permute-start.13 = (bf16[288,256]{1,0:T(8,128)(2,1)S(1)}, bf16[288,256]{1,0:T(8,128)(2,1)S(1)}, u32[]{:S(2)}, u32[]{:S(2)}) collective-permute-start(bf16[288,256]{1,0:T(8,128)(2,1)S(1)} %collective-permute-done.9.refs_9_), channel_id=1, source_target_pairs={{0,224},{32,0},{64,32},{96,64},{128,96},{160,128},{192,160},{224,1... | collective-permute-start | bytes 442376 | tf_op jit(solution)/shard_map/ppermute | solution.py:486
  38.6 11.5 %copy-start.20 = (bf16[288,256]{1,0:T(8,128)(2,1)}, bf16[288,256]{1,0:T(8,128)(2,1)S(1)}, u32[]{:S(2)}) copy-start(bf16[288,256]{1,0:T(8,128)(2,1)S(1)} %collective-permute-done.7.refs_7_) | copy-start | bytes 442372
  38.6 7.6 %collective-permute-start.11 = (bf16[288,256]{1,0:T(8,128)(2,1)S(1)}, bf16[288,256]{1,0:T(8,128)(2,1)S(1)}, u32[]{:S(2)}, u32[]{:S(2)}) collective-permute-start(bf16[288,256]{1,0:T(8,128)(2,1)S(1)} %collective-permute-done.7.refs_7_), channel_id=1, source_target_pairs={{0,224},{32,0},{64,32},{96,64},{128,96},{160,128},{192,160},{224,1... | collective-permute-start | bytes 442376 | tf_op jit(solution)/shard_map/ppermute | solution.py:486
  39.8 10.3 %copy-start.21 = (bf16[288,256]{1,0:T(8,128)(2,1)}, bf16[288,256]{1,0:T(8,128)(2,1)S(1)}, u32[]{:S(2)}) copy-start(bf16[288,256]{1,0:T(8,128)(2,1)S(1)} %collective-permute-done.10.refs_10_) | copy-start | bytes 442372
  39.8 6.7 %collective-permute-start.14 = (bf16[288,256]{1,0:T(8,128)(2,1)S(1)}, bf16[288,256]{1,0:T(8,128)(2,1)S(1)}, u32[]{:S(2)}, u32[]{:S(2)}) collective-permute-start(bf16[288,256]{1,0:T(8,128)(2,1)S(1)} %collective-permute-done.10.refs_10_), channel_id=1, source_target_pairs={{0,32},{32,64},{64,96},{96,128},{128,160},{160,192},{192,224},{224... | collective-permute-start | bytes 442376 | tf_op jit(solution)/shard_map/ppermute | solution.py:484
  43.0 7.1 %copy-start.22 = (bf16[288,256]{1,0:T(8,128)(2,1)}, bf16[288,256]{1,0:T(8,128)(2,1)S(1)}, u32[]{:S(2)}) copy-start(bf16[288,256]{1,0:T(8,128)(2,1)S(1)} %collective-permute-done.8.refs_8_) | copy-start | bytes 442372
  43.0 6.4 %collective-permute-start.12 = (bf16[288,256]{1,0:T(8,128)(2,1)S(1)}, bf16[288,256]{1,0:T(8,128)(2,1)S(1)}, u32[]{:S(2)}, u32[]{:S(2)}) collective-permute-start(bf16[288,256]{1,0:T(8,128)(2,1)S(1)} %collective-permute-done.8.refs_8_), channel_id=1, source_target_pairs={{0,32},{32,64},{64,96},{96,128},{128,160},{160,192},{192,224},{224... | collective-permute-start | bytes 442376 | tf_op jit(solution)/shard_map/ppermute | solution.py:484
  43.0 7.1 %copy-start.23 = (bf16[288,256]{1,0:T(8,128)(2,1)}, bf16[288,256]{1,0:T(8,128)(2,1)S(1)}, u32[]{:S(2)}) copy-start(bf16[288,256]{1,0:T(8,128)(2,1)S(1)} %collective-permute-done.13.refs_13_) | copy-start | bytes 442372
  43.0 6.3 %collective-permute-start.15 = (bf16[288,256]{1,0:T(8,128)(2,1)S(1)}, bf16[288,256]{1,0:T(8,128)(2,1)S(1)}, u32[]{:S(2)}, u32[]{:S(2)}) collective-permute-start(bf16[288,256]{1,0:T(8,128)(2,1)S(1)} %collective-permute-done.13.refs_13_), channel_id=1, source_target_pairs={{0,224},{32,0},{64,32},{96,64},{128,96},{160,128},{192,160},{224,1... | collective-permute-start | bytes 442376 | tf_op jit(solution)/shard_map/ppermute | solution.py:486
  46.2 3.9 %copy-start.24 = (bf16[288,256]{1,0:T(8,128)(2,1)}, bf16[288,256]{1,0:T(8,128)(2,1)S(1)}, u32[]{:S(2)}) copy-start(bf16[288,256]{1,0:T(8,128)(2,1)S(1)} %collective-permute-done.11.refs_11_) | copy-start | bytes 442372
  46.5 3.7 %copy-start.25 = (bf16[288,256]{1,0:T(8,128)(2,1)}, bf16[288,256]{1,0:T(8,128)(2,1)S(1)}, u32[]{:S(2)}) copy-start(bf16[288,256]{1,0:T(8,128)(2,1)S(1)} %collective-permute-done.14.refs_14_) | copy-start | bytes 442372
  49.4 0.8 copy-start.26
  49.4 0.7 copy-start.27
  50.2 14.7 %copy-start.6 = (s32[64]{0:T(128)S(1)}, s32[64]{0:T(128)}, u32[]{:S(2)}) copy-start(s32[64]{0:T(128)} %get-tuple-element.39.ids) | copy-start | bytes 772
  56.0 1.9 %collective-permute-start.16 = (f32[2,136,256]{2,1,0:T(8,128)}, f32[2,136,256]{2,1,0:T(8,128)S(1)}, u32[]{:S(2)}, u32[]{:S(2)}) collective-permute-start(f32[2,136,256]{2,1,0:T(8,128)} %get-tuple-element.43.mine), channel_id=1, source_target_pairs={{0,8},{8,0},{1,9},{9,1},{2,10},{10,2},{3,11},{11,3},{4,12},{12,4},... | collective-permute-start | bytes 835592 | tf_op jit(solution)/shard_map/ppermute | solution.py:535
  57.9 1.0 copy-start.3
  58.9 6.0 %collective-permute-start.17 = (bf16[2,144,256]{2,1,0:T(8,128)(2,1)S(1)}, bf16[2,144,256]{2,1,0:T(8,128)(2,1)S(1)}, u32[]{:S(2)}, u32[]{:S(2)}) collective-permute-start(bf16[2,144,256]{2,1,0:T(8,128)(2,1)S(1)} %join_cores.1.items.near), channel_id=1, source_target_pairs={{0,16},{16,0},{1,17},{17,1},{2,18},{18,2},{3,19},{19,3},{4,20},{20... | collective-permute-start | bytes 442376 | tf_op jit(solution)/shard_map/ppermute | solution.py:538
  65.4 0.6 copy-start.4
  66.1 34.1 %collective-permute-start.25 = (bf16[16,288,256]{2,1,0:T(8,128)(2,1)}, bf16[16,288,256]{2,1,0:T(8,128)(2,1)}, u32[]{:S(2)}, u32[]{:S(2)}) collective-permute-start(bf16[16,288,256]{2,1,0:T(8,128)(2,1)} %get-tuple-element.57.kept), channel_id=1, source_target_pairs={{0,8},{8,0},{1,9},{9,1},{2,10},{10,2},{3,11},{11,3},{4,12},{12,4},... | collective-permute-start | bytes 7077896 | tf_op jit(solution)/shard_map/ppermute | solution.py:560
  66.1 36.7 %all-to-all-start.1 = ((bf16[8,144,256]{2,1,0:T(8,128)(2,1)}), bf16[8,144,256]{2,1,0:T(8,128)(2,1)S(1)}, u32[]{:S(2)}, u32[]{:S(2)}) async-start(bf16[8,144,256]{2,1,0:T(8,128)(2,1)} %repeat_own.1), calls=%async_computation.1 | async-start | bytes 1179648 | tf_op jit(solution)/shard_map/all_to_all | solution.py:548
  72.8 8.7 %collective-permute-start.18 = (bf16[144,256]{1,0:T(8,128)(2,1)S(1)}, bf16[144,256]{1,0:T(8,128)(2,1)S(1)}, u32[]{:S(2)}, u32[]{:S(2)}) collective-permute-start(bf16[144,256]{1,0:T(8,128)(2,1)S(1)} %get-tuple-element.49), channel_id=1, source_target_pairs={{0,32},{32,64},{64,96},{96,128},{128,160},{160,192},{192,224},{224... | collective-permute-start | bytes 221192 | tf_op jit(solution)/shard_map/ppermute | solution.py:558
  72.8 12.1 %collective-permute-start.19 = (bf16[144,256]{1,0:T(8,128)(2,1)S(1)}, bf16[144,256]{1,0:T(8,128)(2,1)S(1)}, u32[]{:S(2)}, u32[]{:S(2)}) collective-permute-start(bf16[144,256]{1,0:T(8,128)(2,1)S(1)} %get-tuple-element.50), channel_id=1, source_target_pairs={{0,64},{32,96},{64,128},{96,160},{128,192},{160,224},{192,0},{224,... | collective-permute-start | bytes 221192 | tf_op jit(solution)/shard_map/ppermute | solution.py:558
  78.2 11.3 %collective-permute-start.20 = (bf16[144,256]{1,0:T(8,128)(2,1)S(1)}, bf16[144,256]{1,0:T(8,128)(2,1)S(1)}, u32[]{:S(2)}, u32[]{:S(2)}) collective-permute-start(bf16[144,256]{1,0:T(8,128)(2,1)S(1)} %get-tuple-element.51), channel_id=1, source_target_pairs={{0,96},{32,128},{64,160},{96,192},{128,224},{160,0},{192,32},{224,... | collective-permute-start | bytes 221192 | tf_op jit(solution)/shard_map/ppermute | solution.py:558
  78.2 11.3 %collective-permute-start.21 = (bf16[144,256]{1,0:T(8,128)(2,1)S(1)}, bf16[144,256]{1,0:T(8,128)(2,1)S(1)}, u32[]{:S(2)}, u32[]{:S(2)}) collective-permute-start(bf16[144,256]{1,0:T(8,128)(2,1)S(1)} %get-tuple-element.52), channel_id=1, source_target_pairs={{0,128},{32,160},{64,192},{96,224},{128,0},{160,32},{192,64},{224,... | collective-permute-start | bytes 221192 | tf_op jit(solution)/shard_map/ppermute | solution.py:558
  81.5 15.5 %copy-start.28 = (bf16[144,256]{1,0:T(8,128)(2,1)}, bf16[144,256]{1,0:T(8,128)(2,1)S(1)}, u32[]{:S(2)}) copy-start(bf16[144,256]{1,0:T(8,128)(2,1)S(1)} %collective-permute-done.18.refs_1_) | copy-start | bytes 221188
  81.5 11.0 %collective-permute-start.22 = (bf16[144,256]{1,0:T(8,128)(2,1)S(1)}, bf16[144,256]{1,0:T(8,128)(2,1)S(1)}, u32[]{:S(2)}, u32[]{:S(2)}) collective-permute-start(bf16[144,256]{1,0:T(8,128)(2,1)S(1)} %get-tuple-element.53), channel_id=1, source_target_pairs={{0,160},{32,192},{64,224},{96,0},{128,32},{160,64},{192,96},{224,1... | collective-permute-start | bytes 221192 | tf_op jit(solution)/shard_map/ppermute | solution.py:558
  84.9 12.1 %copy-start.29 = (bf16[144,256]{1,0:T(8,128)(2,1)}, bf16[144,256]{1,0:T(8,128)(2,1)S(1)}, u32[]{:S(2)}) copy-start(bf16[144,256]{1,0:T(8,128)(2,1)S(1)} %collective-permute-done.19.refs_2_) | copy-start | bytes 221188
  84.9 10.2 %collective-permute-start.23 = (bf16[144,256]{1,0:T(8,128)(2,1)S(1)}, bf16[144,256]{1,0:T(8,128)(2,1)S(1)}, u32[]{:S(2)}, u32[]{:S(2)}) collective-permute-start(bf16[144,256]{1,0:T(8,128)(2,1)S(1)} %get-tuple-element.54), channel_id=1, source_target_pairs={{0,192},{32,224},{64,0},{96,32},{128,64},{160,96},{192,128},{224,1... | collective-permute-start | bytes 221192 | tf_op jit(solution)/shard_map/ppermute | solution.py:558
  89.5 7.6 %copy-start.30 = (bf16[144,256]{1,0:T(8,128)(2,1)}, bf16[144,256]{1,0:T(8,128)(2,1)S(1)}, u32[]{:S(2)}) copy-start(bf16[144,256]{1,0:T(8,128)(2,1)S(1)} %collective-permute-done.20.refs_3_) | copy-start | bytes 221188
  89.5 7.6 %collective-permute-start.24 = (bf16[144,256]{1,0:T(8,128)(2,1)S(1)}, bf16[144,256]{1,0:T(8,128)(2,1)S(1)}, u32[]{:S(2)}, u32[]{:S(2)}) collective-permute-start(bf16[144,256]{1,0:T(8,128)(2,1)S(1)} %get-tuple-element.55), channel_id=1, source_target_pairs={{0,224},{32,0},{64,32},{96,64},{128,96},{160,128},{192,160},{224,1... | collective-permute-start | bytes 221192 | tf_op jit(solution)/shard_map/ppermute | solution.py:558
  89.5 7.6 %copy-start.31 = (bf16[144,256]{1,0:T(8,128)(2,1)}, bf16[144,256]{1,0:T(8,128)(2,1)S(1)}, u32[]{:S(2)}) copy-start(bf16[144,256]{1,0:T(8,128)(2,1)S(1)} %collective-permute-done.21.refs_4_) | copy-start | bytes 221188
  92.5 4.6 %copy-start.32 = (bf16[144,256]{1,0:T(8,128)(2,1)}, bf16[144,256]{1,0:T(8,128)(2,1)S(1)}, u32[]{:S(2)}) copy-start(bf16[144,256]{1,0:T(8,128)(2,1)S(1)} %collective-permute-done.22.refs_5_) | copy-start | bytes 221188
  95.1 1.9 %copy-start.33 = (bf16[144,256]{1,0:T(8,128)(2,1)}, bf16[144,256]{1,0:T(8,128)(2,1)S(1)}, u32[]{:S(2)}) copy-start(bf16[144,256]{1,0:T(8,128)(2,1)S(1)} %collective-permute-done.23.refs_6_) | copy-start | bytes 221188
  100.2 2.6 %copy-start.10 = (bf16[8,144,256]{2,1,0:T(8,128)(2,1)S(1)}, bf16[8,144,256]{2,1,0:T(8,128)(2,1)}, u32[]{:S(2)}) copy-start(bf16[8,144,256]{2,1,0:T(8,128)(2,1)} %pick_partner.1) | copy-start | bytes 1769476
  102.8 19.5 %copy-start.11 = (bf16[8,144,256]{2,1,0:T(8,128)(2,1)}, bf16[8,144,256]{2,1,0:T(8,128)(2,1)S(1)}, u32[]{:S(2)}) copy-start(bf16[8,144,256]{2,1,0:T(8,128)(2,1)S(1)} %all-to-all-done.1.own) | copy-start | bytes 1769476
  122.3 20.7 %copy-start.7 = (s32[64]{0:T(128)S(1)}, s32[64]{0:T(128)}, u32[]{:S(2)}) copy-start(s32[64]{0:T(128)} %get-tuple-element.39.ids) | copy-start | bytes 772
  134.2 8.8 %copy-start = (bf16[16,288,256]{2,1,0:T(8,128)(2,1)S(1)}, bf16[16,288,256]{2,1,0:T(8,128)(2,1)}, u32[]{:S(2)}) copy-start(bf16[16,288,256]{2,1,0:T(8,128)(2,1)} %get-tuple-element.57.kept) | copy-start | bytes 7077892
  134.2 2.0 %collective-permute-start.26 = (bf16[16,48,256]{2,1,0:T(8,128)(2,1)}, bf16[16,48,256]{2,1,0:T(8,128)(2,1)S(1)}, u32[]{:S(2)}, u32[]{:S(2)}) collective-permute-start(bf16[16,48,256]{2,1,0:T(8,128)(2,1)} %get-tuple-element.62), channel_id=1, source_target_pairs={{0,8},{8,0},{1,9},{9,1},{2,10},{10,2},{3,11},{11,3},{4,12},{12,4},... | collective-permute-start | bytes 1179656 | tf_op jit(solution)/shard_map/ppermute | solution.py:612
  136.2 1.1 copy-start.2
  137.3 5.6 %copy-start.8 = (bf16[16,128]{1,0:T(8,128)(2,1)S(1)}, bf16[16,128]{1,0:T(8,128)(2,1)}, u32[]{:S(2)}) copy-start(bf16[16,128]{1,0:T(8,128)(2,1)} %get-tuple-element.64.crows) | copy-start | bytes 12292
  138.2 19.3 %all-to-all-start.3 = ((bf16[16,48,256]{2,1,0:T(8,128)(2,1)}), bf16[16,48,256]{2,1,0:T(8,128)(2,1)S(1)}, u32[]{:S(2)}, u32[]{:S(2)}) async-start(bf16[16,48,256]{2,1,0:T(8,128)(2,1)} %add_core.1), calls=%async_computation.3 | async-start | bytes 786432 | tf_op jit(solution)/shard_map/all_to_all | solution.py:613
  142.9 0.8 copy-start.5
  143.8 24.6 %copy-start.9 = (f32[128]{0:T(128)S(1)}, f32[128]{0:T(128)}, u32[]{:S(2)}) copy-start(f32[128]{0:T(128)} %param.12) | copy-start | bytes 1540
  (1 other events, 0.6 us)

commit v3 on v2

--- a/solution.py
+++ b/solution.py
@@ -29,7 +29,7 @@
 VM = pl.BlockSpec(memory_space=pltpu.VMEM)
 SM = pl.BlockSpec(memory_space=pltpu.SMEM)
 HBM = pl.BlockSpec(memory_space=pltpu.HBM)
-WINDOW, GROUP, WANTED, MATE_STEP, HEADS, CORE = 16, 17, 18, 26, 27, 33
+WINDOW, GROUP, WANTED, MATE_STEP, HEADS, CORE, OWN = 16, 17, 18, 26, 27, 33, 34
 
 
 def call(kernel, outs, ins, scratch=(), far=(), far_out=(), flops=0, bytes_accessed=0, name=None, limit=48):
@@ -71,11 +71,13 @@
     ids[WINDOW] = window
     ids[GROUP] = group
     for k in range(NZ):
-        ids[WANTED + k] = (partner[((z + k) % NZ) * 4 + here] & 3) ^ here
-    ids[MATE_STEP] = (z - (mate >> 2) + NZ) % NZ
+        ids[WANTED + k] = (partner[k * 4 + here] & 3) ^ here
+    ids[MATE_STEP] = mate >> 2
     for n, x in enumerate((lengths[group], lengths[mate], labels[group], labels[mate], group, mate)):
         ids[HEADS + n] = x
     ids[CORE] = c
+    for n, (dy, dx) in enumerate(AROUND):
+        ids[OWN + n] = (((window >> 1) + dy) & 3) * 2 + ((window & 1) ^ dx)
     for copy in copies:
         copy.wait()
     s1, rest = halves(score[...])
@@ -111,17 +113,20 @@
                     out[4 * h + r, :, BLK * (first + k) : BLK * (first + k + 1)] = y[BLK * k :][:BLK, BLK * r :][:, :BLK]
 
 
-def project(ids, hidden, sibling, *refs):
-    blocks, (out, kept, x, w, exts, sems, out_sems) = refs[:-7], refs[-7:]
+def project(first_block, count, ids, hidden, sibling, *refs):
+    blocks, (out, kept, ahead, x, w, exts, sems, ahead_sems, out_sems) = refs[:count], refs[count:]
+
+    def columns(n):
+        return pl.ds(pl.multiple_of(ids[n] * ROWS, ROWS), ROWS)
+
     arrivals, leaving = [], []
     for n, block in enumerate(blocks):
-        columns = pl.ds(pl.multiple_of(ids[n] * ROWS, ROWS), ROWS)
         at = slice(ROWS * n, ROWS * (n + 1))
         pairs = (
             (block.at[0:ROWS], w.at[at]),
             (block.at[ROWS:BLOCK], exts.at[n]),
-            (hidden.at[:, columns], x.at[0:BLK, at]),
-            (sibling.at[:, columns], x.at[BLK : 2 * BLK, at]),
+            (hidden.at[:, columns(first_block + n)], x.at[0:BLK, at]),
+            (sibling.at[:, columns(first_block + n)], x.at[BLK : 2 * BLK, at]),
         )
         arrivals.append([pltpu.make_async_copy(a, b, sems.at[n, i]) for i, (a, b) in enumerate(pairs)])
         leaving.append(pltpu.make_async_copy(w.at[at], kept.at[n, 0:ROWS], out_sems.at[n, 0]))
@@ -129,10 +134,19 @@
     for group in arrivals:
         for copy in group:
             copy.start()
+    handed = []
+    for n in range(LAST_STEP):
+        at = slice(ROWS * n, ROWS * (n + 1))
+        for m, source in enumerate((hidden, sibling)):
+            target = ahead.at[BLK * m : BLK * (m + 1), at]
+            handed.append(
+                pltpu.make_async_copy(source.at[:, columns(len(ORDER) - LAST_STEP + n)], target, ahead_sems.at[n, m])
+            )
+            handed[-1].start()
     acc = jnp.zeros((2 * BLK, 2 * HEAD), F32)
     wide = [jnp.zeros((BLK, BLK), F32)] * 2
-    many = 4
-    for first in range(0, len(blocks), many):
+    for first in range(0, count, 4):
+        many = min(4, count - first)
         for n in range(first, first + many):
             for copy in arrivals[n]:
                 copy.wait()
@@ -146,50 +160,62 @@
             for m in range(2):
                 product = x[BLK * m : BLK * (m + 1), ROWS * n : ROWS * (n + 1)].astype(F32) * row
                 wide[m] += product[:, 0:BLK] + product[:, BLK : 2 * BLK]
-    zeros = jnp.zeros((8, 2 * HEAD), F32)
+    add_sums(None, acc, wide, out)
+    for copy in handed + leaving:
+        copy.wait()
+
+
+def add_sums(sums, acc, wide, out):
     for m in range(2):
+        qk = acc[BLK * m : BLK * (m + 1)]
         total = jnp.sum(wide[m].T, axis=0, keepdims=True)
-        out[m, 0:BLK, :] = acc[BLK * m : BLK * (m + 1)]
-        out[m, BLK : BLK + 8, :] = zeros + jnp.concatenate([total, total], axis=1)
-    for copy in leaving:
+        ext = jnp.broadcast_to(jnp.concatenate([total, total], axis=1), (8, 2 * HEAD))
+        out[m, 0:BLK, :] = qk if sums is None else sums[m, 0:BLK, :] + qk
+        out[m, BLK : BLK + 8, :] = ext if sums is None else sums[m, BLK : BLK + 8, :] + ext
+
+
+def project_last(before, ahead, *refs):
+    blocks, (out, kept, x, sums, sems) = refs[:LAST_STEP], refs[LAST_STEP:]
+    pairs = [(block, kept.at[n]) for n, block in enumerate(blocks)] + [(ahead, x), (before, sums)]
+    copies = [pltpu.make_async_copy(a, b, sems.at[n]) for n, (a, b) in enumerate(pairs)]
+    for copy in copies:
+        copy.start()
+    for copy in copies:
         copy.wait()
-
-
-def join_cores(mine, theirs, items):
+    acc = jnp.zeros((2 * BLK, 2 * HEAD), F32)
+    wide = [jnp.zeros((BLK, BLK), F32)] * 2
+    for n in range(LAST_STEP):
+        at = slice(ROWS * n, ROWS * (n + 1))
+        acc += jnp.dot(x[:, at], kept[n, 0:ROWS, :], preferred_element_type=F32)
+        ext = kept[n, ROWS : ROWS + EXT, :].astype(F32)
+        row = ext[0:1] + ext[1:2]
+        for m in range(2):
+            product = x[BLK * m : BLK * (m + 1), at].astype(F32) * row
+            wide[m] += product[:, 0:BLK] + product[:, BLK : 2 * BLK]
+    add_sums(sums, acc, wide, out)
+
+
+def join_cores(mine, theirs, items, first):
     row = lax.broadcasted_iota(jnp.int32, (EXT, 2 * HEAD), 0)
     for n in range(2):
         full = mine[n] + theirs[1 - n]
         high, low = halves(full[BLK : BLK + 1, 0:BLK])
         items[n, 0:BLK, :] = full[0:BLK].astype(BF16)
         items[n, BLK : BLK + EXT, :] = jnp.where(row == 0, jnp.concatenate([high, low], axis=1), 0.0).astype(BF16)
-
-
-def repeat_own(items, out, sems):
-    copies = [pltpu.make_async_copy(items.at[0], out.at[s], sems.at[s]) for s in range(NSEQ)]
-    for copy in copies:
-        copy.start()
-    for copy in copies:
-        copy.wait()
-
-
-def pick_for_planes(ids, near, side, *refs):
-    outs, items = refs[:-1], refs[-1]
+    first[...] = items[0]
+
+
+def pick_for_planes(ids, near, side, out, items):
     items[0:2] = near[...]
     items[2:4] = side[...]
-    for k, out in enumerate(outs):
-        out[...] = items[ids[WANTED + k]]
-
-
-def pick_partner(ids, *refs):
-    received, (out, mine, sem, sems) = refs[:-4], refs[-4:]
-    for k, ref in enumerate(received):
-
-        @pl.when(ids[MATE_STEP] == k)
-        def _(ref=ref):
-            copy = pltpu.make_async_copy(ref, mine, sem.at[0])
-            copy.start()
-            copy.wait()
-
+    for z in range(NZ):
+        out[z] = items[ids[WANTED + z]]
+
+
+def pick_partner(ids, received, out, mine, sem, sems):
+    copy = pltpu.make_async_copy(received.at[ids[MATE_STEP]], mine, sem.at[0])
+    copy.start()
+    copy.wait()
     copies = [pltpu.make_async_copy(mine, out.at[s], sems.at[s]) for s in range(NSEQ)]
     for copy in copies:
         copy.start()
@@ -197,28 +223,22 @@
         copy.wait()
 
 
-def collect_values(ids, kept, swapped, out, rows, sems):
-    copies = [
-        pltpu.make_async_copy(ref.at[:, ROWS + EXT : BLOCK, :], rows.at[n], sems.at[n])
-        for n, ref in enumerate((kept, swapped))
-    ]
-    for copy in copies:
-        copy.start()
-    for flip, copy in enumerate(copies):
-        copy.wait()
-        for n in range(len(ORDER)):
-            d = ids[n] ^ flip
-            for h in range(2):
-                start = pl.multiple_of(d * SHARE + EXT * h, EXT)
-                out[pl.ds(start, EXT), :] = rows[flip, n, :, HEAD * h : HEAD * (h + 1)]
-
-
 def attention(
     ids,
-    own,
     mate,
+    own_0,
+    own_1,
+    own_2,
+    own_3,
+    own_4,
+    own_5,
+    own_6,
+    own_7,
     hidden,
-    values,
+    kept_a,
+    kept_b,
+    swapped_a,
+    swapped_b,
     keep,
     send,
     grads,
@@ -237,23 +257,33 @@
     cacc,
     all_grads,
     columns,
+    value_parts,
     value_rows,
     shares,
     ext,
     sems,
     late_sems,
 ):
-    copies = []
-    for n, (ref, q, k) in enumerate(((mate, q_mate, k_mate), (own, q_own, k_own))):
-        copies.append(pltpu.make_async_copy(ref.at[:, 0:BLK, 0:HEAD], q, sems.at[3 * n]))
-        copies.append(pltpu.make_async_copy(ref.at[:, 0:BLK, HEAD : 2 * HEAD], k, sems.at[3 * n + 1]))
-        copies.append(pltpu.make_async_copy(ref.at[:, BLK : BLK + EXT, :], exts.at[n], sems.at[3 * n + 2]))
+    pieces = [
+        (mate.at[:, 0:BLK, 0:HEAD], q_mate),
+        (mate.at[:, 0:BLK, HEAD : 2 * HEAD], k_mate),
+        (mate.at[:, BLK : BLK + EXT, :], exts.at[0]),
+    ]
+    for n, ref in enumerate((own_0, own_1, own_2, own_3, own_4, own_5, own_6, own_7)):
+        at = ids[OWN + n]
+        pieces.append((ref.at[0:BLK, 0:HEAD], q_own.at[at]))
+        pieces.append((ref.at[0:BLK, HEAD : 2 * HEAD], k_own.at[at]))
+        pieces.append((ref.at[BLK : BLK + EXT, :], exts.at[1, at]))
+    copies = [pltpu.make_async_copy(a, b, sems.at[n]) for n, (a, b) in enumerate(pieces)]
     for copy in copies:
         copy.start()
     late = [
         pltpu.make_async_copy(hidden, columns, late_sems.at[0]),
-        pltpu.make_async_copy(values, value_rows, late_sems.at[1]),
     ]
+    for n, ref in enumerate((kept_a, kept_b, swapped_a, swapped_b)):
+        first, count = PARTS[n % 2]
+        part = value_parts.at[n // 2, first : first + count]
+        late.append(pltpu.make_async_copy(ref.at[:, ROWS + EXT : BLOCK, :], part, late_sems.at[1 + n]))
     for copy in late:
         copy.start()
     cacc[...] = jnp.zeros_like(cacc)
@@ -333,7 +363,7 @@
     def both(n, z):
         return first(n, z[0]), second(n, z[1])
 
-    z_own, z_mate = lax.fori_loop(0, SEQLEN // TB, both, (zero, zero))
+    z_own, z_mate = lax.fori_loop(0, SEQLEN // TB, both, (zero, zero), unroll=SEQLEN // TB)
 
     def head(z_row, length, label, index):
         count = jnp.full((1, 1), BLK * length, jnp.int32).astype(F32)
@@ -365,6 +395,11 @@
 
     for copy in late:
         copy.wait()
+    for flip in range(2):
+        for n in range(len(ORDER)):
+            for h in range(2):
+                start = pl.multiple_of((ids[n] ^ flip) * SHARE + EXT * h, EXT)
+                value_rows[pl.ds(start, EXT), :] = value_parts[flip, n, :, HEAD * h : HEAD * (h + 1)]
     chunk = 256
     wide = []
     for n in range(COLS // chunk):
@@ -452,12 +487,14 @@
     gs[...] = readout
 
 
-def hidden_grads(ids, grads, crows, kept, swapped, out):
+def hidden_grads(ids, grads, crows, *refs):
+    kept, out = refs[:-1], refs[-1]
     g = grads[...]
     c = crows[...].astype(F32).T.astype(BF16)
-    for flip, ref in enumerate((kept, swapped)):
-        for n in range(len(ORDER)):
-            start = pl.multiple_of((ids[n] ^ flip) * ROWS, ROWS)
+    for part, ref in enumerate(kept):
+        first, count = PARTS[part % 2]
+        for n in range(count):
+            start = pl.multiple_of((ids[first + n] ^ (part // 2)) * ROWS, ROWS)
             y = lax.dot_general(g, ref[n, 0:ROWS, :], LAST, preferred_element_type=F32)
             y += jnp.dot(c, ref[n, ROWS : ROWS + EXT, :], preferred_element_type=F32)
             out[:, pl.ds(start, ROWS)] = y.astype(BF16)
@@ -475,16 +512,15 @@
             ORDER.append((_step, _x))
 
 
-def gather_weights(block, other, up, down):
-    found = {(0, 0): block, (0, 1): other, (-1, 0): up, (1, 0): down}
-    for dz, dx in ORDER[2:]:
-        if (dz, dx) in found:
-            continue
-        if dz < 0:
-            found[(dz, dx)] = lax.ppermute(found[(dz + 1, dx)], "z", UP)
-        else:
-            found[(dz, dx)] = lax.ppermute(found[(dz - 1, dx)], "z", DOWN)
-    return [found[key] for key in ORDER]
+AROUND = [(0, 0), (0, 1), (1, 0), (1, 1), (-1, 0), (-1, 1), (2, 0), (2, 1)]
+LAST_STEP = 4
+PARTS = ((0, 12), (12, LAST_STEP))
+
+
+def ring_step(found, key):
+    dz, dx = key
+    step, way = (1, UP) if dz < 0 else (-1, DOWN)
+    found[key] = lax.ppermute(found[(dz + step, dx)], "z", way)
 
 
 def per_device(hidden, w_query, w_key, w_value, score_vec, labels, lengths, partner):
@@ -510,74 +546,82 @@
     down = lax.ppermute(block, "z", DOWN)
     later, _ = lax.optimization_barrier((tokens, block))
     split = call(split_columns, shape((NSEQ, BLK, COLS), BF16), (later,), name="split_columns", flops=1 << 30)
-    other, split = lax.optimization_barrier((other, split))
+    found = {(0, 0): block, (0, 1): other, (-1, 0): up, (1, 0): down}
+    second = ((-1, 1), (1, 1), (-2, 0), (2, 0))
+    for key in second:
+        ring_step(found, key)
+    split, *arrived = lax.optimization_barrier((split, *[found[key] for key in second]))
+    found.update(zip(second, arrived))
     hidden_t = lax.all_to_all(split, SEQ, 0, 0, tiled=True)
-    blocks = gather_weights(block, other, up, down)
-
-    partial, kept = call(
-        project,
-        (shape((2, BLK + 8, 2 * HEAD), F32), shape((len(ORDER), BLOCK, ROWS), BF16)),
-        (ids, tokens, sibling, *blocks),
-        far=range(1, 3 + len(ORDER)),
-        far_out=((len(ORDER), BLOCK, ROWS),),
+    for key in ORDER:
+        if key not in found:
+            ring_step(found, key)
+    partial_shape = shape((2, BLK + 8, 2 * HEAD), F32)
+
+    first, count = PARTS[0]
+    partial, kept_early, ahead = call(
+        functools.partial(project, first, count),
+        (partial_shape, shape((count, BLOCK, ROWS), BF16), shape((2 * BLK, LAST_STEP * ROWS), BF16)),
+        (ids, tokens, sibling, *[found[key] for key in ORDER[first : first + count]]),
+        far=range(1, 3 + count),
+        far_out=((count, BLOCK, ROWS),),
         scratch=[
-            pltpu.VMEM((2 * BLK, len(ORDER) * ROWS), BF16),
-            pltpu.VMEM((len(ORDER) * ROWS, ROWS), BF16),
-            pltpu.VMEM((len(ORDER), 2 * EXT, ROWS), BF16),
-            pltpu.SemaphoreType.DMA((len(ORDER), 4)),
-            pltpu.SemaphoreType.DMA((len(ORDER), 2)),
+            pltpu.VMEM((2 * BLK, count * ROWS), BF16),
+            pltpu.VMEM((count * ROWS, ROWS), BF16),
+            pltpu.VMEM((count, 2 * EXT, ROWS), BF16),
+            pltpu.SemaphoreType.DMA((count, 4)),
+            pltpu.SemaphoreType.DMA((LAST_STEP, 2)),
+            pltpu.SemaphoreType.DMA((count, 2)),
         ],
+        limit=62,
         name="project",
+        flops=count << 25,
+        bytes_accessed=count << 19,
+    )
+    partial, kept_late = call(
+        project_last,
+        (partial_shape, shape((LAST_STEP, BLOCK, ROWS), BF16)),
+        (partial, ahead, *[found[key] for key in ORDER[-LAST_STEP:]]),
+        far=range(2 + LAST_STEP),
+        scratch=[
+            pltpu.VMEM((2 * BLK, LAST_STEP * ROWS), BF16),
+            pltpu.VMEM(partial_shape.shape, F32),
+            pltpu.SemaphoreType.DMA((2 + LAST_STEP,)),
+        ],
         limit=62,
-        flops=1 << 29,
-        bytes_accessed=6 << 20,
+        name="project_last",
+        flops=LAST_STEP << 25,
     )
     theirs = lax.ppermute(partial, "c", SWAP)
-    theirs, hidden_t = lax.optimization_barrier((theirs, hidden_t))
-    items = call(join_cores, shape((2, *item), BF16), (partial, theirs), name="join_cores")
+    items, mine = call(
+        join_cores, (shape((2, *item), BF16), shape(item, BF16)), (partial, theirs), name="join_cores"
+    )
     side = lax.ppermute(items, "xl", SWAP)
-    repeated = call(
-        repeat_own,
-        shape((NSEQ, *item), BF16),
-        (items,),
-        far_out=((NSEQ, *item),),
-        scratch=[pltpu.SemaphoreType.DMA((NSEQ,))],
-        name="repeat_own",
-    )
-    side, repeated = lax.optimization_barrier((side, repeated))
-    own = lax.all_to_all(repeated, SEQ, 0, 0, tiled=True)
     slots = call(
         pick_for_planes,
-        tuple(shape(item, BF16) for _ in range(NZ)),
+        shape((NZ, *item), BF16),
         (ids, items, side),
         scratch=[pltpu.VMEM((4, *item), BF16)],
         name="pick_for_planes",
     )
-    arrived = {0: slots[0]}
-    for k in (4, 3, 5, 2, 6, 1, 7):
-        arrived[k] = lax.ppermute(slots[k], "z", [(i, (i + k) % NZ) for i in range(NZ)])
-    kept, _ = lax.optimization_barrier((kept, slots[0]))
-    swapped = lax.ppermute(kept, "c", SWAP)
-    values = call(
-        collect_values,
-        shape((COLS, HEAD), BF16),
-        (ids, kept, swapped),
-        far=(1, 2),
-        scratch=[pltpu.VMEM((2, len(ORDER), EXT, ROWS), BF16), pltpu.SemaphoreType.DMA((2,))],
-        name="collect_values",
-        limit=62,
-    )
+    slots, hidden_t, *kept = lax.optimization_barrier((slots, hidden_t, kept_early, kept_late))
+    arrived = lax.all_to_all(slots, "z", 0, 0, tiled=True)
+    kept += [lax.ppermute(part, "c", SWAP) for part in kept]
+    windows = {(0, 0): mine, (0, 1): lax.ppermute(mine, "xh", SWAP)}
+    for dy in (1, -1, 2):
+        for dx in (0, 1):
+            windows[(dy, dx)] = lax.ppermute(windows[(0, dx)], "y", [(i, (i - dy) % 4) for i in range(4)])
+    arrived, *own = lax.optimization_barrier((arrived, *[windows[key] for key in AROUND]))
     theirs = call(
         pick_partner,
         shape((NSEQ, *item), BF16),
-        (ids, *[arrived[k] for k in range(NZ)]),
-        far=range(1, 1 + NZ),
+        (ids, arrived),
+        far=(1,),
         far_out=((NSEQ, *item),),
         scratch=[pltpu.VMEM(item, BF16), pltpu.SemaphoreType.DMA((1,)), pltpu.SemaphoreType.DMA((NSEQ,))],
         name="pick_partner",
         limit=62,
     )
-    theirs, values = lax.optimization_barrier((theirs, values))
     mate = lax.all_to_all(theirs, SEQ, 0, 0, tiled=True)
 
     message = (NDP // 2, SHARE + EXT, 2 * HEAD)
@@ -585,8 +629,8 @@
     keep, send, grads, crows = call(
         attention,
         (shape(message, F32), shape(message, BF16), shape((BLK, 2 * HEAD), BF16), shape((EXT, BLK), BF16)),
-        (ids, own, mate, hidden_t, values),
-        far=(1, 2, 3, 4),
+        (ids, mate, *own, hidden_t, *kept),
+        far=range(1, 15),
         scratch=[
             pltpu.VMEM((2, NSEQ, EXT, 2 * HEAD), BF16),
             pltpu.VMEM((HEAD, SEQLEN), BF16),
@@ -599,11 +643,12 @@
             pltpu.VMEM((SEQLEN, BLK), F32),
             pltpu.VMEM((2 * HEAD + EXT, SEQLEN), BF16),
             pltpu.VMEM((NSEQ, BLK, COLS), BF16),
+            pltpu.VMEM((2, len(ORDER), EXT, ROWS), BF16),
             pltpu.VMEM((COLS, HEAD), BF16),
             pltpu.VMEM((2, NDP // 2, SHARE, 2 * HEAD), F32),
             ext,
-            pltpu.SemaphoreType.DMA((6,)),
-            pltpu.SemaphoreType.DMA((2,)),
+            pltpu.SemaphoreType.DMA((27,)),
+            pltpu.SemaphoreType.DMA((5,)),
         ],
         name="attention",
         limit=62,
@@ -614,7 +659,7 @@
     grad_hidden = call(
         hidden_grads,
         shape((BLK, NDP * ROWS), BF16),
-        (ids, grads, crows, kept, swapped),
+        (ids, grads, crows, *kept),
         name="hidden_grads",
         flops=1 << 29,
         bytes_accessed=6 << 20,

time: 170 us -> 161 us (0.947)
  blocking collectives: 30.3 us -> 10.9 us
  waiting for transfers between devices: 37.1 us -> 48.8 us
    all_to_all x1 -> x0, blocking collectives: 19.5 us -> none  [per_device(): mate = lax.all_to_all(theirs, SEQ, 0, 0, tiled=True)]
    all_to_all x1 -> x2, waiting for transfers between devices: 0.01 us -> 15.2 us  [the longest x1 12.5 us: per_device(): mate = lax.all_to_all(theirs, SEQ, 0, 0, tiled=True)]
    ppermute x20 -> x21, waiting for transfers between devices: 19.5 us -> 12.8 us  [the longest x12 8.62 us: ring_step(): found[key] = lax.ppermute(found[dz + step, dx], 'z', way)]
    ppermute x20 -> x21, starting transfers between devices: 32.2 us -> 26.7 us  [the longest x12 14.4 us: ring_step(): found[key] = lax.ppermute(found[dz + step, dx], 'z', way)]
    all_to_all x1 -> x2, starting transfers between devices: 6.72 us -> 11.7 us  [the longest x1 7.46 us: per_device(): mate = lax.all_to_all(theirs, SEQ, 0, 0, tiled=True)]
    ppermute x1, starting transfers between devices: 1.94 us -> 5.93 us  [per_device(): down = lax.ppermute(block, 'z', DOWN)]
    ppermute x1, waiting for transfers between devices: 0.01 us -> 3.53 us  [per_device(): down = lax.ppermute(block, 'z', DOWN)]
    ppermute x1, starting transfers between devices: 1.99 us -> 0.01 us  [per_device(): up = lax.ppermute(block, 'z', UP)]
  transfers between devices with their start and end apart: 30 -> 32, of which waited for: 18 -> 16; matrix products, arithmetic and copies ran while one was open for 0% -> 0% of each run, Pallas kernels for 13% -> 14%
where the time goes in v3:
time: 161 us; the launch traced here: 160 us
  starting transfers between devices  57.4 us (36%)
  waiting for transfers between devices  48.8 us (30%)
  Pallas kernels  35.4 us (22%)
  blocking collectives  10.9 us (7%)
  local copies, waits for them, and re-layouts  6 us (4%)
    pallas_call x12, Pallas kernels, call(): pl.pallas_call(kernel, out_shape=outs, in_specs=[SM if a.dtype == jnp.int...  35.4 us
    ppermute x12, starting transfers between devices, ring_step(): found[key] = lax.ppermute(found[dz + step, dx], 'z', way)  14.4 us
    all_to_all x1, waiting for transfers between devices, per_device(): mate = lax.all_to_all(theirs, SEQ, 0, 0, tiled=True)  12.5 us
    all_to_all x1, blocking collectives, per_device(): arrived = lax.all_to_all(sums, SEQ, 0, 0, tiled=True)  10.9 us
    all_to_all x1, waiting for transfers between devices, per_device(): arrived = lax.all_to_all(shares, ('z', 'xl'), 0, 0, tiled=True)  9.17 us
    ppermute x12, waiting for transfers between devices, ring_step(): found[key] = lax.ppermute(found[dz + step, dx], 'z', way)  8.62 us
    ppermute x6, starting transfers between devices, per_device(): lax.ppermute(windows[0, dx], 'y', [(i, (i - dy) % 4) for i in range(4)])  8.45 us
    all_to_all x1, starting transfers between devices, per_device(): mate = lax.all_to_all(theirs, SEQ, 0, 0, tiled=True)  7.46 us
  transfers between devices with their start and end apart: 32, of which 16 were waited for; matrix products, arithmetic and copies ran while one was open for 0% of the time, Pallas kernels for 14%

profile of v3, /device:TPU:2, one launch (start us, length us, event | category | flops | bytes accessed | tf_op | source)
XLA Modules:
  0.0 160.1 jit_solution(3291724502218503888)
XLA Ops:
  0.6 0.1 collective-permute-start
  0.7 0.6 pad_add_fusion.pos
  1.3 2.5 %pack_weights.1 = (bf16[288,256]{1,0:T(8,128)(2,1)}, s32[64]{0:T(128)}) custom-call(s32[4]{0:T(128)} %pad_add_fusion.pos, s32[32]{0:T(128)} %lengths.1, s32[32]{0:T(128)} %labels.1, s32[32]{0:T(128)} %partner.1, bf16[256,128]{1,0:T(8,128)(2,1)} %wq.1, bf16[256,128]{1,0:T(8,128)(2,1)} %wk.1, bf16[256,128]{1,0:T(8,128)(2,1)} %wv.1, f32[1,128]{1,0:T(1,128)} %bitcast.13), custom_call_target="tpu_custom_call" | custom-call | tf_op jit(solution)/shard_map/pack_weights/pallas_call | solution.py:36
  3.8 5.9 %collective-permute-start.3 = (bf16[288,256]{1,0:T(8,128)(2,1)}, bf16[288,256]{1,0:T(8,128)(2,1)S(1)}, u32[]{:S(2)}, u32[]{:S(2)}) collective-permute-start(bf16[288,256]{1,0:T(8,128)(2,1)} %get-tuple-element.46.refs_0_), channel_id=1, source_target_pairs={{0,224},{32,0},{64,32},{96,64},{128,96},{160,128},{192,160},{224,1... | collective-permute-start | bytes 442376 | tf_op jit(solution)/shard_map/ppermute | solution.py:546
  9.7 0.5 collective-permute-start.1
  10.3 3.5 %collective-permute-done.3.refs_3_ = bf16[288,256]{1,0:T(8,128)(2,1)S(1)} collective-permute-done((bf16[288,256]{1,0:T(8,128)(2,1)}, bf16[288,256]{1,0:T(8,128)(2,1)S(1)}, u32[]{:S(2)}, u32[]{:S(2)}) %collective-permute-start.3) | collective-permute-done | bytes 147488 | tf_op jit(solution)/shard_map/ppermute | solution.py:546
  13.8 3.6 %collective-permute-start.7 = (bf16[288,256]{1,0:T(8,128)(2,1)S(1)}, bf16[288,256]{1,0:T(8,128)(2,1)S(1)}, u32[]{:S(2)}, u32[]{:S(2)}) collective-permute-start(bf16[288,256]{1,0:T(8,128)(2,1)S(1)} %collective-permute-done.3.refs_3_), channel_id=1, source_target_pairs={{0,224},{32,0},{64,32},{96,64},{128,96},{160,128},{192,160},{224,1... | collective-permute-start | bytes 442376 | tf_op jit(solution)/shard_map/ppermute | solution.py:523
  17.4 3.2 %collective-permute-start.5 = (bf16[288,256]{1,0:T(8,128)(2,1)S(1)}, bf16[288,256]{1,0:T(8,128)(2,1)S(1)}, u32[]{:S(2)}, u32[]{:S(2)}) collective-permute-start(bf16[288,256]{1,0:T(8,128)(2,1)S(1)} %collective-permute-done.1.refs_1_), channel_id=1, source_target_pairs={{0,224},{32,0},{64,32},{96,64},{128,96},{160,128},{192,160},{224,1... | collective-permute-start | bytes 442376 | tf_op jit(solution)/shard_map/ppermute | solution.py:523
  20.6 1.6 copy-done
  22.2 2.7 %split_columns.1 = bf16[8,128,1024]{2,1,0:T(8,128)(2,1)} custom-call(bf16[128,8192]{1,0:T(8,128)(2,1)S(1)} %bitcast.12), custom_call_target="tpu_custom_call" | custom-call | flops 1073741824 | tf_op jit(solution)/shard_map/split_columns/pallas_call | solution.py:36
  25.0 2.0 %collective-permute-done.4.refs_4_ = bf16[288,256]{1,0:T(8,128)(2,1)S(1)} collective-permute-done((bf16[288,256]{1,0:T(8,128)(2,1)S(1)}, bf16[288,256]{1,0:T(8,128)(2,1)S(1)}, u32[]{:S(2)}, u32[]{:S(2)}) %collective-permute-start.4) | collective-permute-done | bytes 147488 | tf_op jit(solution)/shard_map/ppermute | solution.py:523
  27.0 6.0 %all-to-all-start = ((bf16[8,128,1024]{2,1,0:T(8,128)(2,1)}), bf16[8,128,1024]{2,1,0:T(8,128)(2,1)}, u32[]{:S(2)}, u32[]{:S(2)}) async-start(bf16[8,128,1024]{2,1,0:T(8,128)(2,1)} %split_columns.1), calls=%async_computation | async-start | bytes 4194304 | tf_op jit(solution)/shard_map/all_to_all | solution.py:555
  33.0 1.3 collective-permute-start.9
  34.3 0.8 collective-permute-start.8
  35.1 0.1 collective-permute-start.10
  35.2 3.7 %collective-permute-done.9.refs_9_ = bf16[288,256]{1,0:T(8,128)(2,1)S(1)} collective-permute-done((bf16[288,256]{1,0:T(8,128)(2,1)S(1)}, bf16[288,256]{1,0:T(8,128)(2,1)S(1)}, u32[]{:S(2)}, u32[]{:S(2)}) %collective-permute-start.9) | collective-permute-done | bytes 147488 | tf_op jit(solution)/shard_map/ppermute | solution.py:523
  38.9 1.8 %collective-permute-start.13 = (bf16[288,256]{1,0:T(8,128)(2,1)S(1)}, bf16[288,256]{1,0:T(8,128)(2,1)}, u32[]{:S(2)}, u32[]{:S(2)}) collective-permute-start(bf16[288,256]{1,0:T(8,128)(2,1)S(1)} %collective-permute-done.9.refs_9_), channel_id=1, source_target_pairs={{0,224},{32,0},{64,32},{96,64},{128,96},{160,128},{192,160},{224,1... | collective-permute-start | bytes 442376 | tf_op jit(solution)/shard_map/ppermute | solution.py:523
  40.7 0.1 collective-permute-start.11
  40.8 0.1 collective-permute-done.8.refs_8_
  40.9 1.8 %collective-permute-start.12 = (bf16[288,256]{1,0:T(8,128)(2,1)S(1)}, bf16[288,256]{1,0:T(8,128)(2,1)}, u32[]{:S(2)}, u32[]{:S(2)}) collective-permute-start(bf16[288,256]{1,0:T(8,128)(2,1)S(1)} %collective-permute-done.8.refs_8_), channel_id=1, source_target_pairs={{0,32},{32,64},{64,96},{96,128},{128,160},{160,192},{192,224},{224... | collective-permute-start | bytes 442376 | tf_op jit(solution)/shard_map/ppermute | solution.py:523
  42.7 0.8 collective-permute-done.10.refs_10_
  43.6 1.9 %collective-permute-done.13.refs_1_ = bf16[288,256]{1,0:T(8,128)(2,1)} collective-permute-done((bf16[288,256]{1,0:T(8,128)(2,1)S(1)}, bf16[288,256]{1,0:T(8,128)(2,1)}, u32[]{:S(2)}, u32[]{:S(2)}) %collective-permute-start.13) | collective-permute-done | bytes 147488 | tf_op jit(solution)/shard_map/ppermute | solution.py:523
  45.5 1.7 %collective-permute-start.15 = (bf16[288,256]{1,0:T(8,128)(2,1)}, bf16[288,256]{1,0:T(8,128)(2,1)}, u32[]{:S(2)}, u32[]{:S(2)}) collective-permute-start(bf16[288,256]{1,0:T(8,128)(2,1)} %collective-permute-done.13.refs_1_), channel_id=1, source_target_pairs={{0,224},{32,0},{64,32},{96,64},{128,96},{160,128},{192,160},{224,1... | collective-permute-start | bytes 442376 | tf_op jit(solution)/shard_map/ppermute | solution.py:523
  47.2 0.1 collective-permute-done.11.refs_11_
  47.2 0.6 copy-done.21
  47.9 5.5 %project.1 = (f32[2,136,256]{2,1,0:T(8,128)}, bf16[12,288,256]{2,1,0:T(8,128)(2,1)}, bf16[256,1024]{1,0:T(8,128)(2,1)}) custom-call(s32[64]{0:T(128)} %get-tuple-element.45.ids, bf16[128,8192]{1,0:T(8,128)(2,1)} %bitcast.11, bf16[128,8192]{1,0:T(8,128)(2,1)} %collective-permute-done.sibling, bf16[288,256]{1,0:T(8,128)(2,1)} %get-tuple-element.46.refs_0_, ...), custom_call_target="tpu_custom_call" | custom-call | flops 402653184 | bytes 6291456 | tf_op jit(solution)/shard_map/project/pallas_call | solution.py:36
  53.4 2.6 %project_last.1 = (f32[2,136,256]{2,1,0:T(8,128)}, bf16[4,288,256]{2,1,0:T(8,128)(2,1)}) custom-call(f32[2,136,256]{2,1,0:T(8,128)} %get-tuple-element.52.before, bf16[256,1024]{1,0:T(8,128)(2,1)} %get-tuple-element.53.ahead, bf16[288,256]{1,0:T(8,128)(2,1)} %collective-permute-done.12.refs_0_, bf16[288,256]{1,0:T(8,128)(2,1)} %collective-permute-done.13.refs_1_, ...), custom_call_target="tpu_custom_call" | custom-call | flops 134217728 | tf_op jit(solution)/shard_map/project_last/pallas_call | solution.py:36
  56.0 0.1 collective-permute-start.16
  56.1 1.8 %collective-permute-done.16.theirs = f32[2,136,256]{2,1,0:T(8,128)S(1)} collective-permute-done((f32[2,136,256]{2,1,0:T(8,128)}, f32[2,136,256]{2,1,0:T(8,128)S(1)}, u32[]{:S(2)}, u32[]{:S(2)}) %collective-permute-start.16) | collective-permute-done | bytes 278560 | tf_op jit(solution)/shard_map/ppermute | solution.py:595
  57.9 1.0 copy-done.4
  58.9 0.0 copy-start.5
  58.9 1.5 collective-permute-start.17
  60.4 4.5 %collective-permute-done.17.side = bf16[2,144,256]{2,1,0:T(8,128)(2,1)S(1)} collective-permute-done((bf16[2,144,256]{2,1,0:T(8,128)(2,1)S(1)}, bf16[2,144,256]{2,1,0:T(8,128)(2,1)S(1)}, u32[]{:S(2)}, u32[]{:S(2)}) %collective-permute-start.17) | collective-permute-done | bytes 147488 | tf_op jit(solution)/shard_map/ppermute | solution.py:599
  64.8 1.5 pick_for_planes.1
  66.3 4.2 %all-to-all-start.1 = ((bf16[8,144,256]{2,1,0:T(8,128)(2,1)}), bf16[8,144,256]{2,1,0:T(8,128)(2,1)}, u32[]{:S(2)}, u32[]{:S(2)}) async-start(bf16[8,144,256]{2,1,0:T(8,128)(2,1)} %pick_for_planes.1), calls=%async_computation.1 | async-start | bytes 1179648 | tf_op jit(solution)/shard_map/all_to_all | solution.py:608
  70.6 3.8 %collective-permute-start.18 = (bf16[144,256]{1,0:T(8,128)(2,1)S(1)}, bf16[144,256]{1,0:T(8,128)(2,1)S(1)}, u32[]{:S(2)}, u32[]{:S(2)}) collective-permute-start(bf16[144,256]{1,0:T(8,128)(2,1)S(1)} %get-tuple-element.62.own_0), channel_id=1, source_target_pairs={{0,1},{1,0},{2,3},{3,2},{4,5},{5,4},{6,7},{7,6},{8,9},{9,8},{10,11... | collective-permute-start | bytes 221192 | tf_op jit(solution)/shard_map/ppermute | solution.py:610
  74.4 3.0 %collective-permute-start.23 = (bf16[144,256]{1,0:T(8,128)(2,1)S(1)}, bf16[144,256]{1,0:T(8,128)(2,1)S(1)}, u32[]{:S(2)}, u32[]{:S(2)}) collective-permute-start(bf16[144,256]{1,0:T(8,128)(2,1)S(1)} %get-tuple-element.62.own_0), channel_id=1, source_target_pairs={{0,4},{2,6},{4,0},{6,2},{1,5},{3,7},{5,1},{7,3},{8,12},{10,14},{12... | collective-permute-start | bytes 221192 | tf_op jit(solution)/shard_map/ppermute | solution.py:613
  77.4 0.6 collective-permute-start.21
  78.0 2.7 %collective-permute-start.19 = (bf16[144,256]{1,0:T(8,128)(2,1)S(1)}, bf16[144,256]{1,0:T(8,128)(2,1)S(1)}, u32[]{:S(2)}, u32[]{:S(2)}) collective-permute-start(bf16[144,256]{1,0:T(8,128)(2,1)S(1)} %get-tuple-element.62.own_0), channel_id=1, source_target_pairs={{0,6},{2,0},{4,2},{6,4},{1,7},{3,1},{5,3},{7,5},{8,14},{10,8},{12,... | collective-permute-start | bytes 221192 | tf_op jit(solution)/shard_map/ppermute | solution.py:613
  80.7 1.2 collective-permute-start.22
  81.9 1.1 collective-permute-done.21.own_4
  83.0 1.0 collective-permute-start.20
  84.0 2.6 %collective-permute-done.24.own_7 = bf16[144,256]{1,0:T(8,128)(2,1)S(1)} collective-permute-done((bf16[144,256]{1,0:T(8,128)(2,1)S(1)}, bf16[144,256]{1,0:T(8,128)(2,1)S(1)}, u32[]{:S(2)}, u32[]{:S(2)}) %collective-permute-start.24) | collective-permute-done | bytes 73760 | tf_op jit(solution)/shard_map/ppermute | solution.py:613
  86.5 0.5 collective-permute-done.22.own_5
  87.1 0.1 copy-done.26
  87.2 0.6 copy-done.27
  87.8 2.6 %all-to-all-done.1.received = bf16[8,144,256]{2,1,0:T(8,128)(2,1)} async-done(((bf16[8,144,256]{2,1,0:T(8,128)(2,1)}), bf16[8,144,256]{2,1,0:T(8,128)(2,1)}, u32[]{:S(2)}, u32[]{:S(2)}) %all-to-all-start.1) | async-done | bytes 589856 | tf_op jit(solution)/shard_map/all_to_all | solution.py:608
  90.4 2.4 %pick_partner.1 = bf16[8,144,256]{2,1,0:T(8,128)(2,1)} custom-call(s32[64]{0:T(128)} %get-tuple-element.45.ids, bf16[8,144,256]{2,1,0:T(8,128)(2,1)} %all-to-all-done.1.received), custom_call_target="tpu_custom_call" | custom-call | tf_op jit(solution)/shard_map/pick_partner/pallas_call | solution.py:36
  92.9 7.5 %all-to-all-start.2 = ((bf16[8,144,256]{2,1,0:T(8,128)(2,1)}), bf16[8,144,256]{2,1,0:T(8,128)(2,1)S(1)}, u32[]{:S(2)}, u32[]{:S(2)}) async-start(bf16[8,144,256]{2,1,0:T(8,128)(2,1)} %pick_partner.1), calls=%async_computation.2 | async-start | bytes 1179648 | tf_op jit(solution)/shard_map/all_to_all | solution.py:625
  100.3 12.5 %all-to-all-done.2.mate = bf16[8,144,256]{2,1,0:T(8,128)(2,1)S(1)} async-done(((bf16[8,144,256]{2,1,0:T(8,128)(2,1)}), bf16[8,144,256]{2,1,0:T(8,128)(2,1)S(1)}, u32[]{:S(2)}, u32[]{:S(2)}) %all-to-all-start.2) | async-done | bytes 589856 | tf_op jit(solution)/shard_map/all_to_all | solution.py:625
  112.9 0.9 copy-done.11
  113.8 0.0 copy-start.8
  113.8 10.7 %attention.1 = (f32[16,48,256]{2,1,0:T(8,128)}, bf16[16,48,256]{2,1,0:T(8,128)(2,1)}, bf16[128,256]{1,0:T(8,128)(2,1)}, bf16[16,128]{1,0:T(8,128)(2,1)}) custom-call(s32[64]{0:T(128)} %get-tuple-element.45.ids, bf16[8,144,256]{2,1,0:T(8,128)(2,1)} %copy-done.11, bf16[144,256]{1,0:T(8,128)(2,1)} %copy-done.5, bf16[144,256]{1,0:T(8,128)(2,1)} %copy-done.22, ...), custom_call_target="tpu_custom_call" | custom-call | flops 2147483648 | tf_op jit(solution)/shard_map/attention/pallas_call | solution.py:36
  124.5 0.1 collective-permute-start.27
  124.6 1.9 %collective-permute-done.27.received = bf16[16,48,256]{2,1,0:T(8,128)(2,1)S(1)} collective-permute-done((bf16[16,48,256]{2,1,0:T(8,128)(2,1)}, bf16[16,48,256]{2,1,0:T(8,128)(2,1)S(1)}, u32[]{:S(2)}, u32[]{:S(2)}) %collective-permute-start.27) | collective-permute-done | bytes 393248 | tf_op jit(solution)/shard_map/ppermute | solution.py:657
  126.6 1.1 copy-done.3
  127.7 0.8 add_core.1
  128.5 4.8 %all-to-all-start.3 = ((bf16[16,48,256]{2,1,0:T(8,128)(2,1)}), bf16[16,48,256]{2,1,0:T(8,128)(2,1)S(1)}, u32[]{:S(2)}, u32[]{:S(2)}) async-start(bf16[16,48,256]{2,1,0:T(8,128)(2,1)} %add_core.1), calls=%async_computation.3 | async-start | bytes 786432 | tf_op jit(solution)/shard_map/all_to_all | solution.py:658
  133.3 0.0 copy-start.10
  133.3 5.3 %hidden_grads.1 = bf16[128,8192]{1,0:T(8,128)(2,1)} custom-call(s32[64]{0:T(128)S(1)} %copy-done.8, bf16[128,256]{1,0:T(8,128)(2,1)S(1)} %copy-done.6, bf16[16,128]{1,0:T(8,128)(2,1)S(1)} %copy-done.9, bf16[12,288,256]{2,1,0:T(8,128)(2,1)S(1)} %copy-done.2, bf16[4,288,256]{2,1,0:T(8,128)(2,1)} %get-tuple-element.72.kept_b.refs_1_, ...), custom_call_target="tpu_custom_call" | custom-call | flops 536870912 | bytes 6291456 | tf_op jit(solution)/shard_map/hidden_grads/pallas_call | solution.py:36
  138.6 9.2 %all-to-all-done.3.received = bf16[16,48,256]{2,1,0:T(8,128)(2,1)S(1)} async-done(((bf16[16,48,256]{2,1,0:T(8,128)(2,1)}), bf16[16,48,256]{2,1,0:T(8,128)(2,1)S(1)}, u32[]{:S(2)}, u32[]{:S(2)}) %all-to-all-start.3) | async-done | bytes 393248 | tf_op jit(solution)/shard_map/all_to_all | solution.py:658
  147.8 0.1 sum_shares.1
  147.9 10.9 %all_to_all.25.received = bf16[8,48,256]{2,1,0:T(8,128)(2,1)S(1)} all-to-all(bf16[8,48,256]{2,1,0:T(8,128)(2,1)S(1)} %sum_shares.1), channel_id=1, replica_groups=mesh['z'=8,'xl'=2,'c'=2,'y'=4,'xh'=2] {'y','xh'}, dimensions={0} | all-to-all | bytes 393216 | tf_op jit(solution)/shard_map/all_to_all | solution.py:675
  158.7 1.3 unpack.1
  (70 shorter events, 0.2 us)
Async XLA Ops:
  0.6 46.6 %collective-permute-start = (bf16[128,8192]{1,0:T(8,128)(2,1)}, bf16[128,8192]{1,0:T(8,128)(2,1)}, u32[]{:S(2)}, u32[]{:S(2)}) collective-permute-start(bf16[128,8192]{1,0:T(8,128)(2,1)} %bitcast.10), channel_id=1, source_target_pairs={{0,8},{8,0},{1,9},{9,1},{2,10},{10,2},{3,11},{11,3},{4,12},{12,4},... | collective-permute-start | bytes 6291464 | tf_op jit(solution)/shard_map/ppermute | solution.py:544
  3.8 10.0 %collective-permute-start.3 = (bf16[288,256]{1,0:T(8,128)(2,1)}, bf16[288,256]{1,0:T(8,128)(2,1)S(1)}, u32[]{:S(2)}, u32[]{:S(2)}) collective-permute-start(bf16[288,256]{1,0:T(8,128)(2,1)} %get-tuple-element.46.refs_0_), channel_id=1, source_target_pairs={{0,224},{32,0},{64,32},{96,64},{128,96},{160,128},{192,160},{224,1... | collective-permute-start | bytes 442376 | tf_op jit(solution)/shard_map/ppermute | solution.py:546
  9.7 7.7 %collective-permute-start.2 = (bf16[288,256]{1,0:T(8,128)(2,1)}, bf16[288,256]{1,0:T(8,128)(2,1)S(1)}, u32[]{:S(2)}, u32[]{:S(2)}) collective-permute-start(bf16[288,256]{1,0:T(8,128)(2,1)} %get-tuple-element.46.refs_0_), channel_id=1, source_target_pairs={{0,32},{32,64},{64,96},{96,128},{128,160},{160,192},{192,224},{224... | collective-permute-start | bytes 442376 | tf_op jit(solution)/shard_map/ppermute | solution.py:545
  9.7 7.7 %collective-permute-start.1 = (bf16[288,256]{1,0:T(8,128)(2,1)}, bf16[288,256]{1,0:T(8,128)(2,1)S(1)}, u32[]{:S(2)}, u32[]{:S(2)}) collective-permute-start(bf16[288,256]{1,0:T(8,128)(2,1)} %get-tuple-element.46.refs_0_), channel_id=1, source_target_pairs={{0,16},{16,0},{1,17},{17,1},{2,18},{18,2},{3,19},{19,3},{4,20},{20... | collective-permute-start | bytes 442376 | tf_op jit(solution)/shard_map/ppermute | solution.py:543
  13.8 11.1 %copy-start.12 = (bf16[288,256]{1,0:T(8,128)(2,1)}, bf16[288,256]{1,0:T(8,128)(2,1)S(1)}, u32[]{:S(2)}) copy-start(bf16[288,256]{1,0:T(8,128)(2,1)S(1)} %collective-permute-done.3.refs_3_) | copy-start | bytes 442372
  13.8 11.1 %collective-permute-start.7 = (bf16[288,256]{1,0:T(8,128)(2,1)S(1)}, bf16[288,256]{1,0:T(8,128)(2,1)S(1)}, u32[]{:S(2)}, u32[]{:S(2)}) collective-permute-start(bf16[288,256]{1,0:T(8,128)(2,1)S(1)} %collective-permute-done.3.refs_3_), channel_id=1, source_target_pairs={{0,224},{32,0},{64,32},{96,64},{128,96},{160,128},{192,160},{224,1... | collective-permute-start | bytes 442376 | tf_op jit(solution)/shard_map/ppermute | solution.py:523
  17.4 7.5 %copy-start.13 = (bf16[288,256]{1,0:T(8,128)(2,1)}, bf16[288,256]{1,0:T(8,128)(2,1)S(1)}, u32[]{:S(2)}) copy-start(bf16[288,256]{1,0:T(8,128)(2,1)S(1)} %collective-permute-done.2.refs_2_) | copy-start | bytes 442372
  17.4 7.5 %collective-permute-start.6 = (bf16[288,256]{1,0:T(8,128)(2,1)S(1)}, bf16[288,256]{1,0:T(8,128)(2,1)S(1)}, u32[]{:S(2)}, u32[]{:S(2)}) collective-permute-start(bf16[288,256]{1,0:T(8,128)(2,1)S(1)} %collective-permute-done.2.refs_2_), channel_id=1, source_target_pairs={{0,32},{32,64},{64,96},{96,128},{128,160},{160,192},{192,224},{224... | collective-permute-start | bytes 442376 | tf_op jit(solution)/shard_map/ppermute | solution.py:523
  17.4 7.5 %copy-start.14 = (bf16[288,256]{1,0:T(8,128)(2,1)}, bf16[288,256]{1,0:T(8,128)(2,1)S(1)}, u32[]{:S(2)}) copy-start(bf16[288,256]{1,0:T(8,128)(2,1)S(1)} %collective-permute-done.1.refs_1_) | copy-start | bytes 442372
  17.4 7.5 %collective-permute-start.5 = (bf16[288,256]{1,0:T(8,128)(2,1)S(1)}, bf16[288,256]{1,0:T(8,128)(2,1)S(1)}, u32[]{:S(2)}, u32[]{:S(2)}) collective-permute-start(bf16[288,256]{1,0:T(8,128)(2,1)S(1)} %collective-permute-done.1.refs_1_), channel_id=1, source_target_pairs={{0,224},{32,0},{64,32},{96,64},{128,96},{160,128},{192,160},{224,1... | collective-permute-start | bytes 442376 | tf_op jit(solution)/shard_map/ppermute | solution.py:523
  20.6 6.4 %collective-permute-start.4 = (bf16[288,256]{1,0:T(8,128)(2,1)S(1)}, bf16[288,256]{1,0:T(8,128)(2,1)S(1)}, u32[]{:S(2)}, u32[]{:S(2)}) collective-permute-start(bf16[288,256]{1,0:T(8,128)(2,1)S(1)} %collective-permute-done.1.refs_1_), channel_id=1, source_target_pairs={{0,32},{32,64},{64,96},{96,128},{128,160},{160,192},{192,224},{224... | collective-permute-start | bytes 442376 | tf_op jit(solution)/shard_map/ppermute | solution.py:523
  20.6 1.6 copy-start
  24.9 15.8 %copy-start.15 = (bf16[288,256]{1,0:T(8,128)(2,1)}, bf16[288,256]{1,0:T(8,128)(2,1)S(1)}, u32[]{:S(2)}) copy-start(bf16[288,256]{1,0:T(8,128)(2,1)S(1)} %collective-permute-done.7.refs_7_) | copy-start | bytes 442372
  24.9 10.2 %copy-start.16 = (bf16[288,256]{1,0:T(8,128)(2,1)}, bf16[288,256]{1,0:T(8,128)(2,1)S(1)}, u32[]{:S(2)}) copy-start(bf16[288,256]{1,0:T(8,128)(2,1)S(1)} %collective-permute-done.6.refs_6_) | copy-start | bytes 442372
  25.0 8.1 %copy-start.17 = (bf16[288,256]{1,0:T(8,128)(2,1)}, bf16[288,256]{1,0:T(8,128)(2,1)S(1)}, u32[]{:S(2)}) copy-start(bf16[288,256]{1,0:T(8,128)(2,1)S(1)} %collective-permute-done.5.refs_5_) | copy-start | bytes 442372
  27.0 7.4 %copy-start.18 = (bf16[288,256]{1,0:T(8,128)(2,1)}, bf16[288,256]{1,0:T(8,128)(2,1)S(1)}, u32[]{:S(2)}) copy-start(bf16[288,256]{1,0:T(8,128)(2,1)S(1)} %collective-permute-done.4.refs_4_) | copy-start | bytes 442372
  27.0 39.3 %all-to-all-start = ((bf16[8,128,1024]{2,1,0:T(8,128)(2,1)}), bf16[8,128,1024]{2,1,0:T(8,128)(2,1)}, u32[]{:S(2)}, u32[]{:S(2)}) async-start(bf16[8,128,1024]{2,1,0:T(8,128)(2,1)} %split_columns.1), calls=%async_computation | async-start | bytes 4194304 | tf_op jit(solution)/shard_map/all_to_all | solution.py:555
  33.0 5.9 %collective-permute-start.9 = (bf16[288,256]{1,0:T(8,128)(2,1)S(1)}, bf16[288,256]{1,0:T(8,128)(2,1)S(1)}, u32[]{:S(2)}, u32[]{:S(2)}) collective-permute-start(bf16[288,256]{1,0:T(8,128)(2,1)S(1)} %collective-permute-done.5.refs_5_), channel_id=1, source_target_pairs={{0,224},{32,0},{64,32},{96,64},{128,96},{160,128},{192,160},{224,1... | collective-permute-start | bytes 442376 | tf_op jit(solution)/shard_map/ppermute | solution.py:523
  34.3 6.6 %collective-permute-start.8 = (bf16[288,256]{1,0:T(8,128)(2,1)S(1)}, bf16[288,256]{1,0:T(8,128)(2,1)S(1)}, u32[]{:S(2)}, u32[]{:S(2)}) collective-permute-start(bf16[288,256]{1,0:T(8,128)(2,1)S(1)} %collective-permute-done.4.refs_4_), channel_id=1, source_target_pairs={{0,32},{32,64},{64,96},{96,128},{128,160},{160,192},{192,224},{224... | collective-permute-start | bytes 442376 | tf_op jit(solution)/shard_map/ppermute | solution.py:523
  35.1 8.4 %collective-permute-start.10 = (bf16[288,256]{1,0:T(8,128)(2,1)S(1)}, bf16[288,256]{1,0:T(8,128)(2,1)}, u32[]{:S(2)}, u32[]{:S(2)}) collective-permute-start(bf16[288,256]{1,0:T(8,128)(2,1)S(1)} %collective-permute-done.6.refs_6_), channel_id=1, source_target_pairs={{0,32},{32,64},{64,96},{96,128},{128,160},{160,192},{192,224},{224... | collective-permute-start | bytes 442376 | tf_op jit(solution)/shard_map/ppermute | solution.py:523
  38.9 8.3 %copy-start.19 = (bf16[288,256]{1,0:T(8,128)(2,1)}, bf16[288,256]{1,0:T(8,128)(2,1)S(1)}, u32[]{:S(2)}) copy-start(bf16[288,256]{1,0:T(8,128)(2,1)S(1)} %collective-permute-done.9.refs_9_) | copy-start | bytes 442372
  38.9 6.5 %collective-permute-start.13 = (bf16[288,256]{1,0:T(8,128)(2,1)S(1)}, bf16[288,256]{1,0:T(8,128)(2,1)}, u32[]{:S(2)}, u32[]{:S(2)}) collective-permute-start(bf16[288,256]{1,0:T(8,128)(2,1)S(1)} %collective-permute-done.9.refs_9_), channel_id=1, source_target_pairs={{0,224},{32,0},{64,32},{96,64},{128,96},{160,128},{192,160},{224,1... | collective-permute-start | bytes 442376 | tf_op jit(solution)/shard_map/ppermute | solution.py:523
  40.7 6.5 %collective-permute-start.11 = (bf16[288,256]{1,0:T(8,128)(2,1)S(1)}, bf16[288,256]{1,0:T(8,128)(2,1)S(1)}, u32[]{:S(2)}, u32[]{:S(2)}) collective-permute-start(bf16[288,256]{1,0:T(8,128)(2,1)S(1)} %collective-permute-done.7.refs_7_), channel_id=1, source_target_pairs={{0,224},{32,0},{64,32},{96,64},{128,96},{160,128},{192,160},{224,1... | collective-permute-start | bytes 442376 | tf_op jit(solution)/shard_map/ppermute | solution.py:523
  40.9 6.3 %copy-start.20 = (bf16[288,256]{1,0:T(8,128)(2,1)}, bf16[288,256]{1,0:T(8,128)(2,1)S(1)}, u32[]{:S(2)}) copy-start(bf16[288,256]{1,0:T(8,128)(2,1)S(1)} %collective-permute-done.8.refs_8_) | copy-start | bytes 442372
  40.9 12.5 %collective-permute-start.12 = (bf16[288,256]{1,0:T(8,128)(2,1)S(1)}, bf16[288,256]{1,0:T(8,128)(2,1)}, u32[]{:S(2)}, u32[]{:S(2)}) collective-permute-start(bf16[288,256]{1,0:T(8,128)(2,1)S(1)} %collective-permute-done.8.refs_8_), channel_id=1, source_target_pairs={{0,32},{32,64},{64,96},{96,128},{128,160},{160,192},{192,224},{224... | collective-permute-start | bytes 442376 | tf_op jit(solution)/shard_map/ppermute | solution.py:523
  43.5 9.8 %collective-permute-start.14 = (bf16[288,256]{1,0:T(8,128)(2,1)}, bf16[288,256]{1,0:T(8,128)(2,1)}, u32[]{:S(2)}, u32[]{:S(2)}) collective-permute-start(bf16[288,256]{1,0:T(8,128)(2,1)} %collective-permute-done.10.refs_10_), channel_id=1, source_target_pairs={{0,32},{32,64},{64,96},{96,128},{128,160},{160,192},{192,224},{224... | collective-permute-start | bytes 442376 | tf_op jit(solution)/shard_map/ppermute | solution.py:523
  45.5 7.9 %collective-permute-start.15 = (bf16[288,256]{1,0:T(8,128)(2,1)}, bf16[288,256]{1,0:T(8,128)(2,1)}, u32[]{:S(2)}, u32[]{:S(2)}) collective-permute-start(bf16[288,256]{1,0:T(8,128)(2,1)} %collective-permute-done.13.refs_1_), channel_id=1, source_target_pairs={{0,224},{32,0},{64,32},{96,64},{128,96},{160,128},{192,160},{224,1... | collective-permute-start | bytes 442376 | tf_op jit(solution)/shard_map/ppermute | solution.py:523
  47.2 0.7 copy-start.21
  47.9 17.0 %copy-start.7 = (s32[64]{0:T(128)S(1)}, s32[64]{0:T(128)}, u32[]{:S(2)}) copy-start(s32[64]{0:T(128)} %get-tuple-element.45.ids) | copy-start | bytes 772
  53.4 13.0 %copy-start.1 = (bf16[12,288,256]{2,1,0:T(8,128)(2,1)S(1)}, bf16[12,288,256]{2,1,0:T(8,128)(2,1)}, u32[]{:S(2)}) copy-start(bf16[12,288,256]{2,1,0:T(8,128)(2,1)} %get-tuple-element.71.kept_a.refs_0_) | copy-start | bytes 5308420
  56.0 1.9 %collective-permute-start.16 = (f32[2,136,256]{2,1,0:T(8,128)}, f32[2,136,256]{2,1,0:T(8,128)S(1)}, u32[]{:S(2)}, u32[]{:S(2)}) collective-permute-start(f32[2,136,256]{2,1,0:T(8,128)} %get-tuple-element.54.mine), channel_id=1, source_target_pairs={{0,8},{8,0},{1,9},{9,1},{2,10},{10,2},{3,11},{11,3},{4,12},{12,4},... | collective-permute-start | bytes 835592 | tf_op jit(solution)/shard_map/ppermute | solution.py:595
  57.9 1.0 copy-start.4
  58.9 34.0 %copy-start.5 = (bf16[144,256]{1,0:T(8,128)(2,1)}, bf16[144,256]{1,0:T(8,128)(2,1)S(1)}, u32[]{:S(2)}) copy-start(bf16[144,256]{1,0:T(8,128)(2,1)S(1)} %get-tuple-element.62.own_0) | copy-start | bytes 221188
  58.9 6.0 %collective-permute-start.17 = (bf16[2,144,256]{2,1,0:T(8,128)(2,1)S(1)}, bf16[2,144,256]{2,1,0:T(8,128)(2,1)S(1)}, u32[]{:S(2)}, u32[]{:S(2)}) collective-permute-start(bf16[2,144,256]{2,1,0:T(8,128)(2,1)S(1)} %get-tuple-element.55.near), channel_id=1, source_target_pairs={{0,16},{16,0},{1,17},{17,1},{2,18},{18,2},{3,19},{19,3},{4,20},{20... | collective-permute-start | bytes 442376 | tf_op jit(solution)/shard_map/ppermute | solution.py:599
  66.3 47.4 %collective-permute-start.25 = (bf16[12,288,256]{2,1,0:T(8,128)(2,1)S(1)}, bf16[12,288,256]{2,1,0:T(8,128)(2,1)}, u32[]{:S(2)}, u32[]{:S(2)}) collective-permute-start(bf16[12,288,256]{2,1,0:T(8,128)(2,1)S(1)} %copy-done.1), channel_id=1, source_target_pairs={{0,8},{8,0},{1,9},{9,1},{2,10},{10,2},{3,11},{11,3},{4,12},{12,4},... | collective-permute-start | bytes 5308424 | tf_op jit(solution)/shard_map/ppermute | solution.py:609
  66.3 24.1 %all-to-all-start.1 = ((bf16[8,144,256]{2,1,0:T(8,128)(2,1)}), bf16[8,144,256]{2,1,0:T(8,128)(2,1)}, u32[]{:S(2)}, u32[]{:S(2)}) async-start(bf16[8,144,256]{2,1,0:T(8,128)(2,1)} %pick_for_planes.1), calls=%async_computation.1 | async-start | bytes 1179648 | tf_op jit(solution)/shard_map/all_to_all | solution.py:608
  70.6 10.1 %collective-permute-start.18 = (bf16[144,256]{1,0:T(8,128)(2,1)S(1)}, bf16[144,256]{1,0:T(8,128)(2,1)S(1)}, u32[]{:S(2)}, u32[]{:S(2)}) collective-permute-start(bf16[144,256]{1,0:T(8,128)(2,1)S(1)} %get-tuple-element.62.own_0), channel_id=1, source_target_pairs={{0,1},{1,0},{2,3},{3,2},{4,5},{5,4},{6,7},{7,6},{8,9},{9,8},{10,11... | collective-permute-start | bytes 221192 | tf_op jit(solution)/shard_map/ppermute | solution.py:610
  74.4 6.2 %collective-permute-start.23 = (bf16[144,256]{1,0:T(8,128)(2,1)S(1)}, bf16[144,256]{1,0:T(8,128)(2,1)S(1)}, u32[]{:S(2)}, u32[]{:S(2)}) collective-permute-start(bf16[144,256]{1,0:T(8,128)(2,1)S(1)} %get-tuple-element.62.own_0), channel_id=1, source_target_pairs={{0,4},{2,6},{4,0},{6,2},{1,5},{3,7},{5,1},{7,3},{8,12},{10,14},{12... | collective-permute-start | bytes 221192 | tf_op jit(solution)/shard_map/ppermute | solution.py:613
  77.4 5.6 %collective-permute-start.21 = (bf16[144,256]{1,0:T(8,128)(2,1)S(1)}, bf16[144,256]{1,0:T(8,128)(2,1)S(1)}, u32[]{:S(2)}, u32[]{:S(2)}) collective-permute-start(bf16[144,256]{1,0:T(8,128)(2,1)S(1)} %get-tuple-element.62.own_0), channel_id=1, source_target_pairs={{0,2},{2,4},{4,6},{6,0},{1,3},{3,5},{5,7},{7,1},{8,10},{10,12},{12... | collective-permute-start | bytes 221192 | tf_op jit(solution)/shard_map/ppermute | solution.py:613
  78.0 6.0 %collective-permute-start.19 = (bf16[144,256]{1,0:T(8,128)(2,1)S(1)}, bf16[144,256]{1,0:T(8,128)(2,1)S(1)}, u32[]{:S(2)}, u32[]{:S(2)}) collective-permute-start(bf16[144,256]{1,0:T(8,128)(2,1)S(1)} %get-tuple-element.62.own_0), channel_id=1, source_target_pairs={{0,6},{2,0},{4,2},{6,4},{1,7},{3,1},{5,3},{7,5},{8,14},{10,8},{12,... | collective-permute-start | bytes 221192 | tf_op jit(solution)/shard_map/ppermute | solution.py:613
  80.6 33.1 %copy-start.22 = (bf16[144,256]{1,0:T(8,128)(2,1)}, bf16[144,256]{1,0:T(8,128)(2,1)S(1)}, u32[]{:S(2)}) copy-start(bf16[144,256]{1,0:T(8,128)(2,1)S(1)} %collective-permute-done.18.own_1) | copy-start | bytes 221188
  80.6 5.9 %collective-permute-start.24 = (bf16[144,256]{1,0:T(8,128)(2,1)S(1)}, bf16[144,256]{1,0:T(8,128)(2,1)S(1)}, u32[]{:S(2)}, u32[]{:S(2)}) collective-permute-start(bf16[144,256]{1,0:T(8,128)(2,1)S(1)} %collective-permute-done.18.own_1), channel_id=1, source_target_pairs={{0,4},{2,6},{4,0},{6,2},{1,5},{3,7},{5,1},{7,3},{8,12},{10,14},{12... | collective-permute-start | bytes 221192 | tf_op jit(solution)/shard_map/ppermute | solution.py:613
  80.6 33.1 %copy-start.23 = (bf16[144,256]{1,0:T(8,128)(2,1)}, bf16[144,256]{1,0:T(8,128)(2,1)S(1)}, u32[]{:S(2)}) copy-start(bf16[144,256]{1,0:T(8,128)(2,1)S(1)} %collective-permute-done.23.own_6) | copy-start | bytes 221188
  80.7 6.4 %collective-permute-start.22 = (bf16[144,256]{1,0:T(8,128)(2,1)S(1)}, bf16[144,256]{1,0:T(8,128)(2,1)S(1)}, u32[]{:S(2)}, u32[]{:S(2)}) collective-permute-start(bf16[144,256]{1,0:T(8,128)(2,1)S(1)} %collective-permute-done.18.own_1), channel_id=1, source_target_pairs={{0,2},{2,4},{4,6},{6,0},{1,3},{3,5},{5,7},{7,1},{8,10},{10,12},{12... | collective-permute-start | bytes 221192 | tf_op jit(solution)/shard_map/ppermute | solution.py:613
  82.9 4.1 %copy-start.24 = (bf16[144,256]{1,0:T(8,128)(2,1)}, bf16[144,256]{1,0:T(8,128)(2,1)S(1)}, u32[]{:S(2)}) copy-start(bf16[144,256]{1,0:T(8,128)(2,1)S(1)} %collective-permute-done.21.own_4) | copy-start | bytes 221188
  83.0 4.8 %collective-permute-start.20 = (bf16[144,256]{1,0:T(8,128)(2,1)S(1)}, bf16[144,256]{1,0:T(8,128)(2,1)}, u32[]{:S(2)}, u32[]{:S(2)}) collective-permute-start(bf16[144,256]{1,0:T(8,128)(2,1)S(1)} %collective-permute-done.18.own_1), channel_id=1, source_target_pairs={{0,6},{2,0},{4,2},{6,4},{1,7},{3,1},{5,3},{7,5},{8,14},{10,8},{12,... | collective-permute-start | bytes 221192 | tf_op jit(solution)/shard_map/ppermute | solution.py:613
  84.0 3.1 %copy-start.25 = (bf16[144,256]{1,0:T(8,128)(2,1)}, bf16[144,256]{1,0:T(8,128)(2,1)S(1)}, u32[]{:S(2)}) copy-start(bf16[144,256]{1,0:T(8,128)(2,1)S(1)} %collective-permute-done.19.own_2) | copy-start | bytes 221188
  84.0 16.4 %collective-permute-start.26 = (bf16[4,288,256]{2,1,0:T(8,128)(2,1)}, bf16[4,288,256]{2,1,0:T(8,128)(2,1)}, u32[]{:S(2)}, u32[]{:S(2)}) collective-permute-start(bf16[4,288,256]{2,1,0:T(8,128)(2,1)} %get-tuple-element.72.kept_b.refs_1_), channel_id=1, source_target_pairs={{0,8},{8,0},{1,9},{9,1},{2,10},{10,2},{3,11},{11,3},{4,12},{12,4},... | collective-permute-start | bytes 1769480 | tf_op jit(solution)/shard_map/ppermute | solution.py:609
  86.5 0.6 copy-start.26
  87.2 0.6 copy-start.27
  92.9 20.0 %all-to-all-start.2 = ((bf16[8,144,256]{2,1,0:T(8,128)(2,1)}), bf16[8,144,256]{2,1,0:T(8,128)(2,1)S(1)}, u32[]{:S(2)}, u32[]{:S(2)}) async-start(bf16[8,144,256]{2,1,0:T(8,128)(2,1)} %pick_partner.1), calls=%async_computation.2 | async-start | bytes 1179648 | tf_op jit(solution)/shard_map/all_to_all | solution.py:625
  112.9 0.9 copy-start.11
  113.8 19.5 %copy-start.8 = (s32[64]{0:T(128)S(1)}, s32[64]{0:T(128)}, u32[]{:S(2)}) copy-start(s32[64]{0:T(128)} %get-tuple-element.45.ids) | copy-start | bytes 772
  124.5 8.8 %copy-start.2 = (bf16[12,288,256]{2,1,0:T(8,128)(2,1)S(1)}, bf16[12,288,256]{2,1,0:T(8,128)(2,1)}, u32[]{:S(2)}) copy-start(bf16[12,288,256]{2,1,0:T(8,128)(2,1)} %get-tuple-element.71.kept_a.refs_0_) | copy-start | bytes 5308420
  124.5 2.0 %collective-permute-start.27 = (bf16[16,48,256]{2,1,0:T(8,128)(2,1)}, bf16[16,48,256]{2,1,0:T(8,128)(2,1)S(1)}, u32[]{:S(2)}, u32[]{:S(2)}) collective-permute-start(bf16[16,48,256]{2,1,0:T(8,128)(2,1)} %get-tuple-element.74), channel_id=1, source_target_pairs={{0,8},{8,0},{1,9},{9,1},{2,10},{10,2},{3,11},{11,3},{4,12},{12,4},... | collective-permute-start | bytes 1179656 | tf_op jit(solution)/shard_map/ppermute | solution.py:657
  126.6 1.1 copy-start.3
  127.7 5.6 %copy-start.6 = (bf16[128,256]{1,0:T(8,128)(2,1)S(1)}, bf16[128,256]{1,0:T(8,128)(2,1)}, u32[]{:S(2)}) copy-start(bf16[128,256]{1,0:T(8,128)(2,1)} %get-tuple-element.75.grads) | copy-start | bytes 196612
  127.7 5.6 %copy-start.9 = (bf16[16,128]{1,0:T(8,128)(2,1)S(1)}, bf16[16,128]{1,0:T(8,128)(2,1)}, u32[]{:S(2)}) copy-start(bf16[16,128]{1,0:T(8,128)(2,1)} %get-tuple-element.76.crows) | copy-start | bytes 12292
  128.5 19.3 %all-to-all-start.3 = ((bf16[16,48,256]{2,1,0:T(8,128)(2,1)}), bf16[16,48,256]{2,1,0:T(8,128)(2,1)S(1)}, u32[]{:S(2)}, u32[]{:S(2)}) async-start(bf16[16,48,256]{2,1,0:T(8,128)(2,1)} %add_core.1), calls=%async_computation.3 | async-start | bytes 786432 | tf_op jit(solution)/shard_map/all_to_all | solution.py:658
  133.3 25.4 %copy-start.10 = (f32[128]{0:T(128)S(1)}, f32[128]{0:T(128)}, u32[]{:S(2)}) copy-start(f32[128]{0:T(128)} %param.12) | copy-start | bytes 1540

commit v4 on v3

--- a/solution.py
+++ b/solution.py
@@ -21,6 +21,7 @@
 BLOCK = ROWS + 2 * EXT
 SHARE = ROWS // NSEQ
 COLS = NDP * SHARE
+MESSAGE = 2 * SHARE + EXT
 SEQLEN = NSEQ * BLK
 TB = 256
 DP = ("z", "xl", "c")
@@ -113,86 +114,53 @@
                     out[4 * h + r, :, BLK * (first + k) : BLK * (first + k + 1)] = y[BLK * k :][:BLK, BLK * r :][:, :BLK]
 
 
-def project(first_block, count, ids, hidden, sibling, *refs):
-    blocks, (out, kept, ahead, x, w, exts, sems, ahead_sems, out_sems) = refs[:count], refs[count:]
-
-    def columns(n):
-        return pl.ds(pl.multiple_of(ids[n] * ROWS, ROWS), ROWS)
-
-    arrivals, leaving = [], []
+def project(ids, hidden, sibling, *refs):
+    count = len(ORDER)
+    blocks, (out, x, w, exts, sems) = refs[:count], refs[count:]
+    arrivals = []
     for n, block in enumerate(blocks):
+        columns = pl.ds(pl.multiple_of(ids[n] * ROWS, ROWS), ROWS)
         at = slice(ROWS * n, ROWS * (n + 1))
         pairs = (
             (block.at[0:ROWS], w.at[at]),
-            (block.at[ROWS:BLOCK], exts.at[n]),
-            (hidden.at[:, columns(first_block + n)], x.at[0:BLK, at]),
-            (sibling.at[:, columns(first_block + n)], x.at[BLK : 2 * BLK, at]),
+            (block.at[ROWS : ROWS + EXT], exts.at[n]),
+            (hidden.at[:, columns], x.at[0:BLK, at]),
+            (sibling.at[:, columns], x.at[BLK : 2 * BLK, at]),
         )
         arrivals.append([pltpu.make_async_copy(a, b, sems.at[n, i]) for i, (a, b) in enumerate(pairs)])
-        leaving.append(pltpu.make_async_copy(w.at[at], kept.at[n, 0:ROWS], out_sems.at[n, 0]))
-        leaving.append(pltpu.make_async_copy(exts.at[n], kept.at[n, ROWS:BLOCK], out_sems.at[n, 1]))
-    for group in arrivals:
-        for copy in group:
+        for copy in arrivals[n]:
             copy.start()
-    handed = []
-    for n in range(LAST_STEP):
-        at = slice(ROWS * n, ROWS * (n + 1))
-        for m, source in enumerate((hidden, sibling)):
-            target = ahead.at[BLK * m : BLK * (m + 1), at]
-            handed.append(
-                pltpu.make_async_copy(source.at[:, columns(len(ORDER) - LAST_STEP + n)], target, ahead_sems.at[n, m])
-            )
-            handed[-1].start()
     acc = jnp.zeros((2 * BLK, 2 * HEAD), F32)
     wide = [jnp.zeros((BLK, BLK), F32)] * 2
-    for first in range(0, count, 4):
-        many = min(4, count - first)
-        for n in range(first, first + many):
-            for copy in arrivals[n]:
+    many = 4
+    for first in range(0, count, many):
+        for group in arrivals[first : first + many]:
+            for copy in group:
                 copy.wait()
-            leaving[2 * n].start()
-            leaving[2 * n + 1].start()
         at = slice(ROWS * first, ROWS * (first + many))
         acc += jnp.dot(x[:, at], w[at, :], preferred_element_type=F32)
         for n in range(first, first + many):
-            ext = exts[n, 0:EXT, :].astype(F32)
+            ext = exts[n].astype(F32)
             row = ext[0:1] + ext[1:2]
             for m in range(2):
                 product = x[BLK * m : BLK * (m + 1), ROWS * n : ROWS * (n + 1)].astype(F32) * row
                 wide[m] += product[:, 0:BLK] + product[:, BLK : 2 * BLK]
-    add_sums(None, acc, wide, out)
-    for copy in handed + leaving:
+    for m in range(2):
+        total = jnp.sum(wide[m].T, axis=0, keepdims=True)
+        out[m, 0:BLK, :] = acc[BLK * m : BLK * (m + 1)]
+        out[m, BLK : BLK + 8, :] = jnp.broadcast_to(jnp.concatenate([total, total], axis=1), (8, 2 * HEAD))
+
+
+def stack_blocks(*refs):
+    blocks, (out, held, sems, out_sem) = refs[: len(ORDER)], refs[len(ORDER) :]
+    copies = [pltpu.make_async_copy(block, held.at[n], sems.at[n]) for n, block in enumerate(blocks)]
+    for copy in copies:
+        copy.start()
+    for copy in copies:
         copy.wait()
-
-
-def add_sums(sums, acc, wide, out):
-    for m in range(2):
-        qk = acc[BLK * m : BLK * (m + 1)]
-        total = jnp.sum(wide[m].T, axis=0, keepdims=True)
-        ext = jnp.broadcast_to(jnp.concatenate([total, total], axis=1), (8, 2 * HEAD))
-        out[m, 0:BLK, :] = qk if sums is None else sums[m, 0:BLK, :] + qk
-        out[m, BLK : BLK + 8, :] = ext if sums is None else sums[m, BLK : BLK + 8, :] + ext
-
-
-def project_last(before, ahead, *refs):
-    blocks, (out, kept, x, sums, sems) = refs[:LAST_STEP], refs[LAST_STEP:]
-    pairs = [(block, kept.at[n]) for n, block in enumerate(blocks)] + [(ahead, x), (before, sums)]
-    copies = [pltpu.make_async_copy(a, b, sems.at[n]) for n, (a, b) in enumerate(pairs)]
-    for copy in copies:
-        copy.start()
-    for copy in copies:
-        copy.wait()
-    acc = jnp.zeros((2 * BLK, 2 * HEAD), F32)
-    wide = [jnp.zeros((BLK, BLK), F32)] * 2
-    for n in range(LAST_STEP):
-        at = slice(ROWS * n, ROWS * (n + 1))
-        acc += jnp.dot(x[:, at], kept[n, 0:ROWS, :], preferred_element_type=F32)
-        ext = kept[n, ROWS : ROWS + EXT, :].astype(F32)
-        row = ext[0:1] + ext[1:2]
-        for m in range(2):
-            product = x[BLK * m : BLK * (m + 1), at].astype(F32) * row
-            wide[m] += product[:, 0:BLK] + product[:, BLK : 2 * BLK]
-    add_sums(sums, acc, wide, out)
+    copy = pltpu.make_async_copy(held, out, out_sem.at[0])
+    copy.start()
+    copy.wait()
 
 
 def join_cores(mine, theirs, items, first):
@@ -235,10 +203,8 @@
     own_6,
     own_7,
     hidden,
-    kept_a,
-    kept_b,
-    swapped_a,
-    swapped_b,
+    kept,
+    swapped,
     keep,
     send,
     grads,
@@ -280,10 +246,8 @@
     late = [
         pltpu.make_async_copy(hidden, columns, late_sems.at[0]),
     ]
-    for n, ref in enumerate((kept_a, kept_b, swapped_a, swapped_b)):
-        first, count = PARTS[n % 2]
-        part = value_parts.at[n // 2, first : first + count]
-        late.append(pltpu.make_async_copy(ref.at[:, ROWS + EXT : BLOCK, :], part, late_sems.at[1 + n]))
+    for n, ref in enumerate((kept, swapped)):
+        late.append(pltpu.make_async_copy(ref.at[:, ROWS + EXT : BLOCK, :], value_parts.at[n], late_sems.at[1 + n]))
     for copy in late:
         copy.start()
     cacc[...] = jnp.zeros_like(cacc)
@@ -408,93 +372,87 @@
         rows = y[0 : 2 * HEAD].T
         for k in range(chunk // SHARE):
             d = n * (chunk // SHARE) + k
-            shares[(d & 1) ^ ids[CORE], d >> 1] = rows[SHARE * k : SHARE * (k + 1)]
+            for h in range(2):
+                part = rows[SHARE * k : SHARE * (k + 1), HEAD * h : HEAD * (h + 1)]
+                shares[(d & 1) ^ ids[CORE], d >> 1, SHARE * h : SHARE * (h + 1), :] = part
         wide.append(y[2 * HEAD : 2 * HEAD + 1] + y[2 * HEAD + 2 : 2 * HEAD + 3])
     row = lax.broadcasted_iota(jnp.int32, (EXT, chunk), 0)
     gs = jnp.zeros((EXT, HEAD), F32)
     ext[...] = jnp.zeros_like(ext)
     for n, u in enumerate(wide):
         high, low = halves(u)
-        ext[n : n + 1, :] = high
-        ext[4 + n : 5 + n, :] = low
+        ext[2 * n : 2 * n + 1, :] = u[:, 0:HEAD]
+        ext[2 * n + 1 : 2 * n + 2, :] = u[:, HEAD : 2 * HEAD]
         lhs = jnp.where(row == 0, high, jnp.where(row == 1, low, 0.0)).astype(BF16)
         gs += jnp.dot(lhs, value_rows[chunk * n : chunk * (n + 1), :], preferred_element_type=F32)
-    high, low = halves(gs[0:1] + gs[1:2])
-    ext[8:9, 0:HEAD] = high
-    ext[8:9, HEAD : 2 * HEAD] = low
-    high, low = halves(jnp.broadcast_to(term, (1, HEAD)))
-    ext[9:10, 0:HEAD] = high
-    ext[9:10, HEAD : 2 * HEAD] = low
+    for n, total in ((8, gs[0:1] + gs[1:2]), (10, jnp.broadcast_to(term, (1, HEAD)))):
+        high, low = halves(total)
+        ext[n : n + 1, :] = high
+        ext[n + 1 : n + 2, :] = low
     tail = ext[...]
     for m in range(NDP // 2):
-        keep[m, 0:SHARE, :] = shares[0, m]
-        keep[m, SHARE : SHARE + EXT, :] = tail
-        send[m, 0:SHARE, :] = shares[1, m].astype(BF16)
-        send[m, SHARE : SHARE + EXT, :] = tail.astype(BF16)
+        keep[m, 0 : 2 * SHARE, :] = shares[0, m]
+        keep[m, 2 * SHARE : MESSAGE, :] = tail
+        send[m, 0 : 2 * SHARE, :] = shares[1, m].astype(BF16)
+        send[m, 2 * SHARE : MESSAGE, :] = tail.astype(BF16)
 
 
 def add_core(keep, received, out, ext):
-    split_again(keep[0, SHARE : SHARE + EXT, :] + received[0, SHARE : SHARE + EXT, :].astype(F32), ext)
+    split_again(keep[0, 2 * SHARE : MESSAGE, :] + received[0, 2 * SHARE : MESSAGE, :].astype(F32), ext)
     tail = ext[...].astype(BF16)
     for m in range(NDP // 2):
-        out[m, 0:SHARE, :] = (keep[m, 0:SHARE, :] + received[m, 0:SHARE, :].astype(F32)).astype(BF16)
-        out[m, SHARE : SHARE + EXT, :] = tail
+        out[m, 0 : 2 * SHARE, :] = (keep[m, 0 : 2 * SHARE, :] + received[m, 0 : 2 * SHARE, :].astype(F32)).astype(BF16)
+        out[m, 2 * SHARE : MESSAGE, :] = tail
 
 
 def split_again(tail, ext):
-    ext[...] = jnp.zeros_like(ext)
-    high, low = halves(tail[0:4] + tail[4:8])
-    ext[0:4, :] = high
-    ext[4:8, :] = low
-    for n in (8, 9):
-        high, low = halves(tail[n : n + 1, 0:HEAD] + tail[n : n + 1, HEAD : 2 * HEAD])
-        ext[n : n + 1, 0:HEAD] = high
-        ext[n : n + 1, HEAD : 2 * HEAD] = low
+    ext[...] = tail
+    for n in (8, 10):
+        high, low = halves(tail[n : n + 1] + tail[n + 1 : n + 2])
+        ext[n : n + 1, :] = high
+        ext[n + 1 : n + 2, :] = low
 
 
 def sum_shares(received, out, ext):
     acc = received[0].astype(F32)
     for n in range(1, NDP // 2):
         acc += received[n].astype(F32)
-    split_again(acc[SHARE : SHARE + EXT], ext)
-    rows = acc[0:SHARE].astype(BF16)
+    split_again(acc[2 * SHARE : MESSAGE], ext)
+    rows = acc[0 : 2 * SHARE].astype(BF16)
     tail = ext[...].astype(BF16)
     for s in range(NSEQ):
-        out[s, 0:SHARE, :] = rows
-        out[s, SHARE : SHARE + EXT, :] = tail
+        out[s, 0 : 2 * SHARE, :] = rows
+        out[s, 2 * SHARE : MESSAGE, :] = tail
 
 
 def unpack(ids, received, score, gq, gk, gv, gs, loss):
     d = ids[GROUP]
-    sub = lax.broadcasted_iota(jnp.int32, (4, 2 * HEAD), 0)
-    lane = lax.broadcasted_iota(jnp.int32, (SHARE, 2 * HEAD), 1)
-    j = lax.broadcasted_iota(jnp.int32, (SHARE, 2 * HEAD), 0)
-    hit = lane == SHARE * (d % 8) + j
+    sub = lax.broadcasted_iota(jnp.int32, (8, HEAD), 0)
+    lane = lax.broadcasted_iota(jnp.int32, (SHARE, HEAD), 1)
+    j = lax.broadcasted_iota(jnp.int32, (SHARE, HEAD), 0)
+    hit = lane == SHARE * (d & 3) + j
     readout = jnp.zeros((1, HEAD), F32)
     for s in range(NSEQ):
         at = slice(SHARE * s, SHARE * (s + 1))
         block = received[s].astype(F32)
-        gq[at, :] = block[0:SHARE, 0:HEAD]
-        gk[at, :] = block[0:SHARE, HEAD : 2 * HEAD]
-        tail = block[SHARE : SHARE + EXT]
-        u = tail[0:4] + tail[4:8]
-        u = jnp.sum(jnp.where(sub == d // 8, u, 0.0), axis=0, keepdims=True)
+        gq[at, :] = block[0:SHARE]
+        gk[at, :] = block[SHARE : 2 * SHARE]
+        tail = block[2 * SHARE : MESSAGE]
+        u = jnp.sum(jnp.where(sub == d >> 2, tail[0:8], 0.0), axis=0, keepdims=True)
         column = jnp.sum(jnp.where(hit, u, 0.0), axis=1, keepdims=True)
         gv[at, :] = column * score[...]
-        readout += tail[8:9, 0:HEAD] + tail[8:9, HEAD : 2 * HEAD]
+        readout += tail[8:9] + tail[9:10]
         if s == 0:
-            loss[...] = tail[9:10, 0:HEAD] + tail[9:10, HEAD : 2 * HEAD]
+            loss[...] = tail[10:11] + tail[11:12]
     gs[...] = readout
 
 
-def hidden_grads(ids, grads, crows, *refs):
-    kept, out = refs[:-1], refs[-1]
+def hidden_grads(ids, grads, crows, kept, swapped, out):
     g = grads[...]
     c = crows[...].astype(F32).T.astype(BF16)
-    for part, ref in enumerate(kept):
-        first, count = PARTS[part % 2]
-        for n in range(count):
-            start = pl.multiple_of((ids[first + n] ^ (part // 2)) * ROWS, ROWS)
+    for flip, ref in enumerate((kept, swapped)):
+        for n in range(len(ORDER)):
+            start = pl.multiple_of((ids[n] ^ flip) * ROWS, ROWS)
             y = lax.dot_general(g, ref[n, 0:ROWS, :], LAST, preferred_element_type=F32)
             y += jnp.dot(c, ref[n, ROWS : ROWS + EXT, :], preferred_element_type=F32)
             out[:, pl.ds(start, ROWS)] = y.astype(BF16)
@@ -513,10 +471,6 @@
 
 
 AROUND = [(0, 0), (0, 1), (1, 0), (1, 1), (-1, 0), (-1, 1), (2, 0), (2, 1)]
-LAST_STEP = 4
-PARTS = ((0, 12), (12, LAST_STEP))
-
-
 def ring_step(found, key):
     dz, dx = key
     step, way = (1, UP) if dz < 0 else (-1, DOWN)
@@ -546,51 +500,29 @@
     down = lax.ppermute(block, "z", DOWN)
     later, _ = lax.optimization_barrier((tokens, block))
     split = call(split_columns, shape((NSEQ, BLK, COLS), BF16), (later,), name="split_columns", flops=1 << 30)
+    split, other, up, down = lax.optimization_barrier((split, other, up, down))
     found = {(0, 0): block, (0, 1): other, (-1, 0): up, (1, 0): down}
-    second = ((-1, 1), (1, 1), (-2, 0), (2, 0))
-    for key in second:
-        ring_step(found, key)
-    split, *arrived = lax.optimization_barrier((split, *[found[key] for key in second]))
-    found.update(zip(second, arrived))
     hidden_t = lax.all_to_all(split, SEQ, 0, 0, tiled=True)
     for key in ORDER:
         if key not in found:
             ring_step(found, key)
-    partial_shape = shape((2, BLK + 8, 2 * HEAD), F32)
-
-    first, count = PARTS[0]
-    partial, kept_early, ahead = call(
-        functools.partial(project, first, count),
-        (partial_shape, shape((count, BLOCK, ROWS), BF16), shape((2 * BLK, LAST_STEP * ROWS), BF16)),
-        (ids, tokens, sibling, *[found[key] for key in ORDER[first : first + count]]),
+    count = len(ORDER)
+    blocks = [found[key] for key in ORDER]
+    partial = call(
+        project,
+        shape((2, BLK + 8, 2 * HEAD), F32),
+        (ids, tokens, sibling, *blocks),
         far=range(1, 3 + count),
-        far_out=((count, BLOCK, ROWS),),
         scratch=[
             pltpu.VMEM((2 * BLK, count * ROWS), BF16),
             pltpu.VMEM((count * ROWS, ROWS), BF16),
-            pltpu.VMEM((count, 2 * EXT, ROWS), BF16),
+            pltpu.VMEM((count, EXT, ROWS), BF16),
             pltpu.SemaphoreType.DMA((count, 4)),
-            pltpu.SemaphoreType.DMA((LAST_STEP, 2)),
-            pltpu.SemaphoreType.DMA((count, 2)),
         ],
         limit=62,
         name="project",
-        flops=count << 25,
-        bytes_accessed=count << 19,
-    )
-    partial, kept_late = call(
-        project_last,
-        (partial_shape, shape((LAST_STEP, BLOCK, ROWS), BF16)),
-        (partial, ahead, *[found[key] for key in ORDER[-LAST_STEP:]]),
-        far=range(2 + LAST_STEP),
-        scratch=[
-            pltpu.VMEM((2 * BLK, LAST_STEP * ROWS), BF16),
-            pltpu.VMEM(partial_shape.shape, F32),
-            pltpu.SemaphoreType.DMA((2 + LAST_STEP,)),
-        ],
-        limit=62,
-        name="project_last",
-        flops=LAST_STEP << 25,
+        flops=1 << 29,
+        bytes_accessed=6 << 20,
     )
     theirs = lax.ppermute(partial, "c", SWAP)
     items, mine = call(
@@ -604,14 +536,29 @@
         scratch=[pltpu.VMEM((4, *item), BF16)],
         name="pick_for_planes",
     )
-    slots, hidden_t, *kept = lax.optimization_barrier((slots, hidden_t, kept_early, kept_late))
+    slots, hidden_t, *blocks = lax.optimization_barrier((slots, hidden_t, *blocks))
     arrived = lax.all_to_all(slots, "z", 0, 0, tiled=True)
-    kept += [lax.ppermute(part, "c", SWAP) for part in kept]
+    kept = call(
+        stack_blocks,
+        shape((count, BLOCK, ROWS), BF16),
+        blocks,
+        far=range(count),
+        far_out=((count, BLOCK, ROWS),),
+        scratch=[
+            pltpu.VMEM((count, BLOCK, ROWS), BF16),
+            pltpu.SemaphoreType.DMA((count,)),
+            pltpu.SemaphoreType.DMA((1,)),
+        ],
+        limit=62,
+        name="stack_blocks",
+        bytes_accessed=5 << 20,
+    )
     windows = {(0, 0): mine, (0, 1): lax.ppermute(mine, "xh", SWAP)}
     for dy in (1, -1, 2):
         for dx in (0, 1):
             windows[(dy, dx)] = lax.ppermute(windows[(0, dx)], "y", [(i, (i - dy) % 4) for i in range(4)])
-    arrived, *own = lax.optimization_barrier((arrived, *[windows[key] for key in AROUND]))
+    arrived, kept, *own = lax.optimization_barrier((arrived, kept, *[windows[key] for key in AROUND]))
+    swapped = lax.ppermute(kept, "c", SWAP)
     theirs = call(
         pick_partner,
         shape((NSEQ, *item), BF16),
@@ -624,13 +571,13 @@
     )
     mate = lax.all_to_all(theirs, SEQ, 0, 0, tiled=True)
 
-    message = (NDP // 2, SHARE + EXT, 2 * HEAD)
-    ext = pltpu.VMEM((EXT, 2 * HEAD), F32)
+    message = (NDP // 2, MESSAGE, HEAD)
+    ext = pltpu.VMEM((EXT, HEAD), F32)
     keep, send, grads, crows = call(
         attention,
         (shape(message, F32), shape(message, BF16), shape((BLK, 2 * HEAD), BF16), shape((EXT, BLK), BF16)),
-        (ids, mate, *own, hidden_t, *kept),
-        far=range(1, 15),
+        (ids, mate, *own, hidden_t, kept, swapped),
+        far=range(1, 13),
         scratch=[
             pltpu.VMEM((2, NSEQ, EXT, 2 * HEAD), BF16),
             pltpu.VMEM((HEAD, SEQLEN), BF16),
@@ -645,10 +592,10 @@
             pltpu.VMEM((NSEQ, BLK, COLS), BF16),
             pltpu.VMEM((2, len(ORDER), EXT, ROWS), BF16),
             pltpu.VMEM((COLS, HEAD), BF16),
-            pltpu.VMEM((2, NDP // 2, SHARE, 2 * HEAD), F32),
+            pltpu.VMEM((2, NDP // 2, 2 * SHARE, HEAD), F32),
             ext,
             pltpu.SemaphoreType.DMA((27,)),
-            pltpu.SemaphoreType.DMA((5,)),
+            pltpu.SemaphoreType.DMA((3,)),
         ],
         name="attention",
         limit=62,
@@ -659,7 +606,7 @@
     grad_hidden = call(
         hidden_grads,
         shape((BLK, NDP * ROWS), BF16),
-        (ids, grads, crows, *kept),
+        (ids, grads, crows, kept, swapped),
         name="hidden_grads",
         flops=1 << 29,
         bytes_accessed=6 << 20,
@@ -667,7 +614,7 @@
     arrived, grad_hidden = lax.optimization_barrier((arrived, grad_hidden))
     sums = call(
         sum_shares,
-        shape((NSEQ, SHARE + EXT, 2 * HEAD), BF16),
+        shape((NSEQ, MESSAGE, HEAD), BF16),
         (arrived,),
         scratch=[ext],
         name="sum_shares",

time: 161 us -> 154 us (0.957)
  waiting for transfers between devices: 48.8 us -> 27.5 us
  blocking collectives: 10.9 us -> 29.6 us
  starting transfers between devices: 57.4 us -> 51.2 us
  local copies, waits for them, and re-layouts: 6 us -> 8.33 us
    all_to_all x0 -> x1, blocking collectives: none -> 18.9 us  [per_device(): mate = lax.all_to_all(theirs, SEQ, 0, 0, tiled=True)]
    all_to_all x1 -> x0, waiting for transfers between devices: 12.5 us -> none  [per_device(): mate = lax.all_to_all(theirs, SEQ, 0, 0, tiled=True)]
    all_to_all x1 -> x0, starting transfers between devices: 7.46 us -> none  [per_device(): mate = lax.all_to_all(theirs, SEQ, 0, 0, tiled=True)]
    all_to_all x1, waiting for transfers between devices: 9.17 us -> 4.47 us  [per_device(): arrived = lax.all_to_all(shares, ('z', 'xl'), 0, 0, tiled=True)]
    ppermute x6, waiting for transfers between devices: 4.18 us -> 0.02 us  [per_device(): lax.ppermute(windows[0, dx], 'y', [(i, (i - dy) % 4) for i in range(4)])]
    ppermute x1, waiting for transfers between devices: 3.53 us -> 0.01 us  [per_device(): down = lax.ppermute(block, 'z', DOWN)]
    ppermute x1, waiting for transfers between devices: 0.01 us -> 2.58 us  [per_device(): up = lax.ppermute(block, 'z', UP)]
    unnamed x56 -> x66, local copies, waits for them, and re-layouts: 6 us -> 8.33 us
  transfers between devices with their start and end apart: 32 -> 30, of which waited for: 16 -> 14; matrix products, arithmetic and copies ran while one was open for 0% -> 0% of each run, Pallas kernels for 14% -> 15%
where the time goes in v4:
time: 154 us; the launch traced here: 153 us
  starting transfers between devices  51.2 us (33%)
  Pallas kernels  35.3 us (23%)
  blocking collectives  29.6 us (19%)
  waiting for transfers between devices  27.5 us (18%)
  local copies, waits for them, and re-layouts  8.33 us (5%)
    pallas_call x12, Pallas kernels, call(): pl.pallas_call(kernel, out_shape=outs, in_specs=[SM if a.dtype == jnp.int...  35.3 us
    all_to_all x1, blocking collectives, per_device(): mate = lax.all_to_all(theirs, SEQ, 0, 0, tiled=True)  18.9 us
    ppermute x12, starting transfers between devices, ring_step(): found[key] = lax.ppermute(found[dz + step, dx], 'z', way)  14.6 us
    all_to_all x1, blocking collectives, per_device(): arrived = lax.all_to_all(sums, SEQ, 0, 0, tiled=True)  10.7 us
    ppermute x12, waiting for transfers between devices, ring_step(): found[key] = lax.ppermute(found[dz + step, dx], 'z', way)  10.1 us
    ppermute x6, starting transfers between devices, per_device(): lax.ppermute(windows[0, dx], 'y', [(i, (i - dy) % 4) for i in range(4)])  9.91 us
    unnamed x66, local copies, waits for them, and re-layouts  8.33 us
    all_to_all x1, starting transfers between devices, per_device(): hidden_t = lax.all_to_all(split, SEQ, 0, 0, tiled=True)  6.04 us
  transfers between devices with their start and end apart: 30, of which 14 were waited for; matrix products, arithmetic and copies ran while one was open for 0% of the time, Pallas kernels for 15%

profile of v4, /device:TPU:2, one launch (start us, length us, event | category | flops | bytes accessed | tf_op | source)
XLA Modules:
  0.0 153.4 jit_solution(14566577500562056111)
XLA Ops:
  0.6 0.1 collective-permute-start
  0.7 0.6 pad_add_fusion.pos
  1.3 2.5 %pack_weights.1 = (bf16[288,256]{1,0:T(8,128)(2,1)}, s32[64]{0:T(128)}) custom-call(s32[4]{0:T(128)} %pad_add_fusion.pos, s32[32]{0:T(128)} %lengths.1, s32[32]{0:T(128)} %labels.1, s32[32]{0:T(128)} %partner.1, bf16[256,128]{1,0:T(8,128)(2,1)} %wq.1, bf16[256,128]{1,0:T(8,128)(2,1)} %wk.1, bf16[256,128]{1,0:T(8,128)(2,1)} %wv.1, f32[1,128]{1,0:T(1,128)} %bitcast.13), custom_call_target="tpu_custom_call" | custom-call | tf_op jit(solution)/shard_map/pack_weights/pallas_call | solution.py:37
  3.8 5.9 %collective-permute-start.3 = (bf16[288,256]{1,0:T(8,128)(2,1)}, bf16[288,256]{1,0:T(8,128)(2,1)S(1)}, u32[]{:S(2)}, u32[]{:S(2)}) collective-permute-start(bf16[288,256]{1,0:T(8,128)(2,1)} %get-tuple-element.63.refs_0_), channel_id=1, source_target_pairs={{0,224},{32,0},{64,32},{96,64},{128,96},{160,128},{192,160},{224,1... | collective-permute-start | bytes 442376 | tf_op jit(solution)/shard_map/ppermute | solution.py:500
  9.7 0.5 collective-permute-start.1
  10.3 1.6 %copy-done.1 = bf16[1,128,8192]{2,1,0:T(8,128)(2,1)S(1)} copy-done((bf16[1,128,8192]{2,1,0:T(8,128)(2,1)S(1)}, bf16[1,128,8192]{2,1,0:T(8,128)(2,1)}, u32[]{:S(2)}) %copy-start.1) | copy-done | bytes 2097176
  11.9 2.7 %split_columns.1 = bf16[8,128,1024]{2,1,0:T(8,128)(2,1)} custom-call(bf16[128,8192]{1,0:T(8,128)(2,1)S(1)} %bitcast.12), custom_call_target="tpu_custom_call" | custom-call | flops 1073741824 | tf_op jit(solution)/shard_map/split_columns/pallas_call | solution.py:37
  14.5 2.6 %collective-permute-done.2.refs_2_ = bf16[288,256]{1,0:T(8,128)(2,1)S(1)} collective-permute-done((bf16[288,256]{1,0:T(8,128)(2,1)}, bf16[288,256]{1,0:T(8,128)(2,1)S(1)}, u32[]{:S(2)}, u32[]{:S(2)}) %collective-permute-start.2) | collective-permute-done | bytes 147488 | tf_op jit(solution)/shard_map/ppermute | solution.py:499
  17.1 6.0 %all-to-all-start = ((bf16[8,128,1024]{2,1,0:T(8,128)(2,1)}), bf16[8,128,1024]{2,1,0:T(8,128)(2,1)}, u32[]{:S(2)}, u32[]{:S(2)}) async-start(bf16[8,128,1024]{2,1,0:T(8,128)(2,1)} %split_columns.1), calls=%async_computation | async-start | bytes 4194304 | tf_op jit(solution)/shard_map/all_to_all | solution.py:505
  23.2 1.7 %collective-permute-start.5 = (bf16[288,256]{1,0:T(8,128)(2,1)S(1)}, bf16[288,256]{1,0:T(8,128)(2,1)S(1)}, u32[]{:S(2)}, u32[]{:S(2)}) collective-permute-start(bf16[288,256]{1,0:T(8,128)(2,1)S(1)} %collective-permute-done.1.refs_1_), channel_id=1, source_target_pairs={{0,224},{32,0},{64,32},{96,64},{128,96},{160,128},{192,160},{224,1... | collective-permute-start | bytes 442376 | tf_op jit(solution)/shard_map/ppermute | solution.py:477
  24.9 0.3 collective-permute-start.6
  25.2 0.1 collective-permute-start.4
  25.3 3.0 %collective-permute-done.5.refs_5_ = bf16[288,256]{1,0:T(8,128)(2,1)S(1)} collective-permute-done((bf16[288,256]{1,0:T(8,128)(2,1)S(1)}, bf16[288,256]{1,0:T(8,128)(2,1)S(1)}, u32[]{:S(2)}, u32[]{:S(2)}) %collective-permute-start.5) | collective-permute-done | bytes 147488 | tf_op jit(solution)/shard_map/ppermute | solution.py:477
  28.3 2.9 %collective-permute-start.9 = (bf16[288,256]{1,0:T(8,128)(2,1)S(1)}, bf16[288,256]{1,0:T(8,128)(2,1)S(1)}, u32[]{:S(2)}, u32[]{:S(2)}) collective-permute-start(bf16[288,256]{1,0:T(8,128)(2,1)S(1)} %collective-permute-done.5.refs_5_), channel_id=1, source_target_pairs={{0,224},{32,0},{64,32},{96,64},{128,96},{160,128},{192,160},{224,1... | collective-permute-start | bytes 442376 | tf_op jit(solution)/shard_map/ppermute | solution.py:477
  31.2 0.1 collective-permute-start.7
  31.3 0.6 collective-permute-done.6.refs_6_
  31.9 1.3 collective-permute-start.10
  33.3 0.9 collective-permute-done.4.refs_4_
  34.2 0.6 collective-permute-done.9.refs_9_
  34.7 2.9 %collective-permute-start.13 = (bf16[288,256]{1,0:T(8,128)(2,1)S(1)}, bf16[288,256]{1,0:T(8,128)(2,1)S(1)}, u32[]{:S(2)}, u32[]{:S(2)}) collective-permute-start(bf16[288,256]{1,0:T(8,128)(2,1)S(1)} %collective-permute-done.9.refs_9_), channel_id=1, source_target_pairs={{0,224},{32,0},{64,32},{96,64},{128,96},{160,128},{192,160},{224,1... | collective-permute-start | bytes 442376 | tf_op jit(solution)/shard_map/ppermute | solution.py:477
  37.6 0.4 collective-permute-done.7.refs_7_
  38.0 2.0 %collective-permute-start.11 = (bf16[288,256]{1,0:T(8,128)(2,1)S(1)}, bf16[288,256]{1,0:T(8,128)(2,1)S(1)}, u32[]{:S(2)}, u32[]{:S(2)}) collective-permute-start(bf16[288,256]{1,0:T(8,128)(2,1)S(1)} %collective-permute-done.7.refs_7_), channel_id=1, source_target_pairs={{0,224},{32,0},{64,32},{96,64},{128,96},{160,128},{192,160},{224,1... | collective-permute-start | bytes 442376 | tf_op jit(solution)/shard_map/ppermute | solution.py:477
  40.0 1.5 collective-permute-done.8.refs_8_
  41.5 3.2 %collective-permute-start.15 = (bf16[288,256]{1,0:T(8,128)(2,1)S(1)}, bf16[288,256]{1,0:T(8,128)(2,1)S(1)}, u32[]{:S(2)}, u32[]{:S(2)}) collective-permute-start(bf16[288,256]{1,0:T(8,128)(2,1)S(1)} %collective-permute-done.13.refs_13_), channel_id=1, source_target_pairs={{0,224},{32,0},{64,32},{96,64},{128,96},{160,128},{192,160},{224,1... | collective-permute-start | bytes 442376 | tf_op jit(solution)/shard_map/ppermute | solution.py:477
  44.7 1.6 %collective-permute-done.14.refs_14_ = bf16[288,256]{1,0:T(8,128)(2,1)S(1)} collective-permute-done((bf16[288,256]{1,0:T(8,128)(2,1)S(1)}, bf16[288,256]{1,0:T(8,128)(2,1)S(1)}, u32[]{:S(2)}, u32[]{:S(2)}) %collective-permute-start.14) | collective-permute-done | bytes 147488 | tf_op jit(solution)/shard_map/ppermute | solution.py:477
  46.4 1.6 %collective-permute-done.12.refs_12_ = bf16[288,256]{1,0:T(8,128)(2,1)S(1)} collective-permute-done((bf16[288,256]{1,0:T(8,128)(2,1)S(1)}, bf16[288,256]{1,0:T(8,128)(2,1)S(1)}, u32[]{:S(2)}, u32[]{:S(2)}) %collective-permute-start.12) | collective-permute-done | bytes 147488 | tf_op jit(solution)/shard_map/ppermute | solution.py:477
  48.1 0.6 copy-done.24
  48.6 0.1 copy-done.25
  48.7 5.2 %project.1.mine = f32[2,136,256]{2,1,0:T(8,128)} custom-call(s32[64]{0:T(128)} %get-tuple-element.54.ids, bf16[128,8192]{1,0:T(8,128)(2,1)} %bitcast.11, bf16[128,8192]{1,0:T(8,128)(2,1)} %collective-permute-done.sibling, bf16[288,256]{1,0:T(8,128)(2,1)} %get-tuple-element.63.refs_0_, bf16[288,256]{1,0:T(8,128)(2,1)} %copy-done.13, ...), custom_call_target="tpu_custom_call" | custom-call | flops 536870912 | bytes 6291456 | tf_op jit(solution)/shard_map/project/pallas_call | solution.py:37
  53.9 0.1 collective-permute-start.16
  54.0 1.8 %collective-permute-done.16.theirs = f32[2,136,256]{2,1,0:T(8,128)S(1)} collective-permute-done((f32[2,136,256]{2,1,0:T(8,128)}, f32[2,136,256]{2,1,0:T(8,128)S(1)}, u32[]{:S(2)}, u32[]{:S(2)}) %collective-permute-start.16) | collective-permute-done | bytes 278560 | tf_op jit(solution)/shard_map/ppermute | solution.py:527
  55.7 1.0 copy-done.2
  56.7 0.0 copy-start.4
  56.8 1.6 %collective-permute-start.17 = (bf16[2,144,256]{2,1,0:T(8,128)(2,1)S(1)}, bf16[2,144,256]{2,1,0:T(8,128)(2,1)S(1)}, u32[]{:S(2)}, u32[]{:S(2)}) collective-permute-start(bf16[2,144,256]{2,1,0:T(8,128)(2,1)S(1)} %get-tuple-element.60.near), channel_id=1, source_target_pairs={{0,16},{16,0},{1,17},{17,1},{2,18},{18,2},{3,19},{19,3},{4,20},{20... | collective-permute-start | bytes 442376 | tf_op jit(solution)/shard_map/ppermute | solution.py:531
  58.4 4.4 %collective-permute-done.17.side = bf16[2,144,256]{2,1,0:T(8,128)(2,1)S(1)} collective-permute-done((bf16[2,144,256]{2,1,0:T(8,128)(2,1)S(1)}, bf16[2,144,256]{2,1,0:T(8,128)(2,1)S(1)}, u32[]{:S(2)}, u32[]{:S(2)}) %collective-permute-start.17) | collective-permute-done | bytes 147488 | tf_op jit(solution)/shard_map/ppermute | solution.py:531
  62.7 1.4 pick_for_planes.1
  64.1 4.3 %all-to-all-start.1 = ((bf16[8,144,256]{2,1,0:T(8,128)(2,1)}), bf16[8,144,256]{2,1,0:T(8,128)(2,1)S(1)}, u32[]{:S(2)}, u32[]{:S(2)}) async-start(bf16[8,144,256]{2,1,0:T(8,128)(2,1)} %pick_for_planes.1), calls=%async_computation.1 | async-start | bytes 1179648 | tf_op jit(solution)/shard_map/all_to_all | solution.py:540
  68.5 2.8 %collective-permute-start.18 = (bf16[144,256]{1,0:T(8,128)(2,1)S(1)}, bf16[144,256]{1,0:T(8,128)(2,1)S(1)}, u32[]{:S(2)}, u32[]{:S(2)}) collective-permute-start(bf16[144,256]{1,0:T(8,128)(2,1)S(1)} %get-tuple-element.81.own_0), channel_id=1, source_target_pairs={{0,1},{1,0},{2,3},{3,2},{4,5},{5,4},{6,7},{7,6},{8,9},{9,8},{10,11... | collective-permute-start | bytes 221192 | tf_op jit(solution)/shard_map/ppermute | solution.py:556
  71.3 3.0 %collective-permute-start.23 = (bf16[144,256]{1,0:T(8,128)(2,1)S(1)}, bf16[144,256]{1,0:T(8,128)(2,1)S(1)}, u32[]{:S(2)}, u32[]{:S(2)}) collective-permute-start(bf16[144,256]{1,0:T(8,128)(2,1)S(1)} %get-tuple-element.81.own_0), channel_id=1, source_target_pairs={{0,4},{2,6},{4,0},{6,2},{1,5},{3,7},{5,1},{7,3},{8,12},{10,14},{12... | collective-permute-start | bytes 221192 | tf_op jit(solution)/shard_map/ppermute | solution.py:559
  74.2 0.6 collective-permute-start.21
  74.8 2.7 %collective-permute-start.19 = (bf16[144,256]{1,0:T(8,128)(2,1)S(1)}, bf16[144,256]{1,0:T(8,128)(2,1)S(1)}, u32[]{:S(2)}, u32[]{:S(2)}) collective-permute-start(bf16[144,256]{1,0:T(8,128)(2,1)S(1)} %get-tuple-element.81.own_0), channel_id=1, source_target_pairs={{0,6},{2,0},{4,2},{6,4},{1,7},{3,1},{5,3},{7,5},{8,14},{10,8},{12,... | collective-permute-start | bytes 221192 | tf_op jit(solution)/shard_map/ppermute | solution.py:559
  77.5 0.5 collective-permute-start.24
  77.9 0.5 collective-permute-start.22
  78.4 2.8 %collective-permute-start.20 = (bf16[144,256]{1,0:T(8,128)(2,1)S(1)}, bf16[144,256]{1,0:T(8,128)(2,1)S(1)}, u32[]{:S(2)}, u32[]{:S(2)}) collective-permute-start(bf16[144,256]{1,0:T(8,128)(2,1)S(1)} %collective-permute-done.18.own_1), channel_id=1, source_target_pairs={{0,6},{2,0},{4,2},{6,4},{1,7},{3,1},{5,3},{7,5},{8,14},{10,8},{12,... | collective-permute-start | bytes 221192 | tf_op jit(solution)/shard_map/ppermute | solution.py:559
  81.2 3.3 %stack_blocks.1.kept = bf16[16,288,256]{2,1,0:T(8,128)(2,1)} custom-call(bf16[288,256]{1,0:T(8,128)(2,1)} %get-tuple-element.63.refs_0_, bf16[288,256]{1,0:T(8,128)(2,1)} %copy-done.13, bf16[288,256]{1,0:T(8,128)(2,1)} %copy-done.12, bf16[288,256]{1,0:T(8,128)(2,1)} %copy-done.11, bf16[288,256]{1,0:T(8,128)(2,1)} %copy-done.16, bf16[288,256]{1,0:T(8,128)(2,1)} %copy-done.14, ...), custom_call_target="tpu_custom_call" | custom-call | bytes 5242880 | tf_op jit(solution)/shard_map/stack_blocks/pallas_call | solution.py:37
  84.5 0.0 copy-start.29
  84.6 2.3 %all-to-all-done.1.received = bf16[8,144,256]{2,1,0:T(8,128)(2,1)S(1)} async-done(((bf16[8,144,256]{2,1,0:T(8,128)(2,1)}), bf16[8,144,256]{2,1,0:T(8,128)(2,1)S(1)}, u32[]{:S(2)}, u32[]{:S(2)}) %all-to-all-start.1) | async-done | bytes 589856 | tf_op jit(solution)/shard_map/all_to_all | solution.py:540
  86.9 0.8 copy-done.10
  87.7 2.5 %pick_partner.1 = bf16[8,144,256]{2,1,0:T(8,128)(2,1)} custom-call(s32[64]{0:T(128)} %get-tuple-element.54.ids, bf16[8,144,256]{2,1,0:T(8,128)(2,1)} %copy-done.10), custom_call_target="tpu_custom_call" | custom-call | tf_op jit(solution)/shard_map/pick_partner/pallas_call | solution.py:37
  90.2 18.9 %all_to_all.25.mate = bf16[8,144,256]{2,1,0:T(8,128)(2,1)} all-to-all(bf16[8,144,256]{2,1,0:T(8,128)(2,1)} %pick_partner.1), channel_id=1, replica_groups=mesh['z'=8,'xl'=2,'c'=2,'y'=4,'xh'=2] {'y','xh'}, dimensions={0} | all-to-all | bytes 1179648 | tf_op jit(solution)/shard_map/all_to_all | solution.py:572
  109.1 10.4 %attention.1 = (f32[16,80,128]{2,1,0:T(8,128)}, bf16[16,80,128]{2,1,0:T(8,128)(2,1)}, bf16[128,256]{1,0:T(8,128)(2,1)}, bf16[16,128]{1,0:T(8,128)(2,1)}) custom-call(s32[64]{0:T(128)} %get-tuple-element.54.ids, bf16[8,144,256]{2,1,0:T(8,128)(2,1)} %all_to_all.25.mate, bf16[144,256]{1,0:T(8,128)(2,1)} %copy-done.4, bf16[144,256]{1,0:T(8,128)(2,1)} %copy-done.26, ...), custom_call_target="tpu_custom_call" | custom-call | flops 2147483648 | tf_op jit(solution)/shard_map/attention/pallas_call | solution.py:37
  119.5 0.1 collective-permute-start.26
  119.6 1.8 %collective-permute-done.26.received = bf16[16,80,128]{2,1,0:T(8,128)(2,1)S(1)} collective-permute-done((bf16[16,80,128]{2,1,0:T(8,128)(2,1)}, bf16[16,80,128]{2,1,0:T(8,128)(2,1)S(1)}, u32[]{:S(2)}, u32[]{:S(2)}) %collective-permute-start.26) | collective-permute-done | bytes 327712 | tf_op jit(solution)/shard_map/ppermute | solution.py:604
  121.5 1.1 copy-done.3
  122.5 0.8 add_core.1
  123.3 5.1 %all-to-all-start.3 = ((bf16[16,80,128]{2,1,0:T(8,128)(2,1)}), bf16[16,80,128]{2,1,0:T(8,128)(2,1)S(1)}, u32[]{:S(2)}, u32[]{:S(2)}) async-start(bf16[16,80,128]{2,1,0:T(8,128)(2,1)} %add_core.1), calls=%async_computation.3 | async-start | bytes 655360 | tf_op jit(solution)/shard_map/all_to_all | solution.py:605
  128.5 1.7 %copy-done = bf16[16,288,256]{2,1,0:T(8,128)(2,1)S(1)} copy-done((bf16[16,288,256]{2,1,0:T(8,128)(2,1)S(1)}, bf16[16,288,256]{2,1,0:T(8,128)(2,1)}, u32[]{:S(2)}) %copy-start) | copy-done | bytes 2359320
  130.1 0.8 copy-done.5
  131.0 0.7 copy-done.8
  131.7 5.2 %hidden_grads.1 = bf16[128,8192]{1,0:T(8,128)(2,1)} custom-call(s32[64]{0:T(128)S(1)} %copy-done.7, bf16[128,256]{1,0:T(8,128)(2,1)S(1)} %copy-done.5, bf16[16,128]{1,0:T(8,128)(2,1)S(1)} %copy-done.8, bf16[16,288,256]{2,1,0:T(8,128)(2,1)S(1)} %copy-done, bf16[16,288,256]{2,1,0:T(8,128)(2,1)} %collective-permute-done.25.swapped), custom_call_target="tpu_custom_call" | custom-call | flops 536870912 | bytes 6291456 | tf_op jit(solution)/shard_map/hidden_grads/pallas_call | solution.py:37
  136.8 4.5 %all-to-all-done.3.received = bf16[16,80,128]{2,1,0:T(8,128)(2,1)S(1)} async-done(((bf16[16,80,128]{2,1,0:T(8,128)(2,1)}), bf16[16,80,128]{2,1,0:T(8,128)(2,1)S(1)}, u32[]{:S(2)}, u32[]{:S(2)}) %all-to-all-start.3) | async-done | bytes 327712 | tf_op jit(solution)/shard_map/all_to_all | solution.py:605
  141.3 0.1 sum_shares.1
  141.4 10.7 %all_to_all.26.received = bf16[8,80,128]{2,1,0:T(8,128)(2,1)S(1)} all-to-all(bf16[8,80,128]{2,1,0:T(8,128)(2,1)S(1)} %sum_shares.1), channel_id=1, replica_groups=mesh['z'=8,'xl'=2,'c'=2,'y'=4,'xh'=2] {'y','xh'}, dimensions={0} | all-to-all | bytes 327680 | tf_op jit(solution)/shard_map/all_to_all | solution.py:622
  152.1 1.3 unpack.1
  (77 shorter events, 0.2 us)
Async XLA Ops:
  0.6 47.3 %collective-permute-start = (bf16[128,8192]{1,0:T(8,128)(2,1)}, bf16[128,8192]{1,0:T(8,128)(2,1)}, u32[]{:S(2)}, u32[]{:S(2)}) collective-permute-start(bf16[128,8192]{1,0:T(8,128)(2,1)} %bitcast.10), channel_id=1, source_target_pairs={{0,8},{8,0},{1,9},{9,1},{2,10},{10,2},{3,11},{11,3},{4,12},{12,4},... | collective-permute-start | bytes 6291464 | tf_op jit(solution)/shard_map/ppermute | solution.py:498
  3.8 10.7 %collective-permute-start.3 = (bf16[288,256]{1,0:T(8,128)(2,1)}, bf16[288,256]{1,0:T(8,128)(2,1)S(1)}, u32[]{:S(2)}, u32[]{:S(2)}) collective-permute-start(bf16[288,256]{1,0:T(8,128)(2,1)} %get-tuple-element.63.refs_0_), channel_id=1, source_target_pairs={{0,224},{32,0},{64,32},{96,64},{128,96},{160,128},{192,160},{224,1... | collective-permute-start | bytes 442376 | tf_op jit(solution)/shard_map/ppermute | solution.py:500
  9.7 7.4 %collective-permute-start.2 = (bf16[288,256]{1,0:T(8,128)(2,1)}, bf16[288,256]{1,0:T(8,128)(2,1)S(1)}, u32[]{:S(2)}, u32[]{:S(2)}) collective-permute-start(bf16[288,256]{1,0:T(8,128)(2,1)} %get-tuple-element.63.refs_0_), channel_id=1, source_target_pairs={{0,32},{32,64},{64,96},{96,128},{128,160},{160,192},{192,224},{224... | collective-permute-start | bytes 442376 | tf_op jit(solution)/shard_map/ppermute | solution.py:499
  9.7 7.4 %collective-permute-start.1 = (bf16[288,256]{1,0:T(8,128)(2,1)}, bf16[288,256]{1,0:T(8,128)(2,1)S(1)}, u32[]{:S(2)}, u32[]{:S(2)}) collective-permute-start(bf16[288,256]{1,0:T(8,128)(2,1)} %get-tuple-element.63.refs_0_), channel_id=1, source_target_pairs={{0,16},{16,0},{1,17},{17,1},{2,18},{18,2},{3,19},{19,3},{4,20},{20... | collective-permute-start | bytes 442376 | tf_op jit(solution)/shard_map/ppermute | solution.py:497
  10.3 1.6 %copy-start.1 = (bf16[1,128,8192]{2,1,0:T(8,128)(2,1)S(1)}, bf16[1,128,8192]{2,1,0:T(8,128)(2,1)}, u32[]{:S(2)}) copy-start(bf16[1,128,8192]{2,1,0:T(8,128)(2,1)} %param.8) | copy-start | bytes 6291460
  14.5 16.7 %copy-start.11 = (bf16[288,256]{1,0:T(8,128)(2,1)}, bf16[288,256]{1,0:T(8,128)(2,1)S(1)}, u32[]{:S(2)}) copy-start(bf16[288,256]{1,0:T(8,128)(2,1)S(1)} %collective-permute-done.3.refs_3_) | copy-start | bytes 442372
  17.1 7.8 %copy-start.12 = (bf16[288,256]{1,0:T(8,128)(2,1)}, bf16[288,256]{1,0:T(8,128)(2,1)S(1)}, u32[]{:S(2)}) copy-start(bf16[288,256]{1,0:T(8,128)(2,1)S(1)} %collective-permute-done.2.refs_2_) | copy-start | bytes 442372
  17.1 8.1 %copy-start.13 = (bf16[288,256]{1,0:T(8,128)(2,1)}, bf16[288,256]{1,0:T(8,128)(2,1)S(1)}, u32[]{:S(2)}) copy-start(bf16[288,256]{1,0:T(8,128)(2,1)S(1)} %collective-permute-done.1.refs_1_) | copy-start | bytes 442372
  17.1 47.0 %all-to-all-start = ((bf16[8,128,1024]{2,1,0:T(8,128)(2,1)}), bf16[8,128,1024]{2,1,0:T(8,128)(2,1)}, u32[]{:S(2)}, u32[]{:S(2)}) async-start(bf16[8,128,1024]{2,1,0:T(8,128)(2,1)} %split_columns.1), calls=%async_computation | async-start | bytes 4194304 | tf_op jit(solution)/shard_map/all_to_all | solution.py:505
  23.2 5.1 %collective-permute-start.5 = (bf16[288,256]{1,0:T(8,128)(2,1)S(1)}, bf16[288,256]{1,0:T(8,128)(2,1)S(1)}, u32[]{:S(2)}, u32[]{:S(2)}) collective-permute-start(bf16[288,256]{1,0:T(8,128)(2,1)S(1)} %collective-permute-done.1.refs_1_), channel_id=1, source_target_pairs={{0,224},{32,0},{64,32},{96,64},{128,96},{160,128},{192,160},{224,1... | collective-permute-start | bytes 442376 | tf_op jit(solution)/shard_map/ppermute | solution.py:477
  24.9 7.0 %collective-permute-start.6 = (bf16[288,256]{1,0:T(8,128)(2,1)S(1)}, bf16[288,256]{1,0:T(8,128)(2,1)S(1)}, u32[]{:S(2)}, u32[]{:S(2)}) collective-permute-start(bf16[288,256]{1,0:T(8,128)(2,1)S(1)} %collective-permute-done.2.refs_2_), channel_id=1, source_target_pairs={{0,32},{32,64},{64,96},{96,128},{128,160},{160,192},{192,224},{224... | collective-permute-start | bytes 442376 | tf_op jit(solution)/shard_map/ppermute | solution.py:477
  25.2 9.0 %collective-permute-start.4 = (bf16[288,256]{1,0:T(8,128)(2,1)S(1)}, bf16[288,256]{1,0:T(8,128)(2,1)S(1)}, u32[]{:S(2)}, u32[]{:S(2)}) collective-permute-start(bf16[288,256]{1,0:T(8,128)(2,1)S(1)} %collective-permute-done.1.refs_1_), channel_id=1, source_target_pairs={{0,32},{32,64},{64,96},{96,128},{128,160},{160,192},{192,224},{224... | collective-permute-start | bytes 442376 | tf_op jit(solution)/shard_map/ppermute | solution.py:477
  28.3 19.7 %copy-start.14 = (bf16[288,256]{1,0:T(8,128)(2,1)}, bf16[288,256]{1,0:T(8,128)(2,1)S(1)}, u32[]{:S(2)}) copy-start(bf16[288,256]{1,0:T(8,128)(2,1)S(1)} %collective-permute-done.5.refs_5_) | copy-start | bytes 442372
  28.3 6.4 %collective-permute-start.9 = (bf16[288,256]{1,0:T(8,128)(2,1)S(1)}, bf16[288,256]{1,0:T(8,128)(2,1)S(1)}, u32[]{:S(2)}, u32[]{:S(2)}) collective-permute-start(bf16[288,256]{1,0:T(8,128)(2,1)S(1)} %collective-permute-done.5.refs_5_), channel_id=1, source_target_pairs={{0,224},{32,0},{64,32},{96,64},{128,96},{160,128},{192,160},{224,1... | collective-permute-start | bytes 442376 | tf_op jit(solution)/shard_map/ppermute | solution.py:477
  31.2 6.7 %collective-permute-start.7 = (bf16[288,256]{1,0:T(8,128)(2,1)S(1)}, bf16[288,256]{1,0:T(8,128)(2,1)S(1)}, u32[]{:S(2)}, u32[]{:S(2)}) collective-permute-start(bf16[288,256]{1,0:T(8,128)(2,1)S(1)} %collective-permute-done.3.refs_3_), channel_id=1, source_target_pairs={{0,224},{32,0},{64,32},{96,64},{128,96},{160,128},{192,160},{224,1... | collective-permute-start | bytes 442376 | tf_op jit(solution)/shard_map/ppermute | solution.py:477
  31.9 16.0 %copy-start.15 = (bf16[288,256]{1,0:T(8,128)(2,1)}, bf16[288,256]{1,0:T(8,128)(2,1)S(1)}, u32[]{:S(2)}) copy-start(bf16[288,256]{1,0:T(8,128)(2,1)S(1)} %collective-permute-done.6.refs_6_) | copy-start | bytes 442372
  31.9 8.1 %collective-permute-start.10 = (bf16[288,256]{1,0:T(8,128)(2,1)S(1)}, bf16[288,256]{1,0:T(8,128)(2,1)S(1)}, u32[]{:S(2)}, u32[]{:S(2)}) collective-permute-start(bf16[288,256]{1,0:T(8,128)(2,1)S(1)} %collective-permute-done.6.refs_6_), channel_id=1, source_target_pairs={{0,32},{32,64},{64,96},{96,128},{128,160},{160,192},{192,224},{224... | collective-permute-start | bytes 442376 | tf_op jit(solution)/shard_map/ppermute | solution.py:477
  34.2 13.8 %copy-start.16 = (bf16[288,256]{1,0:T(8,128)(2,1)}, bf16[288,256]{1,0:T(8,128)(2,1)S(1)}, u32[]{:S(2)}) copy-start(bf16[288,256]{1,0:T(8,128)(2,1)S(1)} %collective-permute-done.4.refs_4_) | copy-start | bytes 442372
  34.2 7.3 %collective-permute-start.8 = (bf16[288,256]{1,0:T(8,128)(2,1)S(1)}, bf16[288,256]{1,0:T(8,128)(2,1)S(1)}, u32[]{:S(2)}, u32[]{:S(2)}) collective-permute-start(bf16[288,256]{1,0:T(8,128)(2,1)S(1)} %collective-permute-done.4.refs_4_), channel_id=1, source_target_pairs={{0,32},{32,64},{64,96},{96,128},{128,160},{160,192},{192,224},{224... | collective-permute-start | bytes 442376 | tf_op jit(solution)/shard_map/ppermute | solution.py:477
  34.7 13.3 %copy-start.17 = (bf16[288,256]{1,0:T(8,128)(2,1)}, bf16[288,256]{1,0:T(8,128)(2,1)S(1)}, u32[]{:S(2)}) copy-start(bf16[288,256]{1,0:T(8,128)(2,1)S(1)} %collective-permute-done.9.refs_9_) | copy-start | bytes 442372
  34.7 6.7 %collective-permute-start.13 = (bf16[288,256]{1,0:T(8,128)(2,1)S(1)}, bf16[288,256]{1,0:T(8,128)(2,1)S(1)}, u32[]{:S(2)}, u32[]{:S(2)}) collective-permute-start(bf16[288,256]{1,0:T(8,128)(2,1)S(1)} %collective-permute-done.9.refs_9_), channel_id=1, source_target_pairs={{0,224},{32,0},{64,32},{96,64},{128,96},{160,128},{192,160},{224,1... | collective-permute-start | bytes 442376 | tf_op jit(solution)/shard_map/ppermute | solution.py:477
  38.0 10.0 %copy-start.18 = (bf16[288,256]{1,0:T(8,128)(2,1)}, bf16[288,256]{1,0:T(8,128)(2,1)S(1)}, u32[]{:S(2)}) copy-start(bf16[288,256]{1,0:T(8,128)(2,1)S(1)} %collective-permute-done.7.refs_7_) | copy-start | bytes 442372
  38.0 6.8 %collective-permute-start.11 = (bf16[288,256]{1,0:T(8,128)(2,1)S(1)}, bf16[288,256]{1,0:T(8,128)(2,1)S(1)}, u32[]{:S(2)}, u32[]{:S(2)}) collective-permute-start(bf16[288,256]{1,0:T(8,128)(2,1)S(1)} %collective-permute-done.7.refs_7_), channel_id=1, source_target_pairs={{0,224},{32,0},{64,32},{96,64},{128,96},{160,128},{192,160},{224,1... | collective-permute-start | bytes 442376 | tf_op jit(solution)/shard_map/ppermute | solution.py:477
  40.0 8.0 %copy-start.19 = (bf16[288,256]{1,0:T(8,128)(2,1)}, bf16[288,256]{1,0:T(8,128)(2,1)S(1)}, u32[]{:S(2)}) copy-start(bf16[288,256]{1,0:T(8,128)(2,1)S(1)} %collective-permute-done.10.refs_10_) | copy-start | bytes 442372
  40.0 6.4 %collective-permute-start.14 = (bf16[288,256]{1,0:T(8,128)(2,1)S(1)}, bf16[288,256]{1,0:T(8,128)(2,1)S(1)}, u32[]{:S(2)}, u32[]{:S(2)}) collective-permute-start(bf16[288,256]{1,0:T(8,128)(2,1)S(1)} %collective-permute-done.10.refs_10_), channel_id=1, source_target_pairs={{0,32},{32,64},{64,96},{96,128},{128,160},{160,192},{192,224},{224... | collective-permute-start | bytes 442376 | tf_op jit(solution)/shard_map/ppermute | solution.py:477
  41.5 6.5 %copy-start.20 = (bf16[288,256]{1,0:T(8,128)(2,1)}, bf16[288,256]{1,0:T(8,128)(2,1)S(1)}, u32[]{:S(2)}) copy-start(bf16[288,256]{1,0:T(8,128)(2,1)S(1)} %collective-permute-done.8.refs_8_) | copy-start | bytes 442372
  41.5 6.5 %collective-permute-start.12 = (bf16[288,256]{1,0:T(8,128)(2,1)S(1)}, bf16[288,256]{1,0:T(8,128)(2,1)S(1)}, u32[]{:S(2)}, u32[]{:S(2)}) collective-permute-start(bf16[288,256]{1,0:T(8,128)(2,1)S(1)} %collective-permute-done.8.refs_8_), channel_id=1, source_target_pairs={{0,32},{32,64},{64,96},{96,128},{128,160},{160,192},{192,224},{224... | collective-permute-start | bytes 442376 | tf_op jit(solution)/shard_map/ppermute | solution.py:477
  41.5 6.5 %copy-start.21 = (bf16[288,256]{1,0:T(8,128)(2,1)}, bf16[288,256]{1,0:T(8,128)(2,1)S(1)}, u32[]{:S(2)}) copy-start(bf16[288,256]{1,0:T(8,128)(2,1)S(1)} %collective-permute-done.13.refs_13_) | copy-start | bytes 442372
  41.5 6.5 %collective-permute-start.15 = (bf16[288,256]{1,0:T(8,128)(2,1)S(1)}, bf16[288,256]{1,0:T(8,128)(2,1)S(1)}, u32[]{:S(2)}, u32[]{:S(2)}) collective-permute-start(bf16[288,256]{1,0:T(8,128)(2,1)S(1)} %collective-permute-done.13.refs_13_), channel_id=1, source_target_pairs={{0,224},{32,0},{64,32},{96,64},{128,96},{160,128},{192,160},{224,1... | collective-permute-start | bytes 442376 | tf_op jit(solution)/shard_map/ppermute | solution.py:477
  44.7 3.3 %copy-start.22 = (bf16[288,256]{1,0:T(8,128)(2,1)}, bf16[288,256]{1,0:T(8,128)(2,1)S(1)}, u32[]{:S(2)}) copy-start(bf16[288,256]{1,0:T(8,128)(2,1)S(1)} %collective-permute-done.11.refs_11_) | copy-start | bytes 442372
  46.4 1.7 %copy-start.23 = (bf16[288,256]{1,0:T(8,128)(2,1)}, bf16[288,256]{1,0:T(8,128)(2,1)S(1)}, u32[]{:S(2)}) copy-start(bf16[288,256]{1,0:T(8,128)(2,1)S(1)} %collective-permute-done.14.refs_14_) | copy-start | bytes 442372
  47.9 0.7 copy-start.24
  48.0 0.7 copy-start.25
  48.7 14.1 %copy-start.6 = (s32[64]{0:T(128)S(1)}, s32[64]{0:T(128)}, u32[]{:S(2)}) copy-start(s32[64]{0:T(128)} %get-tuple-element.54.ids) | copy-start | bytes 772
  53.9 1.9 %collective-permute-start.16 = (f32[2,136,256]{2,1,0:T(8,128)}, f32[2,136,256]{2,1,0:T(8,128)S(1)}, u32[]{:S(2)}, u32[]{:S(2)}) collective-permute-start(f32[2,136,256]{2,1,0:T(8,128)} %project.1.mine), channel_id=1, source_target_pairs={{0,8},{8,0},{1,9},{9,1},{2,10},{10,2},{3,11},{11,3},{4,12},{12,4},... | collective-permute-start | bytes 835592 | tf_op jit(solution)/shard_map/ppermute | solution.py:527
  55.7 1.0 copy-start.2
  56.7 27.7 %copy-start.4 = (bf16[144,256]{1,0:T(8,128)(2,1)}, bf16[144,256]{1,0:T(8,128)(2,1)S(1)}, u32[]{:S(2)}) copy-start(bf16[144,256]{1,0:T(8,128)(2,1)S(1)} %get-tuple-element.81.own_0) | copy-start | bytes 221188
  56.8 6.0 %collective-permute-start.17 = (bf16[2,144,256]{2,1,0:T(8,128)(2,1)S(1)}, bf16[2,144,256]{2,1,0:T(8,128)(2,1)S(1)}, u32[]{:S(2)}, u32[]{:S(2)}) collective-permute-start(bf16[2,144,256]{2,1,0:T(8,128)(2,1)S(1)} %get-tuple-element.60.near), channel_id=1, source_target_pairs={{0,16},{16,0},{1,17},{17,1},{2,18},{18,2},{3,19},{19,3},{4,20},{20... | collective-permute-start | bytes 442376 | tf_op jit(solution)/shard_map/ppermute | solution.py:531
  64.1 22.7 %all-to-all-start.1 = ((bf16[8,144,256]{2,1,0:T(8,128)(2,1)}), bf16[8,144,256]{2,1,0:T(8,128)(2,1)S(1)}, u32[]{:S(2)}, u32[]{:S(2)}) async-start(bf16[8,144,256]{2,1,0:T(8,128)(2,1)} %pick_for_planes.1), calls=%async_computation.1 | async-start | bytes 1179648 | tf_op jit(solution)/shard_map/all_to_all | solution.py:540
  68.5 9.0 %collective-permute-start.18 = (bf16[144,256]{1,0:T(8,128)(2,1)S(1)}, bf16[144,256]{1,0:T(8,128)(2,1)S(1)}, u32[]{:S(2)}, u32[]{:S(2)}) collective-permute-start(bf16[144,256]{1,0:T(8,128)(2,1)S(1)} %get-tuple-element.81.own_0), channel_id=1, source_target_pairs={{0,1},{1,0},{2,3},{3,2},{4,5},{5,4},{6,7},{7,6},{8,9},{9,8},{10,11... | collective-permute-start | bytes 221192 | tf_op jit(solution)/shard_map/ppermute | solution.py:556
  71.3 7.2 %collective-permute-start.23 = (bf16[144,256]{1,0:T(8,128)(2,1)S(1)}, bf16[144,256]{1,0:T(8,128)(2,1)S(1)}, u32[]{:S(2)}, u32[]{:S(2)}) collective-permute-start(bf16[144,256]{1,0:T(8,128)(2,1)S(1)} %get-tuple-element.81.own_0), channel_id=1, source_target_pairs={{0,4},{2,6},{4,0},{6,2},{1,5},{3,7},{5,1},{7,3},{8,12},{10,14},{12... | collective-permute-start | bytes 221192 | tf_op jit(solution)/shard_map/ppermute | solution.py:559
  74.2 10.2 %collective-permute-start.21 = (bf16[144,256]{1,0:T(8,128)(2,1)S(1)}, bf16[144,256]{1,0:T(8,128)(2,1)S(1)}, u32[]{:S(2)}, u32[]{:S(2)}) collective-permute-start(bf16[144,256]{1,0:T(8,128)(2,1)S(1)} %get-tuple-element.81.own_0), channel_id=1, source_target_pairs={{0,2},{2,4},{4,6},{6,0},{1,3},{3,5},{5,7},{7,1},{8,10},{10,12},{12... | collective-permute-start | bytes 221192 | tf_op jit(solution)/shard_map/ppermute | solution.py:559
  74.8 9.7 %collective-permute-start.19 = (bf16[144,256]{1,0:T(8,128)(2,1)S(1)}, bf16[144,256]{1,0:T(8,128)(2,1)S(1)}, u32[]{:S(2)}, u32[]{:S(2)}) collective-permute-start(bf16[144,256]{1,0:T(8,128)(2,1)S(1)} %get-tuple-element.81.own_0), channel_id=1, source_target_pairs={{0,6},{2,0},{4,2},{6,4},{1,7},{3,1},{5,3},{7,5},{8,14},{10,8},{12,... | collective-permute-start | bytes 221192 | tf_op jit(solution)/shard_map/ppermute | solution.py:559
  77.5 7.0 %copy-start.26 = (bf16[144,256]{1,0:T(8,128)(2,1)}, bf16[144,256]{1,0:T(8,128)(2,1)S(1)}, u32[]{:S(2)}) copy-start(bf16[144,256]{1,0:T(8,128)(2,1)S(1)} %collective-permute-done.18.own_1) | copy-start | bytes 221188
  77.5 7.0 %collective-permute-start.24 = (bf16[144,256]{1,0:T(8,128)(2,1)S(1)}, bf16[144,256]{1,0:T(8,128)(2,1)S(1)}, u32[]{:S(2)}, u32[]{:S(2)}) collective-permute-start(bf16[144,256]{1,0:T(8,128)(2,1)S(1)} %collective-permute-done.18.own_1), channel_id=1, source_target_pairs={{0,4},{2,6},{4,0},{6,2},{1,5},{3,7},{5,1},{7,3},{8,12},{10,14},{12... | collective-permute-start | bytes 221192 | tf_op jit(solution)/shard_map/ppermute | solution.py:559
  77.9 6.6 %collective-permute-start.22 = (bf16[144,256]{1,0:T(8,128)(2,1)S(1)}, bf16[144,256]{1,0:T(8,128)(2,1)S(1)}, u32[]{:S(2)}, u32[]{:S(2)}) collective-permute-start(bf16[144,256]{1,0:T(8,128)(2,1)S(1)} %collective-permute-done.18.own_1), channel_id=1, source_target_pairs={{0,2},{2,4},{4,6},{6,0},{1,3},{3,5},{5,7},{7,1},{8,10},{10,12},{12... | collective-permute-start | bytes 221192 | tf_op jit(solution)/shard_map/ppermute | solution.py:559
  78.4 6.0 %copy-start.27 = (bf16[144,256]{1,0:T(8,128)(2,1)}, bf16[144,256]{1,0:T(8,128)(2,1)S(1)}, u32[]{:S(2)}) copy-start(bf16[144,256]{1,0:T(8,128)(2,1)S(1)} %collective-permute-done.23.own_6) | copy-start | bytes 221188
  78.4 6.1 %collective-permute-start.20 = (bf16[144,256]{1,0:T(8,128)(2,1)S(1)}, bf16[144,256]{1,0:T(8,128)(2,1)S(1)}, u32[]{:S(2)}, u32[]{:S(2)}) collective-permute-start(bf16[144,256]{1,0:T(8,128)(2,1)S(1)} %collective-permute-done.18.own_1), channel_id=1, source_target_pairs={{0,6},{2,0},{4,2},{6,4},{1,7},{3,1},{5,3},{7,5},{8,14},{10,8},{12,... | collective-permute-start | bytes 221192 | tf_op jit(solution)/shard_map/ppermute | solution.py:559
  84.5 24.6 %copy-start.28 = (bf16[144,256]{1,0:T(8,128)(2,1)}, bf16[144,256]{1,0:T(8,128)(2,1)S(1)}, u32[]{:S(2)}) copy-start(bf16[144,256]{1,0:T(8,128)(2,1)S(1)} %collective-permute-done.21.own_4) | copy-start | bytes 221188
  84.5 24.5 %copy-start.29 = (bf16[144,256]{1,0:T(8,128)(2,1)}, bf16[144,256]{1,0:T(8,128)(2,1)S(1)}, u32[]{:S(2)}) copy-start(bf16[144,256]{1,0:T(8,128)(2,1)S(1)} %collective-permute-done.19.own_2) | copy-start | bytes 221188
  84.5 24.5 %copy-start.30 = (bf16[144,256]{1,0:T(8,128)(2,1)}, bf16[144,256]{1,0:T(8,128)(2,1)S(1)}, u32[]{:S(2)}) copy-start(bf16[144,256]{1,0:T(8,128)(2,1)S(1)} %collective-permute-done.24.own_7) | copy-start | bytes 221188
  84.5 24.5 %copy-start.31 = (bf16[144,256]{1,0:T(8,128)(2,1)}, bf16[144,256]{1,0:T(8,128)(2,1)S(1)}, u32[]{:S(2)}) copy-start(bf16[144,256]{1,0:T(8,128)(2,1)S(1)} %collective-permute-done.22.own_5) | copy-start | bytes 221188
  84.6 24.5 %copy-start.32 = (bf16[144,256]{1,0:T(8,128)(2,1)}, bf16[144,256]{1,0:T(8,128)(2,1)S(1)}, u32[]{:S(2)}) copy-start(bf16[144,256]{1,0:T(8,128)(2,1)S(1)} %collective-permute-done.20.own_3) | copy-start | bytes 221188
  86.9 0.8 copy-start.10
  86.9 22.2 %collective-permute-start.25 = (bf16[16,288,256]{2,1,0:T(8,128)(2,1)}, bf16[16,288,256]{2,1,0:T(8,128)(2,1)}, u32[]{:S(2)}, u32[]{:S(2)}) collective-permute-start(bf16[16,288,256]{2,1,0:T(8,128)(2,1)} %stack_blocks.1.kept), channel_id=1, source_target_pairs={{0,8},{8,0},{1,9},{9,1},{2,10},{10,2},{3,11},{11,3},{4,12},{12,4},... | collective-permute-start | bytes 7077896 | tf_op jit(solution)/shard_map/ppermute | solution.py:561
  109.0 19.4 %copy-start.7 = (s32[64]{0:T(128)S(1)}, s32[64]{0:T(128)}, u32[]{:S(2)}) copy-start(s32[64]{0:T(128)} %get-tuple-element.54.ids) | copy-start | bytes 772
  119.5 1.9 %collective-permute-start.26 = (bf16[16,80,128]{2,1,0:T(8,128)(2,1)}, bf16[16,80,128]{2,1,0:T(8,128)(2,1)S(1)}, u32[]{:S(2)}, u32[]{:S(2)}) collective-permute-start(bf16[16,80,128]{2,1,0:T(8,128)(2,1)} %get-tuple-element.92), channel_id=1, source_target_pairs={{0,8},{8,0},{1,9},{9,1},{2,10},{10,2},{3,11},{11,3},{4,12},{12,4},... | collective-permute-start | bytes 983048 | tf_op jit(solution)/shard_map/ppermute | solution.py:604
  121.5 1.1 copy-start.3
  123.3 18.0 %all-to-all-start.3 = ((bf16[16,80,128]{2,1,0:T(8,128)(2,1)}), bf16[16,80,128]{2,1,0:T(8,128)(2,1)S(1)}, u32[]{:S(2)}, u32[]{:S(2)}) async-start(bf16[16,80,128]{2,1,0:T(8,128)(2,1)} %add_core.1), calls=%async_computation.3 | async-start | bytes 655360 | tf_op jit(solution)/shard_map/all_to_all | solution.py:605
  128.5 1.7 %copy-start = (bf16[16,288,256]{2,1,0:T(8,128)(2,1)S(1)}, bf16[16,288,256]{2,1,0:T(8,128)(2,1)}, u32[]{:S(2)}) copy-start(bf16[16,288,256]{2,1,0:T(8,128)(2,1)} %stack_blocks.1.kept) | copy-start | bytes 7077892
  130.1 0.8 copy-start.5
  131.0 0.7 copy-start.8
  131.7 20.4 %copy-start.9 = (f32[128]{0:T(128)S(1)}, f32[128]{0:T(128)}, u32[]{:S(2)}) copy-start(f32[128]{0:T(128)} %param.12) | copy-start | bytes 1540

commit v5 on v4

--- a/solution.py
+++ b/solution.py
@@ -1,4 +1,3 @@
-import functools
 import math
 
 import jax
@@ -173,22 +172,23 @@
     first[...] = items[0]
 
 
-def pick_for_planes(ids, near, side, out, items):
-    items[0:2] = near[...]
-    items[2:4] = side[...]
+def pick_for_planes(ids, near, side, out):
     for z in range(NZ):
-        out[z] = items[ids[WANTED + z]]
-
-
-def pick_partner(ids, received, out, mine, sem, sems):
-    copy = pltpu.make_async_copy(received.at[ids[MATE_STEP]], mine, sem.at[0])
-    copy.start()
-    copy.wait()
-    copies = [pltpu.make_async_copy(mine, out.at[s], sems.at[s]) for s in range(NSEQ)]
-    for copy in copies:
-        copy.start()
-    for copy in copies:
-        copy.wait()
+        which = ids[WANTED + z]
+
+        @pl.when(which < 2)
+        def _(z=z, which=which):
+            out[z] = near[which & 1]
+
+        @pl.when(which >= 2)
+        def _(z=z, which=which):
+            out[z] = side[which & 1]
+
+
+def pick_partner(ids, received, out):
+    mine = received[ids[MATE_STEP]]
+    for s in range(NSEQ):
+        out[s] = mine
 
 
 def attention(
@@ -477,6 +477,10 @@
     found[key] = lax.ppermute(found[(dz + step, dx)], "z", way)
 
 
+def along_y(piece, dy):
+    return lax.ppermute(piece, "y", [(i, (i - dy) % 4) for i in range(4)])
+
+
 def per_device(hidden, w_query, w_key, w_value, score_vec, labels, lengths, partner):
     tokens = hidden.reshape(BLK, NDP * ROWS)
     score = score_vec.reshape(1, HEAD)
@@ -504,7 +508,9 @@
     found = {(0, 0): block, (0, 1): other, (-1, 0): up, (1, 0): down}
     hidden_t = lax.all_to_all(split, SEQ, 0, 0, tiled=True)
     for key in ORDER:
-        if key not in found:
+        if key == (NZ // 2, 1):
+            found[key] = lax.ppermute(other, "z", [(i, (i + NZ // 2) % NZ) for i in range(NZ)])
+        elif key not in found:
             ring_step(found, key)
     count = len(ORDER)
     blocks = [found[key] for key in ORDER]
@@ -533,7 +539,6 @@
         pick_for_planes,
         shape((NZ, *item), BF16),
         (ids, items, side),
-        scratch=[pltpu.VMEM((4, *item), BF16)],
         name="pick_for_planes",
     )
     slots, hidden_t, *blocks = lax.optimization_barrier((slots, hidden_t, *blocks))
@@ -556,19 +561,15 @@
     windows = {(0, 0): mine, (0, 1): lax.ppermute(mine, "xh", SWAP)}
     for dy in (1, -1, 2):
         for dx in (0, 1):
-            windows[(dy, dx)] = lax.ppermute(windows[(0, dx)], "y", [(i, (i - dy) % 4) for i in range(4)])
+            windows[(dy, dx)] = along_y(windows[(0, dx)], dy)
     arrived, kept, *own = lax.optimization_barrier((arrived, kept, *[windows[key] for key in AROUND]))
-    swapped = lax.ppermute(kept, "c", SWAP)
     theirs = call(
         pick_partner,
         shape((NSEQ, *item), BF16),
         (ids, arrived),
-        far=(1,),
-        far_out=((NSEQ, *item),),
-        scratch=[pltpu.VMEM(item, BF16), pltpu.SemaphoreType.DMA((1,)), pltpu.SemaphoreType.DMA((NSEQ,))],
         name="pick_partner",
-        limit=62,
-    )
+    )
+    swapped = lax.ppermute(kept, "c", SWAP)
     mate = lax.all_to_all(theirs, SEQ, 0, 0, tiled=True)
 
     message = (NDP // 2, MESSAGE, HEAD)

time: 154 us -> 160 us (1.039)
  waiting for transfers between devices: 27.5 us -> 31.7 us
  starting transfers between devices: 51.2 us -> 53.6 us
  Pallas kernels: 35.3 us -> 33.5 us
  blocking collectives: 29.6 us -> 31.4 us
    ppermute x12 -> x11, waiting for transfers between devices: 10.1 us -> 14.1 us  [ring_step(): found[key] = lax.ppermute(found[dz + step, dx], 'z', way)]
    pallas_call x12, Pallas kernels: 35.3 us -> 33.5 us  [call(): pl.pallas_call(kernel, out_shape=outs, in_specs=[SM if a.dtype == jnp.int...]
    all_to_all x1, blocking collectives: 18.9 us -> 20.6 us  [per_device(): mate = lax.all_to_all(theirs, SEQ, 0, 0, tiled=True)]
    ppermute x12 -> x11, starting transfers between devices: 14.6 us -> 16 us  [ring_step(): found[key] = lax.ppermute(found[dz + step, dx], 'z', way)]
    ppermute x6 -> x7, starting transfers between devices: 9.91 us -> 11.3 us  [the longest x6 9.58 us: along_y(): return lax.ppermute(piece, 'y', [(i, (i - dy) % 4) for i in range(4)])]
    unnamed x66 -> x64, local copies, waits for them, and re-layouts: 8.33 us -> 7.46 us
  transfers between devices with their start and end apart: 30 -> 30, of which waited for: 14 -> 13; matrix products, arithmetic and copies ran while one was open for 0% -> 0% of each run, Pallas kernels for 15% -> 13%
where the time goes in v5:
time: 160 us; the launch traced here: 159 us
  starting transfers between devices  53.6 us (34%)
  Pallas kernels  33.5 us (21%)
  waiting for transfers between devices  31.7 us (20%)
  blocking collectives  31.4 us (20%)
  local copies, waits for them, and re-layouts  7.46 us (5%)
    pallas_call x12, Pallas kernels, call(): pl.pallas_call(kernel, out_shape=outs, in_specs=[SM if a.dtype == jnp.int...  33.5 us
    all_to_all x1, blocking collectives, per_device(): mate = lax.all_to_all(theirs, SEQ, 0, 0, tiled=True)  20.6 us
    ppermute x11, starting transfers between devices, ring_step(): found[key] = lax.ppermute(found[dz + step, dx], 'z', way)  16 us
    ppermute x11, waiting for transfers between devices, ring_step(): found[key] = lax.ppermute(found[dz + step, dx], 'z', way)  14.1 us
    all_to_all x1, blocking collectives, per_device(): arrived = lax.all_to_all(sums, SEQ, 0, 0, tiled=True)  10.7 us
    ppermute x6, starting transfers between devices, along_y(): return lax.ppermute(piece, 'y', [(i, (i - dy) % 4) for i in range(4)])  9.58 us
    unnamed x64, local copies, waits for them, and re-layouts  7.46 us
    all_to_all x1, starting transfers between devices, per_device(): hidden_t = lax.all_to_all(split, SEQ, 0, 0, tiled=True)  6.04 us
  transfers between devices with their start and end apart: 30, of which 13 were waited for; matrix products, arithmetic and copies ran while one was open for 0% of the time, Pallas kernels for 13%

profile of v5, /device:TPU:2, one launch (start us, length us, event | category | flops | bytes accessed | tf_op | source)
XLA Modules:
  0.0 159.2 jit_solution(4321308401766720059)
XLA Ops:
  0.6 0.1 collective-permute-start
  0.7 0.6 pad_add_fusion.pos
  1.3 2.4 %pack_weights.1 = (bf16[288,256]{1,0:T(8,128)(2,1)}, s32[64]{0:T(128)}) custom-call(s32[4]{0:T(128)} %pad_add_fusion.pos, s32[32]{0:T(128)} %lengths.1, s32[32]{0:T(128)} %labels.1, s32[32]{0:T(128)} %partner.1, bf16[256,128]{1,0:T(8,128)(2,1)} %wq.1, bf16[256,128]{1,0:T(8,128)(2,1)} %wk.1, bf16[256,128]{1,0:T(8,128)(2,1)} %wv.1, f32[1,128]{1,0:T(1,128)} %bitcast.13), custom_call_target="tpu_custom_call" | custom-call | tf_op jit(solution)/shard_map/pack_weights/pallas_call | solution.py:36
  3.8 5.9 %collective-permute-start.3 = (bf16[288,256]{1,0:T(8,128)(2,1)}, bf16[288,256]{1,0:T(8,128)(2,1)S(1)}, u32[]{:S(2)}, u32[]{:S(2)}) collective-permute-start(bf16[288,256]{1,0:T(8,128)(2,1)} %get-tuple-element.63.refs_0_), channel_id=1, source_target_pairs={{0,224},{32,0},{64,32},{96,64},{128,96},{160,128},{192,160},{224,1... | collective-permute-start | bytes 442376 | tf_op jit(solution)/shard_map/ppermute | solution.py:504
  9.7 0.5 collective-permute-start.1
  10.3 1.6 copy-done.1
  11.8 2.7 %split_columns.1 = bf16[8,128,1024]{2,1,0:T(8,128)(2,1)} custom-call(bf16[128,8192]{1,0:T(8,128)(2,1)S(1)} %bitcast.12), custom_call_target="tpu_custom_call" | custom-call | flops 1073741824 | tf_op jit(solution)/shard_map/split_columns/pallas_call | solution.py:36
  14.5 2.6 %collective-permute-done.2.refs_2_ = bf16[288,256]{1,0:T(8,128)(2,1)S(1)} collective-permute-done((bf16[288,256]{1,0:T(8,128)(2,1)}, bf16[288,256]{1,0:T(8,128)(2,1)S(1)}, u32[]{:S(2)}, u32[]{:S(2)}) %collective-permute-start.2) | collective-permute-done | bytes 147488 | tf_op jit(solution)/shard_map/ppermute | solution.py:503
  17.1 0.0 collective-permute-done.1.refs_1_
  17.1 6.0 %all-to-all-start = ((bf16[8,128,1024]{2,1,0:T(8,128)(2,1)}), bf16[8,128,1024]{2,1,0:T(8,128)(2,1)}, u32[]{:S(2)}, u32[]{:S(2)}) async-start(bf16[8,128,1024]{2,1,0:T(8,128)(2,1)} %split_columns.1), calls=%async_computation | async-start | bytes 4194304 | tf_op jit(solution)/shard_map/all_to_all | solution.py:509
  23.1 0.1 collective-permute-start.6
  23.2 3.2 %collective-permute-start.7 = (bf16[288,256]{1,0:T(8,128)(2,1)S(1)}, bf16[288,256]{1,0:T(8,128)(2,1)S(1)}, u32[]{:S(2)}, u32[]{:S(2)}) collective-permute-start(bf16[288,256]{1,0:T(8,128)(2,1)S(1)} %collective-permute-done.3.refs_3_), channel_id=1, source_target_pairs={{0,224},{32,0},{64,32},{96,64},{128,96},{160,128},{192,160},{224,1... | collective-permute-start | bytes 442376 | tf_op jit(solution)/shard_map/ppermute | solution.py:477
  26.5 0.5 collective-permute-start.5
  27.0 1.5 collective-permute-start.4
  28.5 1.8 %collective-permute-done.6.refs_6_ = bf16[288,256]{1,0:T(8,128)(2,1)S(1)} collective-permute-done((bf16[288,256]{1,0:T(8,128)(2,1)S(1)}, bf16[288,256]{1,0:T(8,128)(2,1)S(1)}, u32[]{:S(2)}, u32[]{:S(2)}) %collective-permute-start.6) | collective-permute-done | bytes 147488 | tf_op jit(solution)/shard_map/ppermute | solution.py:477
  30.3 1.7 %collective-permute-start.15 = (bf16[288,256]{1,0:T(8,128)(2,1)S(1)}, bf16[288,256]{1,0:T(8,128)(2,1)S(1)}, u32[]{:S(2)}, u32[]{:S(2)}) collective-permute-start(bf16[288,256]{1,0:T(8,128)(2,1)S(1)} %collective-permute-done.1.refs_1_), channel_id=1, source_target_pairs={{0,128},{32,160},{64,192},{96,224},{128,0},{160,32},{192,64},{224,... | collective-permute-start | bytes 442376 | tf_op jit(solution)/shard_map/ppermute | solution.py:512
  32.0 5.7 %collective-permute-done.5.refs_5_ = bf16[288,256]{1,0:T(8,128)(2,1)S(1)} collective-permute-done((bf16[288,256]{1,0:T(8,128)(2,1)S(1)}, bf16[288,256]{1,0:T(8,128)(2,1)S(1)}, u32[]{:S(2)}, u32[]{:S(2)}) %collective-permute-start.5) | collective-permute-done | bytes 147488 | tf_op jit(solution)/shard_map/ppermute | solution.py:477
  37.7 4.2 %collective-permute-start.9 = (bf16[288,256]{1,0:T(8,128)(2,1)S(1)}, bf16[288,256]{1,0:T(8,128)(2,1)S(1)}, u32[]{:S(2)}, u32[]{:S(2)}) collective-permute-start(bf16[288,256]{1,0:T(8,128)(2,1)S(1)} %collective-permute-done.5.refs_5_), channel_id=1, source_target_pairs={{0,224},{32,0},{64,32},{96,64},{128,96},{160,128},{192,160},{224,1... | collective-permute-start | bytes 442376 | tf_op jit(solution)/shard_map/ppermute | solution.py:477
  42.0 0.0 collective-permute-start.8
  42.0 0.5 collective-permute-done.15.refs_15_
  42.5 2.7 %collective-permute-start.11 = (bf16[288,256]{1,0:T(8,128)(2,1)S(1)}, bf16[288,256]{1,0:T(8,128)(2,1)S(1)}, u32[]{:S(2)}, u32[]{:S(2)}) collective-permute-start(bf16[288,256]{1,0:T(8,128)(2,1)S(1)} %collective-permute-done.7.refs_7_), channel_id=1, source_target_pairs={{0,224},{32,0},{64,32},{96,64},{128,96},{160,128},{192,160},{224,1... | collective-permute-start | bytes 442376 | tf_op jit(solution)/shard_map/ppermute | solution.py:477
  45.2 0.0 collective-permute-done.10.refs_10_
  45.2 0.0 collective-permute-start.14
  45.2 0.3 collective-permute-done.9.refs_9_
  45.5 3.7 %collective-permute-start.13 = (bf16[288,256]{1,0:T(8,128)(2,1)S(1)}, bf16[288,256]{1,0:T(8,128)(2,1)S(1)}, u32[]{:S(2)}, u32[]{:S(2)}) collective-permute-start(bf16[288,256]{1,0:T(8,128)(2,1)S(1)} %collective-permute-done.9.refs_9_), channel_id=1, source_target_pairs={{0,224},{32,0},{64,32},{96,64},{128,96},{160,128},{192,160},{224,1... | collective-permute-start | bytes 442376 | tf_op jit(solution)/shard_map/ppermute | solution.py:477
  49.2 2.4 %collective-permute-done.14.refs_14_ = bf16[288,256]{1,0:T(8,128)(2,1)S(1)} collective-permute-done((bf16[288,256]{1,0:T(8,128)(2,1)S(1)}, bf16[288,256]{1,0:T(8,128)(2,1)S(1)}, u32[]{:S(2)}, u32[]{:S(2)}) %collective-permute-start.14) | collective-permute-done | bytes 147488 | tf_op jit(solution)/shard_map/ppermute | solution.py:477
  51.6 0.3 collective-permute-done.13.refs_13_
  51.9 3.7 %collective-permute-done.12.refs_12_ = bf16[288,256]{1,0:T(8,128)(2,1)S(1)} collective-permute-done((bf16[288,256]{1,0:T(8,128)(2,1)S(1)}, bf16[288,256]{1,0:T(8,128)(2,1)S(1)}, u32[]{:S(2)}, u32[]{:S(2)}) %collective-permute-start.12) | collective-permute-done | bytes 147488 | tf_op jit(solution)/shard_map/ppermute | solution.py:477
  55.6 0.5 copy-done.24
  56.2 5.2 %project.1.mine = f32[2,136,256]{2,1,0:T(8,128)} custom-call(s32[64]{0:T(128)} %get-tuple-element.54.ids, bf16[128,8192]{1,0:T(8,128)(2,1)} %bitcast.11, bf16[128,8192]{1,0:T(8,128)(2,1)} %collective-permute-done.sibling, bf16[288,256]{1,0:T(8,128)(2,1)} %get-tuple-element.63.refs_0_, bf16[288,256]{1,0:T(8,128)(2,1)} %copy-done.12, ...), custom_call_target="tpu_custom_call" | custom-call | flops 536870912 | bytes 6291456 | tf_op jit(solution)/shard_map/project/pallas_call | solution.py:36
  61.4 0.1 collective-permute-start.16
  61.5 1.8 %collective-permute-done.16.theirs = f32[2,136,256]{2,1,0:T(8,128)S(1)} collective-permute-done((f32[2,136,256]{2,1,0:T(8,128)}, f32[2,136,256]{2,1,0:T(8,128)S(1)}, u32[]{:S(2)}, u32[]{:S(2)}) %collective-permute-start.16) | collective-permute-done | bytes 278560 | tf_op jit(solution)/shard_map/ppermute | solution.py:533
  63.3 1.0 copy-done.2
  64.3 0.0 copy-start.4
  64.3 1.2 collective-permute-start.17
  65.5 4.8 %collective-permute-done.17.side = bf16[2,144,256]{2,1,0:T(8,128)(2,1)S(1)} collective-permute-done((bf16[2,144,256]{2,1,0:T(8,128)(2,1)S(1)}, bf16[2,144,256]{2,1,0:T(8,128)(2,1)S(1)}, u32[]{:S(2)}, u32[]{:S(2)}) %collective-permute-start.17) | collective-permute-done | bytes 147488 | tf_op jit(solution)/shard_map/ppermute | solution.py:537
  70.3 1.5 pick_for_planes.1
  71.8 3.5 %all-to-all-start.1 = ((bf16[8,144,256]{2,1,0:T(8,128)(2,1)}), bf16[8,144,256]{2,1,0:T(8,128)(2,1)S(1)}, u32[]{:S(2)}, u32[]{:S(2)}) async-start(bf16[8,144,256]{2,1,0:T(8,128)(2,1)} %pick_for_planes.1), calls=%async_computation.1 | async-start | bytes 1179648 | tf_op jit(solution)/shard_map/all_to_all | solution.py:545
  75.3 4.0 %collective-permute-start.18 = (bf16[144,256]{1,0:T(8,128)(2,1)S(1)}, bf16[144,256]{1,0:T(8,128)(2,1)S(1)}, u32[]{:S(2)}, u32[]{:S(2)}) collective-permute-start(bf16[144,256]{1,0:T(8,128)(2,1)S(1)} %get-tuple-element.81.own_0), channel_id=1, source_target_pairs={{0,1},{1,0},{2,3},{3,2},{4,5},{5,4},{6,7},{7,6},{8,9},{9,8},{10,11... | collective-permute-start | bytes 221192 | tf_op jit(solution)/shard_map/ppermute | solution.py:561
  79.3 3.0 %collective-permute-start.23 = (bf16[144,256]{1,0:T(8,128)(2,1)S(1)}, bf16[144,256]{1,0:T(8,128)(2,1)S(1)}, u32[]{:S(2)}, u32[]{:S(2)}) collective-permute-start(bf16[144,256]{1,0:T(8,128)(2,1)S(1)} %get-tuple-element.81.own_0), channel_id=1, source_target_pairs={{0,4},{2,6},{4,0},{6,2},{1,5},{3,7},{5,1},{7,3},{8,12},{10,14},{12... | collective-permute-start | bytes 221192 | tf_op jit(solution)/shard_map/ppermute | solution.py:481
  82.4 0.6 collective-permute-start.21
  82.9 2.7 %collective-permute-start.19 = (bf16[144,256]{1,0:T(8,128)(2,1)S(1)}, bf16[144,256]{1,0:T(8,128)(2,1)S(1)}, u32[]{:S(2)}, u32[]{:S(2)}) collective-permute-start(bf16[144,256]{1,0:T(8,128)(2,1)S(1)} %get-tuple-element.81.own_0), channel_id=1, source_target_pairs={{0,6},{2,0},{4,2},{6,4},{1,7},{3,1},{5,3},{7,5},{8,14},{10,8},{12,... | collective-permute-start | bytes 221192 | tf_op jit(solution)/shard_map/ppermute | solution.py:481
  85.6 0.9 collective-permute-start.22
  86.6 2.4 %collective-permute-start.20 = (bf16[144,256]{1,0:T(8,128)(2,1)S(1)}, bf16[144,256]{1,0:T(8,128)(2,1)S(1)}, u32[]{:S(2)}, u32[]{:S(2)}) collective-permute-start(bf16[144,256]{1,0:T(8,128)(2,1)S(1)} %collective-permute-done.18.own_1), channel_id=1, source_target_pairs={{0,6},{2,0},{4,2},{6,4},{1,7},{3,1},{5,3},{7,5},{8,14},{10,8},{12,... | collective-permute-start | bytes 221192 | tf_op jit(solution)/shard_map/ppermute | solution.py:481
  88.9 3.3 %stack_blocks.1.kept = bf16[16,288,256]{2,1,0:T(8,128)(2,1)} custom-call(bf16[288,256]{1,0:T(8,128)(2,1)} %get-tuple-element.63.refs_0_, bf16[288,256]{1,0:T(8,128)(2,1)} %copy-done.12, bf16[288,256]{1,0:T(8,128)(2,1)} %copy-done.11, bf16[288,256]{1,0:T(8,128)(2,1)} %copy-done.10, bf16[288,256]{1,0:T(8,128)(2,1)} %copy-done.16, bf16[288,256]{1,0:T(8,128)(2,1)} %copy-done.15, ...), custom_call_target="tpu_custom_call" | custom-call | bytes 5242880 | tf_op jit(solution)/shard_map/stack_blocks/pallas_call | solution.py:36
  92.3 0.0 copy-start.28
  92.3 1.5 all-to-all-done.1.received
  93.9 0.0 collective-permute-start.25
  93.9 0.6 pick_partner.1
  94.5 20.6 %all_to_all.25.mate = bf16[8,144,256]{2,1,0:T(8,128)(2,1)} all-to-all(bf16[8,144,256]{2,1,0:T(8,128)(2,1)S(1)} %pick_partner.1), channel_id=1, replica_groups=mesh['z'=8,'xl'=2,'c'=2,'y'=4,'xh'=2] {'y','xh'}, dimensions={0} | all-to-all | bytes 1179648 | tf_op jit(solution)/shard_map/all_to_all | solution.py:573
  115.2 10.4 %attention.1 = (f32[16,80,128]{2,1,0:T(8,128)}, bf16[16,80,128]{2,1,0:T(8,128)(2,1)}, bf16[128,256]{1,0:T(8,128)(2,1)}, bf16[16,128]{1,0:T(8,128)(2,1)}) custom-call(s32[64]{0:T(128)} %get-tuple-element.54.ids, bf16[8,144,256]{2,1,0:T(8,128)(2,1)} %all_to_all.25.mate, bf16[144,256]{1,0:T(8,128)(2,1)} %copy-done.4, bf16[144,256]{1,0:T(8,128)(2,1)} %copy-done.25, ...), custom_call_target="tpu_custom_call" | custom-call | flops 2147483648 | tf_op jit(solution)/shard_map/attention/pallas_call | solution.py:36
  125.6 0.1 collective-permute-start.26
  125.7 1.8 %collective-permute-done.26.received = bf16[16,80,128]{2,1,0:T(8,128)(2,1)S(1)} collective-permute-done((bf16[16,80,128]{2,1,0:T(8,128)(2,1)}, bf16[16,80,128]{2,1,0:T(8,128)(2,1)S(1)}, u32[]{:S(2)}, u32[]{:S(2)}) %collective-permute-start.26) | collective-permute-done | bytes 327712 | tf_op jit(solution)/shard_map/ppermute | solution.py:605
  127.5 1.1 copy-done.3
  128.6 0.8 add_core.1
  129.4 4.7 %all-to-all-start.3 = ((bf16[16,80,128]{2,1,0:T(8,128)(2,1)}), bf16[16,80,128]{2,1,0:T(8,128)(2,1)S(1)}, u32[]{:S(2)}, u32[]{:S(2)}) async-start(bf16[16,80,128]{2,1,0:T(8,128)(2,1)} %add_core.1), calls=%async_computation.3 | async-start | bytes 655360 | tf_op jit(solution)/shard_map/all_to_all | solution.py:606
  134.1 1.7 %copy-done = bf16[16,288,256]{2,1,0:T(8,128)(2,1)S(1)} copy-done((bf16[16,288,256]{2,1,0:T(8,128)(2,1)S(1)}, bf16[16,288,256]{2,1,0:T(8,128)(2,1)}, u32[]{:S(2)}) %copy-start) | copy-done | bytes 2359320
  135.8 0.8 copy-done.5
  136.6 0.7 copy-done.8
  137.3 5.2 %hidden_grads.1 = bf16[128,8192]{1,0:T(8,128)(2,1)} custom-call(s32[64]{0:T(128)S(1)} %copy-done.7, bf16[128,256]{1,0:T(8,128)(2,1)S(1)} %copy-done.5, bf16[16,128]{1,0:T(8,128)(2,1)S(1)} %copy-done.8, bf16[16,288,256]{2,1,0:T(8,128)(2,1)S(1)} %copy-done, bf16[16,288,256]{2,1,0:T(8,128)(2,1)} %collective-permute-done.25.swapped), custom_call_target="tpu_custom_call" | custom-call | flops 536870912 | bytes 6291456 | tf_op jit(solution)/shard_map/hidden_grads/pallas_call | solution.py:36
  142.5 4.6 %all-to-all-done.3.received = bf16[16,80,128]{2,1,0:T(8,128)(2,1)S(1)} async-done(((bf16[16,80,128]{2,1,0:T(8,128)(2,1)}), bf16[16,80,128]{2,1,0:T(8,128)(2,1)S(1)}, u32[]{:S(2)}, u32[]{:S(2)}) %all-to-all-start.3) | async-done | bytes 327712 | tf_op jit(solution)/shard_map/all_to_all | solution.py:606
  147.0 0.1 sum_shares.1
  147.1 10.7 %all_to_all.26.received = bf16[8,80,128]{2,1,0:T(8,128)(2,1)S(1)} all-to-all(bf16[8,80,128]{2,1,0:T(8,128)(2,1)S(1)} %sum_shares.1), channel_id=1, replica_groups=mesh['z'=8,'xl'=2,'c'=2,'y'=4,'xh'=2] {'y','xh'}, dimensions={0} | all-to-all | bytes 327680 | tf_op jit(solution)/shard_map/all_to_all | solution.py:623
  157.8 1.3 unpack.1
  (75 shorter events, 0.2 us)
Async XLA Ops:
  0.6 54.9 %collective-permute-start = (bf16[128,8192]{1,0:T(8,128)(2,1)}, bf16[128,8192]{1,0:T(8,128)(2,1)}, u32[]{:S(2)}, u32[]{:S(2)}) collective-permute-start(bf16[128,8192]{1,0:T(8,128)(2,1)} %bitcast.10), channel_id=1, source_target_pairs={{0,8},{8,0},{1,9},{9,1},{2,10},{10,2},{3,11},{11,3},{4,12},{12,4},... | collective-permute-start | bytes 6291464 | tf_op jit(solution)/shard_map/ppermute | solution.py:502
  3.8 10.7 %collective-permute-start.3 = (bf16[288,256]{1,0:T(8,128)(2,1)}, bf16[288,256]{1,0:T(8,128)(2,1)S(1)}, u32[]{:S(2)}, u32[]{:S(2)}) collective-permute-start(bf16[288,256]{1,0:T(8,128)(2,1)} %get-tuple-element.63.refs_0_), channel_id=1, source_target_pairs={{0,224},{32,0},{64,32},{96,64},{128,96},{160,128},{192,160},{224,1... | collective-permute-start | bytes 442376 | tf_op jit(solution)/shard_map/ppermute | solution.py:504
  9.7 7.4 %collective-permute-start.2 = (bf16[288,256]{1,0:T(8,128)(2,1)}, bf16[288,256]{1,0:T(8,128)(2,1)S(1)}, u32[]{:S(2)}, u32[]{:S(2)}) collective-permute-start(bf16[288,256]{1,0:T(8,128)(2,1)} %get-tuple-element.63.refs_0_), channel_id=1, source_target_pairs={{0,32},{32,64},{64,96},{96,128},{128,160},{160,192},{192,224},{224... | collective-permute-start | bytes 442376 | tf_op jit(solution)/shard_map/ppermute | solution.py:503
  9.7 7.4 %collective-permute-start.1 = (bf16[288,256]{1,0:T(8,128)(2,1)}, bf16[288,256]{1,0:T(8,128)(2,1)S(1)}, u32[]{:S(2)}, u32[]{:S(2)}) collective-permute-start(bf16[288,256]{1,0:T(8,128)(2,1)} %get-tuple-element.63.refs_0_), channel_id=1, source_target_pairs={{0,16},{16,0},{1,17},{17,1},{2,18},{18,2},{3,19},{19,3},{4,20},{20... | collective-permute-start | bytes 442376 | tf_op jit(solution)/shard_map/ppermute | solution.py:501
  10.3 1.6 copy-start.1
  14.5 8.7 %copy-start.10 = (bf16[288,256]{1,0:T(8,128)(2,1)}, bf16[288,256]{1,0:T(8,128)(2,1)S(1)}, u32[]{:S(2)}) copy-start(bf16[288,256]{1,0:T(8,128)(2,1)S(1)} %collective-permute-done.3.refs_3_) | copy-start | bytes 442372
  17.1 6.0 %copy-start.11 = (bf16[288,256]{1,0:T(8,128)(2,1)}, bf16[288,256]{1,0:T(8,128)(2,1)S(1)}, u32[]{:S(2)}) copy-start(bf16[288,256]{1,0:T(8,128)(2,1)S(1)} %collective-permute-done.2.refs_2_) | copy-start | bytes 442372
  17.1 13.2 %copy-start.12 = (bf16[288,256]{1,0:T(8,128)(2,1)}, bf16[288,256]{1,0:T(8,128)(2,1)S(1)}, u32[]{:S(2)}) copy-start(bf16[288,256]{1,0:T(8,128)(2,1)S(1)} %collective-permute-done.1.refs_1_) | copy-start | bytes 442372
  17.1 54.7 %all-to-all-start = ((bf16[8,128,1024]{2,1,0:T(8,128)(2,1)}), bf16[8,128,1024]{2,1,0:T(8,128)(2,1)}, u32[]{:S(2)}, u32[]{:S(2)}) async-start(bf16[8,128,1024]{2,1,0:T(8,128)(2,1)} %split_columns.1), calls=%async_computation | async-start | bytes 4194304 | tf_op jit(solution)/shard_map/all_to_all | solution.py:509
  23.1 7.2 %collective-permute-start.6 = (bf16[288,256]{1,0:T(8,128)(2,1)S(1)}, bf16[288,256]{1,0:T(8,128)(2,1)S(1)}, u32[]{:S(2)}, u32[]{:S(2)}) collective-permute-start(bf16[288,256]{1,0:T(8,128)(2,1)S(1)} %collective-permute-done.2.refs_2_), channel_id=1, source_target_pairs={{0,32},{32,64},{64,96},{96,128},{128,160},{160,192},{192,224},{224... | collective-permute-start | bytes 442376 | tf_op jit(solution)/shard_map/ppermute | solution.py:477
  23.2 8.8 %collective-permute-start.7 = (bf16[288,256]{1,0:T(8,128)(2,1)S(1)}, bf16[288,256]{1,0:T(8,128)(2,1)S(1)}, u32[]{:S(2)}, u32[]{:S(2)}) collective-permute-start(bf16[288,256]{1,0:T(8,128)(2,1)S(1)} %collective-permute-done.3.refs_3_), channel_id=1, source_target_pairs={{0,224},{32,0},{64,32},{96,64},{128,96},{160,128},{192,160},{224,1... | collective-permute-start | bytes 442376 | tf_op jit(solution)/shard_map/ppermute | solution.py:477
  26.5 11.2 %collective-permute-start.5 = (bf16[288,256]{1,0:T(8,128)(2,1)S(1)}, bf16[288,256]{1,0:T(8,128)(2,1)S(1)}, u32[]{:S(2)}, u32[]{:S(2)}) collective-permute-start(bf16[288,256]{1,0:T(8,128)(2,1)S(1)} %collective-permute-done.1.refs_1_), channel_id=1, source_target_pairs={{0,224},{32,0},{64,32},{96,64},{128,96},{160,128},{192,160},{224,1... | collective-permute-start | bytes 442376 | tf_op jit(solution)/shard_map/ppermute | solution.py:477
  27.0 15.0 %collective-permute-start.4 = (bf16[288,256]{1,0:T(8,128)(2,1)S(1)}, bf16[288,256]{1,0:T(8,128)(2,1)S(1)}, u32[]{:S(2)}, u32[]{:S(2)}) collective-permute-start(bf16[288,256]{1,0:T(8,128)(2,1)S(1)} %collective-permute-done.1.refs_1_), channel_id=1, source_target_pairs={{0,32},{32,64},{64,96},{96,128},{128,160},{160,192},{192,224},{224... | collective-permute-start | bytes 442376 | tf_op jit(solution)/shard_map/ppermute | solution.py:477
  30.3 25.2 %copy-start.13 = (bf16[288,256]{1,0:T(8,128)(2,1)}, bf16[288,256]{1,0:T(8,128)(2,1)S(1)}, u32[]{:S(2)}) copy-start(bf16[288,256]{1,0:T(8,128)(2,1)S(1)} %collective-permute-done.6.refs_6_) | copy-start | bytes 442372
  30.3 12.1 %collective-permute-start.15 = (bf16[288,256]{1,0:T(8,128)(2,1)S(1)}, bf16[288,256]{1,0:T(8,128)(2,1)S(1)}, u32[]{:S(2)}, u32[]{:S(2)}) collective-permute-start(bf16[288,256]{1,0:T(8,128)(2,1)S(1)} %collective-permute-done.1.refs_1_), channel_id=1, source_target_pairs={{0,128},{32,160},{64,192},{96,224},{128,0},{160,32},{192,64},{224,... | collective-permute-start | bytes 442376 | tf_op jit(solution)/shard_map/ppermute | solution.py:512
  32.0 23.5 %copy-start.14 = (bf16[288,256]{1,0:T(8,128)(2,1)}, bf16[288,256]{1,0:T(8,128)(2,1)S(1)}, u32[]{:S(2)}) copy-start(bf16[288,256]{1,0:T(8,128)(2,1)S(1)} %collective-permute-done.7.refs_7_) | copy-start | bytes 442372
  32.0 13.2 %collective-permute-start.10 = (bf16[288,256]{1,0:T(8,128)(2,1)S(1)}, bf16[288,256]{1,0:T(8,128)(2,1)S(1)}, u32[]{:S(2)}, u32[]{:S(2)}) collective-permute-start(bf16[288,256]{1,0:T(8,128)(2,1)S(1)} %collective-permute-done.6.refs_6_), channel_id=1, source_target_pairs={{0,32},{32,64},{64,96},{96,128},{128,160},{160,192},{192,224},{224... | collective-permute-start | bytes 442376 | tf_op jit(solution)/shard_map/ppermute | solution.py:477
  37.7 17.9 %copy-start.15 = (bf16[288,256]{1,0:T(8,128)(2,1)}, bf16[288,256]{1,0:T(8,128)(2,1)S(1)}, u32[]{:S(2)}) copy-start(bf16[288,256]{1,0:T(8,128)(2,1)S(1)} %collective-permute-done.5.refs_5_) | copy-start | bytes 442372
  37.7 7.8 %collective-permute-start.9 = (bf16[288,256]{1,0:T(8,128)(2,1)S(1)}, bf16[288,256]{1,0:T(8,128)(2,1)S(1)}, u32[]{:S(2)}, u32[]{:S(2)}) collective-permute-start(bf16[288,256]{1,0:T(8,128)(2,1)S(1)} %collective-permute-done.5.refs_5_), channel_id=1, source_target_pairs={{0,224},{32,0},{64,32},{96,64},{128,96},{160,128},{192,160},{224,1... | collective-permute-start | bytes 442376 | tf_op jit(solution)/shard_map/ppermute | solution.py:477
  42.0 13.6 %copy-start.16 = (bf16[288,256]{1,0:T(8,128)(2,1)}, bf16[288,256]{1,0:T(8,128)(2,1)S(1)}, u32[]{:S(2)}) copy-start(bf16[288,256]{1,0:T(8,128)(2,1)S(1)} %collective-permute-done.4.refs_4_) | copy-start | bytes 442372
  42.0 7.2 %collective-permute-start.8 = (bf16[288,256]{1,0:T(8,128)(2,1)S(1)}, bf16[288,256]{1,0:T(8,128)(2,1)S(1)}, u32[]{:S(2)}, u32[]{:S(2)}) collective-permute-start(bf16[288,256]{1,0:T(8,128)(2,1)S(1)} %collective-permute-done.4.refs_4_), channel_id=1, source_target_pairs={{0,32},{32,64},{64,96},{96,128},{128,160},{160,192},{192,224},{224... | collective-permute-start | bytes 442376 | tf_op jit(solution)/shard_map/ppermute | solution.py:477
  42.5 13.1 %copy-start.17 = (bf16[288,256]{1,0:T(8,128)(2,1)}, bf16[288,256]{1,0:T(8,128)(2,1)S(1)}, u32[]{:S(2)}) copy-start(bf16[288,256]{1,0:T(8,128)(2,1)S(1)} %collective-permute-done.15.refs_15_) | copy-start | bytes 442372
  42.5 6.7 %collective-permute-start.11 = (bf16[288,256]{1,0:T(8,128)(2,1)S(1)}, bf16[288,256]{1,0:T(8,128)(2,1)S(1)}, u32[]{:S(2)}, u32[]{:S(2)}) collective-permute-start(bf16[288,256]{1,0:T(8,128)(2,1)S(1)} %collective-permute-done.7.refs_7_), channel_id=1, source_target_pairs={{0,224},{32,0},{64,32},{96,64},{128,96},{160,128},{192,160},{224,1... | collective-permute-start | bytes 442376 | tf_op jit(solution)/shard_map/ppermute | solution.py:477
  45.2 10.4 %copy-start.18 = (bf16[288,256]{1,0:T(8,128)(2,1)}, bf16[288,256]{1,0:T(8,128)(2,1)S(1)}, u32[]{:S(2)}) copy-start(bf16[288,256]{1,0:T(8,128)(2,1)S(1)} %collective-permute-done.10.refs_10_) | copy-start | bytes 442372
  45.2 6.4 %collective-permute-start.14 = (bf16[288,256]{1,0:T(8,128)(2,1)S(1)}, bf16[288,256]{1,0:T(8,128)(2,1)S(1)}, u32[]{:S(2)}, u32[]{:S(2)}) collective-permute-start(bf16[288,256]{1,0:T(8,128)(2,1)S(1)} %collective-permute-done.10.refs_10_), channel_id=1, source_target_pairs={{0,32},{32,64},{64,96},{96,128},{128,160},{160,192},{192,224},{224... | collective-permute-start | bytes 442376 | tf_op jit(solution)/shard_map/ppermute | solution.py:477
  45.5 10.1 %copy-start.19 = (bf16[288,256]{1,0:T(8,128)(2,1)}, bf16[288,256]{1,0:T(8,128)(2,1)S(1)}, u32[]{:S(2)}) copy-start(bf16[288,256]{1,0:T(8,128)(2,1)S(1)} %collective-permute-done.9.refs_9_) | copy-start | bytes 442372
  45.5 6.4 %collective-permute-start.13 = (bf16[288,256]{1,0:T(8,128)(2,1)S(1)}, bf16[288,256]{1,0:T(8,128)(2,1)S(1)}, u32[]{:S(2)}, u32[]{:S(2)}) collective-permute-start(bf16[288,256]{1,0:T(8,128)(2,1)S(1)} %collective-permute-done.9.refs_9_), channel_id=1, source_target_pairs={{0,224},{32,0},{64,32},{96,64},{128,96},{160,128},{192,160},{224,1... | collective-permute-start | bytes 442376 | tf_op jit(solution)/shard_map/ppermute | solution.py:477
  49.2 6.4 %copy-start.20 = (bf16[288,256]{1,0:T(8,128)(2,1)}, bf16[288,256]{1,0:T(8,128)(2,1)S(1)}, u32[]{:S(2)}) copy-start(bf16[288,256]{1,0:T(8,128)(2,1)S(1)} %collective-permute-done.8.refs_8_) | copy-start | bytes 442372
  49.2 6.4 %collective-permute-start.12 = (bf16[288,256]{1,0:T(8,128)(2,1)S(1)}, bf16[288,256]{1,0:T(8,128)(2,1)S(1)}, u32[]{:S(2)}, u32[]{:S(2)}) collective-permute-start(bf16[288,256]{1,0:T(8,128)(2,1)S(1)} %collective-permute-done.8.refs_8_), channel_id=1, source_target_pairs={{0,32},{32,64},{64,96},{96,128},{128,160},{160,192},{192,224},{224... | collective-permute-start | bytes 442376 | tf_op jit(solution)/shard_map/ppermute | solution.py:477
  49.2 6.4 %copy-start.21 = (bf16[288,256]{1,0:T(8,128)(2,1)}, bf16[288,256]{1,0:T(8,128)(2,1)S(1)}, u32[]{:S(2)}) copy-start(bf16[288,256]{1,0:T(8,128)(2,1)S(1)} %collective-permute-done.11.refs_11_) | copy-start | bytes 442372
  51.6 4.1 %copy-start.22 = (bf16[288,256]{1,0:T(8,128)(2,1)}, bf16[288,256]{1,0:T(8,128)(2,1)S(1)}, u32[]{:S(2)}) copy-start(bf16[288,256]{1,0:T(8,128)(2,1)S(1)} %collective-permute-done.14.refs_14_) | copy-start | bytes 442372
  51.9 3.8 %copy-start.23 = (bf16[288,256]{1,0:T(8,128)(2,1)}, bf16[288,256]{1,0:T(8,128)(2,1)S(1)}, u32[]{:S(2)}) copy-start(bf16[288,256]{1,0:T(8,128)(2,1)S(1)} %collective-permute-done.13.refs_13_) | copy-start | bytes 442372
  55.5 0.7 copy-start.24
  56.2 14.1 %copy-start.6 = (s32[64]{0:T(128)S(1)}, s32[64]{0:T(128)}, u32[]{:S(2)}) copy-start(s32[64]{0:T(128)} %get-tuple-element.54.ids) | copy-start | bytes 772
  61.4 1.9 %collective-permute-start.16 = (f32[2,136,256]{2,1,0:T(8,128)}, f32[2,136,256]{2,1,0:T(8,128)S(1)}, u32[]{:S(2)}, u32[]{:S(2)}) collective-permute-start(f32[2,136,256]{2,1,0:T(8,128)} %project.1.mine), channel_id=1, source_target_pairs={{0,8},{8,0},{1,9},{9,1},{2,10},{10,2},{3,11},{11,3},{4,12},{12,4},... | collective-permute-start | bytes 835592 | tf_op jit(solution)/shard_map/ppermute | solution.py:533
  63.3 1.0 copy-start.2
  64.3 27.9 %copy-start.4 = (bf16[144,256]{1,0:T(8,128)(2,1)}, bf16[144,256]{1,0:T(8,128)(2,1)S(1)}, u32[]{:S(2)}) copy-start(bf16[144,256]{1,0:T(8,128)(2,1)S(1)} %get-tuple-element.81.own_0) | copy-start | bytes 221188
  64.3 6.0 %collective-permute-start.17 = (bf16[2,144,256]{2,1,0:T(8,128)(2,1)S(1)}, bf16[2,144,256]{2,1,0:T(8,128)(2,1)S(1)}, u32[]{:S(2)}, u32[]{:S(2)}) collective-permute-start(bf16[2,144,256]{2,1,0:T(8,128)(2,1)S(1)} %get-tuple-element.60.near), channel_id=1, source_target_pairs={{0,16},{16,0},{1,17},{17,1},{2,18},{18,2},{3,19},{19,3},{4,20},{20... | collective-permute-start | bytes 442376 | tf_op jit(solution)/shard_map/ppermute | solution.py:537
  71.8 22.1 %all-to-all-start.1 = ((bf16[8,144,256]{2,1,0:T(8,128)(2,1)}), bf16[8,144,256]{2,1,0:T(8,128)(2,1)S(1)}, u32[]{:S(2)}, u32[]{:S(2)}) async-start(bf16[8,144,256]{2,1,0:T(8,128)(2,1)} %pick_for_planes.1), calls=%async_computation.1 | async-start | bytes 1179648 | tf_op jit(solution)/shard_map/all_to_all | solution.py:545
  75.3 10.3 %collective-permute-start.18 = (bf16[144,256]{1,0:T(8,128)(2,1)S(1)}, bf16[144,256]{1,0:T(8,128)(2,1)S(1)}, u32[]{:S(2)}, u32[]{:S(2)}) collective-permute-start(bf16[144,256]{1,0:T(8,128)(2,1)S(1)} %get-tuple-element.81.own_0), channel_id=1, source_target_pairs={{0,1},{1,0},{2,3},{3,2},{4,5},{5,4},{6,7},{7,6},{8,9},{9,8},{10,11... | collective-permute-start | bytes 221192 | tf_op jit(solution)/shard_map/ppermute | solution.py:561
  79.3 7.2 %collective-permute-start.23 = (bf16[144,256]{1,0:T(8,128)(2,1)S(1)}, bf16[144,256]{1,0:T(8,128)(2,1)S(1)}, u32[]{:S(2)}, u32[]{:S(2)}) collective-permute-start(bf16[144,256]{1,0:T(8,128)(2,1)S(1)} %get-tuple-element.81.own_0), channel_id=1, source_target_pairs={{0,4},{2,6},{4,0},{6,2},{1,5},{3,7},{5,1},{7,3},{8,12},{10,14},{12... | collective-permute-start | bytes 221192 | tf_op jit(solution)/shard_map/ppermute | solution.py:481
  82.4 9.9 %collective-permute-start.21 = (bf16[144,256]{1,0:T(8,128)(2,1)S(1)}, bf16[144,256]{1,0:T(8,128)(2,1)S(1)}, u32[]{:S(2)}, u32[]{:S(2)}) collective-permute-start(bf16[144,256]{1,0:T(8,128)(2,1)S(1)} %get-tuple-element.81.own_0), channel_id=1, source_target_pairs={{0,2},{2,4},{4,6},{6,0},{1,3},{3,5},{5,7},{7,1},{8,10},{10,12},{12... | collective-permute-start | bytes 221192 | tf_op jit(solution)/shard_map/ppermute | solution.py:481
  82.9 9.3 %collective-permute-start.19 = (bf16[144,256]{1,0:T(8,128)(2,1)S(1)}, bf16[144,256]{1,0:T(8,128)(2,1)S(1)}, u32[]{:S(2)}, u32[]{:S(2)}) collective-permute-start(bf16[144,256]{1,0:T(8,128)(2,1)S(1)} %get-tuple-element.81.own_0), channel_id=1, source_target_pairs={{0,6},{2,0},{4,2},{6,4},{1,7},{3,1},{5,3},{7,5},{8,14},{10,8},{12,... | collective-permute-start | bytes 221192 | tf_op jit(solution)/shard_map/ppermute | solution.py:481
  85.6 6.6 %copy-start.25 = (bf16[144,256]{1,0:T(8,128)(2,1)}, bf16[144,256]{1,0:T(8,128)(2,1)S(1)}, u32[]{:S(2)}) copy-start(bf16[144,256]{1,0:T(8,128)(2,1)S(1)} %collective-permute-done.18.own_1) | copy-start | bytes 221188
  85.6 6.7 %collective-permute-start.24 = (bf16[144,256]{1,0:T(8,128)(2,1)S(1)}, bf16[144,256]{1,0:T(8,128)(2,1)S(1)}, u32[]{:S(2)}, u32[]{:S(2)}) collective-permute-start(bf16[144,256]{1,0:T(8,128)(2,1)S(1)} %collective-permute-done.18.own_1), channel_id=1, source_target_pairs={{0,4},{2,6},{4,0},{6,2},{1,5},{3,7},{5,1},{7,3},{8,12},{10,14},{12... | collective-permute-start | bytes 221192 | tf_op jit(solution)/shard_map/ppermute | solution.py:481
  85.6 6.7 %collective-permute-start.22 = (bf16[144,256]{1,0:T(8,128)(2,1)S(1)}, bf16[144,256]{1,0:T(8,128)(2,1)S(1)}, u32[]{:S(2)}, u32[]{:S(2)}) collective-permute-start(bf16[144,256]{1,0:T(8,128)(2,1)S(1)} %collective-permute-done.18.own_1), channel_id=1, source_target_pairs={{0,2},{2,4},{4,6},{6,0},{1,3},{3,5},{5,7},{7,1},{8,10},{10,12},{12... | collective-permute-start | bytes 221192 | tf_op jit(solution)/shard_map/ppermute | solution.py:481
  86.6 5.7 %copy-start.26 = (bf16[144,256]{1,0:T(8,128)(2,1)}, bf16[144,256]{1,0:T(8,128)(2,1)S(1)}, u32[]{:S(2)}) copy-start(bf16[144,256]{1,0:T(8,128)(2,1)S(1)} %collective-permute-done.23.own_6) | copy-start | bytes 221188
  86.6 5.8 %collective-permute-start.20 = (bf16[144,256]{1,0:T(8,128)(2,1)S(1)}, bf16[144,256]{1,0:T(8,128)(2,1)S(1)}, u32[]{:S(2)}, u32[]{:S(2)}) collective-permute-start(bf16[144,256]{1,0:T(8,128)(2,1)S(1)} %collective-permute-done.18.own_1), channel_id=1, source_target_pairs={{0,6},{2,0},{4,2},{6,4},{1,7},{3,1},{5,3},{7,5},{8,14},{10,8},{12,... | collective-permute-start | bytes 221192 | tf_op jit(solution)/shard_map/ppermute | solution.py:481
  92.2 22.9 %copy-start.27 = (bf16[144,256]{1,0:T(8,128)(2,1)}, bf16[144,256]{1,0:T(8,128)(2,1)S(1)}, u32[]{:S(2)}) copy-start(bf16[144,256]{1,0:T(8,128)(2,1)S(1)} %collective-permute-done.21.own_4) | copy-start | bytes 221188
  92.3 22.9 %copy-start.28 = (bf16[144,256]{1,0:T(8,128)(2,1)}, bf16[144,256]{1,0:T(8,128)(2,1)S(1)}, u32[]{:S(2)}) copy-start(bf16[144,256]{1,0:T(8,128)(2,1)S(1)} %collective-permute-done.19.own_2) | copy-start | bytes 221188
  92.3 22.9 %copy-start.29 = (bf16[144,256]{1,0:T(8,128)(2,1)}, bf16[144,256]{1,0:T(8,128)(2,1)S(1)}, u32[]{:S(2)}) copy-start(bf16[144,256]{1,0:T(8,128)(2,1)S(1)} %collective-permute-done.24.own_7) | copy-start | bytes 221188
  92.3 22.9 %copy-start.30 = (bf16[144,256]{1,0:T(8,128)(2,1)}, bf16[144,256]{1,0:T(8,128)(2,1)S(1)}, u32[]{:S(2)}) copy-start(bf16[144,256]{1,0:T(8,128)(2,1)S(1)} %collective-permute-done.22.own_5) | copy-start | bytes 221188
  92.3 22.9 %copy-start.31 = (bf16[144,256]{1,0:T(8,128)(2,1)}, bf16[144,256]{1,0:T(8,128)(2,1)S(1)}, u32[]{:S(2)}) copy-start(bf16[144,256]{1,0:T(8,128)(2,1)S(1)} %collective-permute-done.20.own_3) | copy-start | bytes 221188
  93.9 21.3 %collective-permute-start.25 = (bf16[16,288,256]{2,1,0:T(8,128)(2,1)}, bf16[16,288,256]{2,1,0:T(8,128)(2,1)}, u32[]{:S(2)}, u32[]{:S(2)}) collective-permute-start(bf16[16,288,256]{2,1,0:T(8,128)(2,1)} %stack_blocks.1.kept), channel_id=1, source_target_pairs={{0,8},{8,0},{1,9},{9,1},{2,10},{10,2},{3,11},{11,3},{4,12},{12,4},... | collective-permute-start | bytes 7077896 | tf_op jit(solution)/shard_map/ppermute | solution.py:572
  115.1 19.0 %copy-start.7 = (s32[64]{0:T(128)S(1)}, s32[64]{0:T(128)}, u32[]{:S(2)}) copy-start(s32[64]{0:T(128)} %get-tuple-element.54.ids) | copy-start | bytes 772
  125.6 1.9 %collective-permute-start.26 = (bf16[16,80,128]{2,1,0:T(8,128)(2,1)}, bf16[16,80,128]{2,1,0:T(8,128)(2,1)S(1)}, u32[]{:S(2)}, u32[]{:S(2)}) collective-permute-start(bf16[16,80,128]{2,1,0:T(8,128)(2,1)} %get-tuple-element.92), channel_id=1, source_target_pairs={{0,8},{8,0},{1,9},{9,1},{2,10},{10,2},{3,11},{11,3},{4,12},{12,4},... | collective-permute-start | bytes 983048 | tf_op jit(solution)/shard_map/ppermute | solution.py:605
  127.5 1.1 copy-start.3
  129.4 17.6 %all-to-all-start.3 = ((bf16[16,80,128]{2,1,0:T(8,128)(2,1)}), bf16[16,80,128]{2,1,0:T(8,128)(2,1)S(1)}, u32[]{:S(2)}, u32[]{:S(2)}) async-start(bf16[16,80,128]{2,1,0:T(8,128)(2,1)} %add_core.1), calls=%async_computation.3 | async-start | bytes 655360 | tf_op jit(solution)/shard_map/all_to_all | solution.py:606
  134.1 1.7 %copy-start = (bf16[16,288,256]{2,1,0:T(8,128)(2,1)S(1)}, bf16[16,288,256]{2,1,0:T(8,128)(2,1)}, u32[]{:S(2)}) copy-start(bf16[16,288,256]{2,1,0:T(8,128)(2,1)} %stack_blocks.1.kept) | copy-start | bytes 7077892
  135.8 0.8 copy-start.5
  136.6 0.7 copy-start.8
  137.3 20.5 %copy-start.9 = (f32[128]{0:T(128)S(1)}, f32[128]{0:T(128)}, u32[]{:S(2)}) copy-start(f32[128]{0:T(128)} %param.12) | copy-start | bytes 1540
